TPU v7x, 256 devices: a whole 4x4x8 slice. The times are simulated.
256 devices in a mesh: grp: 2 (over core), row: 4 (over x), col: 32 (over z, y).
Axes of the slice: x: 4, y: 4, z: 8, core: 2. Of those that a mesh axis runs over, the one named last changes fastest.
Arguments:
- resid: bfloat16 [512, 5120], P(('grp', 'col'), 'row'), may hold values from -6 to 6
- query: bfloat16 [128, 4, 4096], P(('row', 'col'), None, 'grp'), may hold values from -11 to 11
- key_new: bfloat16 [128, 4, 1024], P(('row', 'col'), None, 'grp'), may hold values from -6 to 6
- value_new: bfloat16 [128, 4, 1024], P(('row', 'col'), None, 'grp'), may hold values from -6 to 6
- key_cache: bfloat16 [128, 2048, 1024], P(('row', 'col'), None, 'grp'), may hold values from -11 to 11
- value_cache: bfloat16 [128, 2048, 1024], P(('row', 'col'), None, 'grp'), may hold values from -6 to 6
- ctx_len: int32 [128], P(('row', 'col')), may hold values from 512 to 2048, as said below
- ssm_x: bfloat16 [128, 4, 8192], P(('row', 'col'), None, 'grp'), may hold values from -6 to 6
- ssm_gate: bfloat16 [128, 4, 8192], P(('row', 'col'), None, 'grp'), may hold values from -6 to 6
- ssm_b: bfloat16 [128, 4, 128], P(('row', 'col')), may hold values from -6 to 6
- ssm_c: bfloat16 [128, 4, 128], P(('row', 'col')), may hold values from -0.59765625 to 0.59765625
- ssm_dt: float32 [128, 4, 64], P(('row', 'col'), None, 'grp'), may hold values from 0.02 to 1
- decay_rate: float32 [64], P('grp'), may hold values from 0.05 to 8
- skip_gain: float32 [64], P('grp'), may hold values from 0.5 to 1.5
- ssm_state: float32 [128, 64, 128, 128], P(('row', 'col'), 'grp'), may hold values from -2 to 2
- accepted: int32 [128], P(('row', 'col')), may hold values from 0 to 4
- slot_of: int32 [128], replicated, may hold values from 0 to 127, each once
- w_out: bfloat16 [12288, 5120], P(('grp', 'col'), 'row'), may hold values from -0.0546875 to 0.0546875
- norm_gain: float32 [5120], P('row'), may hold values from 0.5 to 1.5
- gate_up: bfloat16 [5120, 2, 21504], P('row', None, ('grp', 'col')), may hold values from -0.078125 to 0.078125
- w_down: bfloat16 [21504, 5120], P(('grp', 'col'), 'row'), may hold values from -0.0390625 to 0.0390625
Outputs:
- layer_out: bfloat16 [512, 5120], P(('grp', 'col'), 'row')
- state_next: float32 [128, 64, 128, 128], P(('row', 'col'), 'grp')
Inputs may be any that keep to these rules, and one draw needn't show every extreme that they name: `ctx_len`: cache entries at positions at or past a slot's length are not part of its context; some slot has length 2048. `slot_of`: each slot holds exactly one request.
All inputs are finite; a program needn't handle non-finite values.
Results may differ from a plain program's by a relative error of at most 0.0052.
Values may be sent and summed in bfloat16 or wider, within the bound.
No kernel may reach another device: no remote copies, remote signals or barrier semaphores. Data moves between devices by JAX's collectives and lax.ppermute only.
A program may use at most 64 MiB of HBM per device.

v0:
```python
import jax
import jax.numpy as jnp
from jax import lax
from jax.sharding import PartitionSpec as P

D = 5120
HD = 128
PH = 128


norm_eps = 1e-05


def visible(length, cache_len, steps_new):
    position = jnp.arange(cache_len + steps_new)[None, :]
    drafts = jnp.arange(steps_new)[:, None]
    return jnp.where(position < cache_len, position < length, position - cache_len <= drafts)


def attend_whole(request):
    queries, keys_new, values_new, keys_cache, values_cache, length = request
    steps_new = queries.shape[0]
    kv_heads = keys_new.shape[1] // HD
    groups = queries.shape[1] // keys_new.shape[1]
    q_heads = queries.reshape(steps_new, kv_heads, groups, HD)
    keys_all = jnp.concatenate([keys_cache, keys_new], 0).reshape(-1, kv_heads, HD)
    values_all = jnp.concatenate([values_cache, values_new], 0).reshape(-1, kv_heads, HD)
    scores = jnp.einsum(
        "qjgd,kjd->jgqk", q_heads, keys_all, preferred_element_type=jnp.float32
    ) * HD ** (-0.5)
    live = visible(length, keys_cache.shape[0], steps_new)
    scores = jnp.where(live[None, None], scores, -jnp.inf)
    peak = jnp.max(scores, axis=-1, keepdims=True)
    weights = jnp.exp(scores - peak)
    total = jnp.sum(weights, axis=-1)
    summed = jnp.einsum(
        "jgqk,kjd->qjgd",
        weights.astype(jnp.bfloat16),
        values_all,
        preferred_element_type=jnp.float32,
    )
    result = summed / jnp.transpose(total, (2, 0, 1))[..., None]
    return result.reshape(steps_new, -1).astype(jnp.bfloat16)


def ssm_scan(ssm_x, ssm_gate, ssm_b, ssm_c, ssm_dt, decay_rate, skip_gain, ssm_state, accepted):
    count = ssm_x.shape[0]
    steps_new = ssm_x.shape[1]
    heads = decay_rate.shape[0]
    inputs = ssm_x.astype(jnp.float32).reshape(count, steps_new, heads, PH)
    in_map = ssm_b.astype(jnp.float32)
    out_map = ssm_c.astype(jnp.float32)
    state = ssm_state
    kept = ssm_state
    outputs = []
    for t in range(steps_new):
        decay = jnp.exp(-ssm_dt[:, t, :] * decay_rate[None, :])
        driven = ssm_dt[:, t, :, None] * inputs[:, t]
        state = (
            decay[:, :, None, None] * state + driven[:, :, :, None] * in_map[:, t, None, None, :]
        )
        readout = jnp.einsum("rhpn,rn->rhp", state, out_map[:, t], precision=lax.Precision.HIGHEST)
        outputs.append(readout + skip_gain[None, :, None] * inputs[:, t])
        kept = jnp.where((accepted > t)[:, None, None, None], state, kept)
    stacked = jnp.stack(outputs, axis=1).reshape(count, steps_new, heads * PH)
    gated = stacked * jax.nn.silu(ssm_gate.astype(jnp.float32))
    return (gated.astype(jnp.bfloat16), kept)


def shards(
    resid,
    query,
    key_new,
    value_new,
    key_cache,
    value_cache,
    ctx_len,
    ssm_x,
    ssm_gate,
    ssm_b,
    ssm_c,
    ssm_dt,
    decay_rate,
    skip_gain,
    ssm_state,
    accepted,
    slot_of,
    w_out,
    norm_gain,
    gate_up,
    w_down,
):
    requests = (query, key_new, value_new, key_cache, value_cache, ctx_len)
    attended = lax.map(attend_whole, requests)
    ssm_out, state_next = ssm_scan(
        ssm_x, ssm_gate, ssm_b, ssm_c, ssm_dt, decay_rate, skip_gain, ssm_state, accepted
    )
    steps_new = query.shape[1]
    local_rows = query.shape[0] * steps_new
    mixed_local = jnp.concatenate([attended, ssm_out], axis=2).reshape(local_rows, -1)
    everything = lax.all_gather(mixed_local, ("row", "col"), axis=0, tiled=True)
    width = everything.shape[1] // lax.axis_size("col")
    gathered = lax.dynamic_slice_in_dim(everything, lax.axis_index("col") * width, width, 1)
    by_slot = gathered.reshape(-1, steps_new, gathered.shape[1])
    mixed_req = jnp.take(by_slot, slot_of, axis=0).reshape(-1, gathered.shape[1])
    piece = mixed_req
    projected = lax.psum_scatter(
        jnp.dot(piece, w_out, preferred_element_type=jnp.float32),
        ("grp", "col"),
        scatter_dimension=0,
        tiled=True,
    )
    stream = resid.astype(jnp.float32) + projected
    squares = lax.psum(jnp.sum(stream * stream, axis=1), "row")
    mean_sq = squares / D
    normed = (stream * lax.rsqrt(mean_sq[:, None] + norm_eps) * norm_gain[None, :]).astype(
        jnp.bfloat16
    )
    hidden_local = gate_up.shape[2]
    both_weights = gate_up.reshape(gate_up.shape[0], 2 * hidden_local)
    partial_sums = jnp.dot(
        lax.all_gather(normed, ("grp", "col"), axis=0, tiled=True),
        both_weights,
        preferred_element_type=jnp.float32,
    )
    summed = lax.psum(partial_sums, "row")
    hidden = (jax.nn.silu(summed[:, :hidden_local]) * summed[:, hidden_local:]).astype(jnp.bfloat16)
    piece = hidden
    down = lax.psum_scatter(
        jnp.dot(piece, w_down, preferred_element_type=jnp.float32),
        ("grp", "col"),
        scatter_dimension=0,
        tiled=True,
    )
    layer_out = (stream + down).astype(jnp.bfloat16)
    return (layer_out, state_next)


def solution(mesh):
    placed = (
        P(("grp", "col"), "row"),
        P(("row", "col"), None, "grp"),
        P(("row", "col"), None, "grp"),
        P(("row", "col"), None, "grp"),
        P(("row", "col"), None, "grp"),
        P(("row", "col"), None, "grp"),
        P(("row", "col")),
        P(("row", "col"), None, "grp"),
        P(("row", "col"), None, "grp"),
        P(("row", "col"), None, None),
        P(("row", "col"), None, None),
        P(("row", "col"), None, "grp"),
        P("grp"),
        P("grp"),
        P(("row", "col"), "grp", None, None),
        P(("row", "col")),
        P(),
        P(("grp", "col"), "row"),
        P("row"),
        P("row", None, ("grp", "col")),
        P(("grp", "col"), "row"),
    )
    return jax.shard_map(
        shards,
        mesh=mesh,
        in_specs=placed,
        out_specs=(P(("grp", "col"), "row"), P(("row", "col"), "grp", None, None)),
        check_vma=False,
    )
```

profile of v0, /device:TPU:2, one launch (start us, length us, event | category | flops | bytes accessed | tf_op | source)
XLA Modules:
  0.0 623.0 jit_solution(7443745353732111233)
XLA Ops:
  7.2 0.0 copy-start
  7.2 0.0 all-gather.6.cloned.1.call-start
  7.2 0.9 slice_bitcast_fusion.11
  8.1 0.8 convert_bitcast_fusion
  8.9 0.7 convert_element_type.45
  9.6 0.8 multiply_exponential_fusion.3
  11.1 3.9 copy.50
  15.0 4.0 copy.51
  19.0 0.0 copy-done.7
  19.0 0.0 copy-done.12
  19.0 2.6 fusion.71
  21.6 0.1 copy.54
  21.7 3.9 copy.48
  25.6 3.9 copy.49
  29.6 0.1 fusion.45
  29.7 0.0 copy-done.9
  29.7 3.0 fusion.14
  32.7 0.0 copy-done.1
  32.7 2.5 fusion.12
  35.2 3.0 fusion.10
  38.2 0.0 copy-start.13
  38.3 3.6 fusion.8
  41.9 0.0 copy-done.2
  41.9 0.0 copy-done.13
  41.9 0.0 copy-start.10
  41.9 0.0 copy-start.6
  41.9 0.0 copy-start.14
  41.9 0.4 fusion.18
  42.4 0.0 copy-start.3
  42.4 0.2 copy-done.10
  42.6 0.1 multiply_add_fusion.11
  42.6 0.0 copy-done.6
  42.7 0.1 fusion.43
  42.8 0.7 copy.55
  43.5 0.0 all-gather.6.cloned.1.call-update
  43.6 0.0 reduce-scatter.3.cloned.1.call-start
  43.6 0.1 broadcast_in_dim.121
  43.7 0.1 broadcast_in_dim.122
  43.9 138.9 %all-gather.6.cloned.1.call-done = bf16[1,512,6144]{2,0,1:T(2,128)(2,1)} async-done(((bf16[1,4,6144]{2,0,1:T(2,128)(2,1)}), bf16[1,512,6144]{2,0,1:T(2,128)(2,1)}) %all-gather.6.cloned.1.call-update) | async-done | bytes 6291472 | tf_op jit(solution)/shard_map/all_gather | solution.py:101
  182.7 2.8 dynamic-slice_reduce_fusion
  185.6 0.1 reshape.387
  185.7 0.8 gather_fusion
  186.5 0.2 gather.7
  186.7 2.1 fusion.36
  188.8 0.0 reduce-scatter.3.cloned.1.call-update
  188.8 0.0 all-gather.4.cloned.1.call-start
  188.8 139.0 %reduce-scatter.3.cloned.1.call-done = f32[8,1280]{1,0:T(8,128)} async-done(((f32[512,1280]{1,0:T(8,128)}), f32[8,1280]{1,0:T(8,128)}) %reduce-scatter.3.cloned.1.call-update) | async-done | bytes 40976 | tf_op jit(solution)/shard_map/reduce_scatter | solution.py:107
  327.9 0.0 copy-done.5
  327.9 0.9 multiply_reduce_fusion
  328.8 8.5 %psum.14 = f32[8]{0:T(128)S(1)} all-reduce(f32[8]{0:T(128)S(1)} %multiply_reduce_fusion), channel_id=1, replica_groups=mesh['grp'=2,'row'=4,'col'=32] {'row'}, use_global_device_ids=true, to_apply=%region_4.5 | all-reduce | flops 8 | bytes 64 | tf_op jit(solution)/shard_map/psum | solution.py:114
  337.3 0.0 copy-done.8
  337.3 1.5 multiply_convert_fusion
  338.8 0.0 all-gather.4.cloned.1.call-update
  338.8 0.0 all-reduce.2.cloned.1.call-start
  338.9 74.8 %all-gather.4.cloned.1.call-done = bf16[512,1280]{1,0:T(8,128)(2,1)} async-done(((bf16[8,1280]{1,0:T(8,128)(2,1)}), bf16[512,1280]{1,0:T(8,128)(2,1)}) %all-gather.4.cloned.1.call-update) | async-done | bytes 1310736 | tf_op jit(solution)/shard_map/all_gather | solution.py:122
  413.6 3.6 fusion.74
  417.2 0.0 all-reduce.2.cloned.1.call-update
  417.2 0.0 reduce-scatter.5.cloned.1.call-start
  417.3 50.4 %all-reduce.2.cloned.1.call-done = f32[512,672]{0,1:T(8,128)} async-done(((f32[512,672]{0,1:T(8,128)}), f32[512,672]{0,1:T(8,128)}) %all-reduce.2.cloned.1.call-update) | async-done | bytes 1376272 | tf_op jit(solution)/shard_map/psum | solution.py:126
  467.7 3.7 fusion.32
  471.4 0.0 reduce-scatter.5.cloned.1.call-update
  472.1 5.1 select_select_fusion
  477.2 137.9 %reduce-scatter.5.cloned.1.call-done = f32[8,1280]{1,0:T(8,128)} async-done(((f32[512,1280]{1,0:T(8,128)}), f32[8,1280]{1,0:T(8,128)}) %reduce-scatter.5.cloned.1.call-update) | async-done | bytes 40976 | tf_op jit(solution)/shard_map/reduce_scatter | solution.py:129
  615.1 1.4 add_convert_fusion
  (25 shorter events, 0.1 us)
Async XLA Ops:
  7.2 406.5 %copy-start = (bf16[1280,2,336]{0,2,1:T(8,128)(2,1)S(1)}, bf16[1280,2,336]{0,2,1:T(8,128)(2,1)}, u32[]{:S(2)}) copy-start(bf16[1280,2,336]{0,2,1:T(8,128)(2,1)} %param.40) | copy-start | bytes 5160964
  7.2 175.6 %all-gather.6.cloned.1.call-start = ((), (), s32[]{:S(2)}) async-start(), calls=%async_computation.6 | async-start | bytes 12681216 | tf_op jit(solution)/shard_map/all_gather | solution.py:101
  15.0 4.0 copy-start.7
  15.0 4.0 copy-start.12
  25.6 4.0 copy-start.9
  29.6 3.1 copy-start.1
  38.2 3.7 copy-start.2
  38.2 3.7 copy-start.13
  41.9 0.7 copy-start.10
  41.9 0.8 copy-start.6
  41.9 1.7 copy-start.14
  42.4 144.3 %copy-start.3 = (bf16[192,1280]{1,0:T(8,128)(2,1)S(1)}, bf16[192,1280]{1,0:T(8,128)(2,1)}, u32[]{:S(2)}) copy-start(bf16[192,1280]{1,0:T(8,128)(2,1)} %param.38) | copy-start | bytes 1474564
  43.6 284.3 %reduce-scatter.3.cloned.1.call-start = ((), (), s32[]{:S(2)}) async-start(), calls=%async_computation.2 | async-start | bytes 2662400 | tf_op jit(solution)/shard_map/reduce_scatter | solution.py:107
  188.8 139.1 %copy-start.5 = (bf16[8,1280]{1,0:T(8,128)(2,1)S(1)}, bf16[8,1280]{1,0:T(8,128)(2,1)}, u32[]{:S(2)}) copy-start(bf16[8,1280]{1,0:T(8,128)(2,1)} %param.21) | copy-start | bytes 61444
  188.8 148.6 %copy-start.8 = (f32[1280]{0:T(1024)S(1)}, f32[1280]{0:T(1024)}, u32[]{:S(2)}) copy-start(f32[1280]{0:T(1024)} %param.39) | copy-start | bytes 15364
  188.8 224.9 %all-gather.4.cloned.1.call-start = ((), (), s32[]{:S(2)}) async-start(), calls=%async_computation.3 | async-start | bytes 1331200 | tf_op jit(solution)/shard_map/all_gather | solution.py:122
  338.8 128.8 %all-reduce.2.cloned.1.call-start = ((), (), s32[]{:S(2)}) async-start(), calls=%async_computation.4 | async-start | bytes 2752512 | tf_op jit(solution)/shard_map/psum | solution.py:126
  413.6 54.0 %copy-start.11 = (bf16[336,1280]{1,0:T(8,128)(2,1)S(1)}, bf16[336,1280]{1,0:T(8,128)(2,1)}, u32[]{:S(2)}) copy-start(bf16[336,1280]{1,0:T(8,128)(2,1)} %param.41) | copy-start | bytes 2580484
  417.2 197.9 %reduce-scatter.5.cloned.1.call-start = ((), (), s32[]{:S(2)}) async-start(), calls=%async_computation.5 | async-start | bytes 2662400 | tf_op jit(solution)/shard_map/reduce_scatter | solution.py:129
  472.1 143.0 %copy-start.4 = (f32[8,1280]{1,0:T(8,128)S(1)}, f32[8,1280]{1,0:T(8,128)}, u32[]{:S(2)}) copy-start(f32[8,1280]{1,0:T(8,128)} %reduce-scatter.3.cloned.1.call-done) | copy-start | bytes 122884
Sparse Core Ops, SparseCore 0:
  43.7 139.0 all-gather.5
  188.9 138.9 reduce-scatter.2
  339.0 74.6 all-gather.3
  417.3 50.2 all-reduce.1
  471.6 143.4 reduce-scatter.4
where the time goes:
time: 624 us; the launch traced here: 623 us
  waiting for transfers between devices  541 us (87%)
  matrix products  24.6 us (4%)
  local copies, waits for them, and re-layouts  21.9 us (4%)
  between operations  15.3 us (2%)
  other arithmetic  11.5 us (2%)
  blocking collectives  8.55 us (1%)
    reduce_scatter x1, waiting for transfers between devices, shards(): lax.psum_scatter(jnp.dot(piece, w_out, preferred_element_type=jnp.float32...  139 us
    all_gather x1, waiting for transfers between devices, shards(): everything = lax.all_gather(mixed_local, ('row', 'col'), axis=0, tiled=True)  139 us
    reduce_scatter x1, waiting for transfers between devices, shards(): lax.psum_scatter(jnp.dot(piece, w_down, preferred_element_type=jnp.float3...  138 us
    all_gather x1, waiting for transfers between devices, shards(): lax.all_gather(normed, ('grp', 'col'), axis=0, tiled=True)  74.8 us
    psum x1, waiting for transfers between devices, shards(): summed = lax.psum(partial_sums, 'row')  50.4 us
  transfers between devices with their start and end apart: 5, of which 5 were waited for; matrix products, arithmetic and copies ran while one was open for 1% of the time, Pallas kernels for 0%

commit v1 on v0

--- a/solution.py
+++ b/solution.py
@@ -67,6 +67,18 @@
     return (gated.astype(jnp.bfloat16), kept)
 
 
+def exchange(blocks, axis):
+    return lax.all_to_all(blocks, axis, 0, 0, tiled=True)
+
+
+def ring_gather(block, axis):
+    size = lax.axis_size(axis)
+    got = [block]
+    for shift in range(1, size):
+        got.append(lax.ppermute(block, axis, [(k, (k + shift) % size) for k in range(size)]))
+    return jnp.stack(got)
+
+
 def shards(
     resid,
     query,
@@ -90,49 +102,64 @@
     gate_up,
     w_down,
 ):
+    f32 = jnp.float32
+    bf16 = jnp.bfloat16
+    rows = lax.axis_size("row")
+    cols = lax.axis_size("col")
+    steps_new = query.shape[1]
+    in_weights = lax.all_gather(jnp.transpose(gate_up, (1, 2, 0)), "grp", axis=0, tiled=False)
+    down_weights = lax.all_gather(w_down, "grp", axis=0, tiled=True)
+
     requests = (query, key_new, value_new, key_cache, value_cache, ctx_len)
     attended = lax.map(attend_whole, requests)
     ssm_out, state_next = ssm_scan(
         ssm_x, ssm_gate, ssm_b, ssm_c, ssm_dt, decay_rate, skip_gain, ssm_state, accepted
     )
-    steps_new = query.shape[1]
-    local_rows = query.shape[0] * steps_new
-    mixed_local = jnp.concatenate([attended, ssm_out], axis=2).reshape(local_rows, -1)
-    everything = lax.all_gather(mixed_local, ("row", "col"), axis=0, tiled=True)
-    width = everything.shape[1] // lax.axis_size("col")
-    gathered = lax.dynamic_slice_in_dim(everything, lax.axis_index("col") * width, width, 1)
-    by_slot = gathered.reshape(-1, steps_new, gathered.shape[1])
-    mixed_req = jnp.take(by_slot, slot_of, axis=0).reshape(-1, gathered.shape[1])
-    piece = mixed_req
-    projected = lax.psum_scatter(
-        jnp.dot(piece, w_out, preferred_element_type=jnp.float32),
-        ("grp", "col"),
-        scatter_dimension=0,
-        tiled=True,
-    )
-    stream = resid.astype(jnp.float32) + projected
-    squares = lax.psum(jnp.sum(stream * stream, axis=1), "row")
-    mean_sq = squares / D
-    normed = (stream * lax.rsqrt(mean_sq[:, None] + norm_eps) * norm_gain[None, :]).astype(
-        jnp.bfloat16
-    )
-    hidden_local = gate_up.shape[2]
-    both_weights = gate_up.reshape(gate_up.shape[0], 2 * hidden_local)
-    partial_sums = jnp.dot(
-        lax.all_gather(normed, ("grp", "col"), axis=0, tiled=True),
-        both_weights,
-        preferred_element_type=jnp.float32,
-    )
-    summed = lax.psum(partial_sums, "row")
-    hidden = (jax.nn.silu(summed[:, :hidden_local]) * summed[:, hidden_local:]).astype(jnp.bfloat16)
-    piece = hidden
-    down = lax.psum_scatter(
-        jnp.dot(piece, w_down, preferred_element_type=jnp.float32),
-        ("grp", "col"),
-        scatter_dimension=0,
-        tiled=True,
-    )
-    layer_out = (stream + down).astype(jnp.bfloat16)
+    mixed_local = jnp.concatenate([attended, ssm_out], axis=2).reshape(steps_new, -1)
+    width = mixed_local.shape[1] // cols
+    pieces = jnp.transpose(mixed_local.reshape(steps_new, cols, width), (1, 0, 2))
+    mine = exchange(pieces, "col")
+    by_slot = ring_gather(mine, "row").reshape(rows * cols, steps_new, width)
+    behind = (lax.axis_index("row") - slot_of // cols) % rows
+    mixed_req = jnp.take(by_slot, behind * cols + slot_of % cols, axis=0).reshape(-1, width)
+    partial = jnp.dot(mixed_req, w_out, preferred_element_type=f32).astype(bf16)
+    partial = partial.reshape(2, -1, partial.shape[1])
+    half = jnp.sum(exchange(partial, "grp").astype(f32), axis=0).astype(bf16)
+    half = exchange(half.reshape(cols, -1, half.shape[1]), "col")
+    stream = resid.astype(f32) + jnp.sum(half.astype(f32), axis=0)
+    scaled = (stream * norm_gain[None, :]).astype(bf16)
+    spread = exchange(jnp.broadcast_to(scaled[None], (cols,) + scaled.shape), "col")
+    tokens = spread.reshape(-1, spread.shape[2])
+    squares = jnp.sum(jnp.square(tokens.astype(f32) / norm_gain[None, :]), axis=1, keepdims=True)
+    high = squares.astype(bf16)
+    low = (squares - high.astype(f32)).astype(bf16)
+    units = in_weights.shape[2]
+    sums = [
+        lax.dot_general(
+            tokens, in_weights[g, k], (((1,), (1,)), ((), ())), preferred_element_type=f32
+        ).astype(bf16)
+        for g in range(2)
+        for k in range(2)
+    ]
+    packed = jnp.concatenate(sums + [high, low], axis=1)
+    packed = packed.reshape(rows, -1, packed.shape[1])
+    summed = jnp.sum(exchange(packed, "row").astype(f32), axis=0)
+    mean_sq = (summed[:, 4 * units] + summed[:, 4 * units + 1]) / D
+    summed = summed * lax.rsqrt(mean_sq[:, None] + norm_eps)
+    hidden = jnp.concatenate(
+        [
+            jax.nn.silu(summed[:, 2 * g * units : (2 * g + 1) * units])
+            * summed[:, (2 * g + 1) * units : (2 * g + 2) * units]
+            for g in range(2)
+        ],
+        axis=1,
+    ).astype(bf16)
+    by_row = ring_gather(hidden, "row")
+    order = (lax.axis_index("row") - jnp.arange(rows)) % rows
+    hidden = jnp.take(by_row, order, axis=0).reshape(-1, hidden.shape[1])
+    down = jnp.dot(hidden, down_weights, preferred_element_type=f32).astype(bf16)
+    down = exchange(down.reshape(cols, -1, down.shape[1]), "col")
+    layer_out = (stream + jnp.sum(down.astype(f32), axis=0)).astype(bf16)
     return (layer_out, state_next)
 
 

time: 624 us -> 207 us (0.33)
  waiting for transfers between devices: 541 us -> 60.4 us
  starting transfers between devices: 0.21 us -> 36.3 us
  blocking collectives: 8.55 us -> 30 us
    reduce_scatter x2 -> x0, waiting for transfers between devices: 277 us -> none  [the longest x1 139 us: shards(): lax.psum_scatter(jnp.dot(piece, w_out, preferred_element_type=jnp.float32...]
    all_gather x2, waiting for transfers between devices: 214 us -> 0.02 us  [the longest x1 0.02 us: shards(): down_weights = lax.all_gather(w_down, 'grp', axis=0, tiled=True)]
    all_to_all x0 -> x4, waiting for transfers between devices: none -> 52.1 us  [exchange(): return lax.all_to_all(blocks, axis, 0, 0, tiled=True)]
    psum x1 -> x0, waiting for transfers between devices: 50.4 us -> none  [shards(): summed = lax.psum(partial_sums, 'row')]
    all_to_all x0 -> x2, blocking collectives: none -> 30 us  [exchange(): return lax.all_to_all(blocks, axis, 0, 0, tiled=True)]
    all_to_all x0 -> x4, starting transfers between devices: none -> 27.3 us  [exchange(): return lax.all_to_all(blocks, axis, 0, 0, tiled=True)]
    ppermute x0 -> x6, starting transfers between devices: none -> 8.93 us  [ring_gather(): lax.ppermute(block, axis, [(k, (k + shift) % size) for k in range(size)])]
    psum x1 -> x0, blocking collectives: 8.55 us -> none  [shards(): squares = lax.psum(jnp.sum(stream * stream, axis=1), 'row')]
  transfers between devices with their start and end apart: 5 -> 12, of which waited for: 5 -> 9; matrix products, arithmetic and copies ran while one was open for 1% -> 4% of each run, Pallas kernels for 0% -> 0%
where the time goes in v1:
time: 207 us; the launch traced here: 206 us
  waiting for transfers between devices  60.4 us (29%)
  starting transfers between devices  36.3 us (18%)
  blocking collectives  30 us (14%)
  matrix products  26.4 us (13%)
  local copies, waits for them, and re-layouts  24.8 us (12%)
  between operations  16 us (8%)
  other arithmetic  12.1 us (6%)
    all_to_all x4, waiting for transfers between devices, exchange(): return lax.all_to_all(blocks, axis, 0, 0, tiled=True)  52.1 us
    all_to_all x2, blocking collectives, exchange(): return lax.all_to_all(blocks, axis, 0, 0, tiled=True)  30 us
    all_to_all x4, starting transfers between devices, exchange(): return lax.all_to_all(blocks, axis, 0, 0, tiled=True)  27.3 us
    dot_general x4, matrix products, ssm_scan(): jnp.einsum('rhpn,rn->rhp', state, out_map[:, t], precision=lax.Precision....  10.7 us
    dot_general x4, matrix products, shards(): lax.dot_general(tokens, in_weights[g, k], (((1,), (1,)), ((), ())), prefe...  9.02 us
    ppermute x6, starting transfers between devices, ring_gather(): lax.ppermute(block, axis, [(k, (k + shift) % size) for k in range(size)])  8.93 us
    ppermute x6, waiting for transfers between devices, ring_gather(): lax.ppermute(block, axis, [(k, (k + shift) % size) for k in range(size)])  6.91 us
    unnamed x71, local copies, waits for them, and re-layouts  5.7 us
  transfers between devices with their start and end apart: 12, of which 9 were waited for; matrix products, arithmetic and copies ran while one was open for 4% of the time, Pallas kernels for 0%

profile of v1, /device:TPU:2, one launch (start us, length us, event | category | flops | bytes accessed | tf_op | source)
XLA Modules:
  0.0 206.0 jit_solution(5817543525281348738)
XLA Ops:
  7.2 0.8 slice_bitcast_fusion.19
  8.0 0.8 convert_bitcast_fusion
  8.8 0.7 convert_element_type.124
  9.5 0.8 multiply_exponential_fusion.3
  11.1 2.9 %copy.122 = bf16[1,2048,512]{1,2,0:T(8,128)(2,1)S(1)} copy(bf16[1,2048,512]{2,1,0:T(8,128)(2,1)} %param.25) | data formatting | bytes 4194304 | tf_op args[4]
  14.0 2.5 %copy.123 = bf16[2048,4,128]{2,0,1:T(8,128)(2,1)} copy(bf16[2048,4,128]{0,2,1:T(8,128)(2,1)S(1)} %bitcast.198) | data formatting | bytes 4194304 | tf_op jit(solution)/shard_map/while/body/eval_jaxpr/concatenate | solution.py:26
  16.6 2.7 %fusion.82 = (f32[4,4,4]{1,2,0:T(4,128)S(1)}, bf16[4,4,4,2052]{3,1,2,0:T(4,128)(2,1)S(1)}) fusion(bf16[4,4,128]{2,0,1:T(4,128)(2,1)S(1)} %bitcast.232, bf16[2048,4,128]{2,0,1:T(8,128)(2,1)} %copy.123, pred[4,2052]{1,0:T(4,128)(4,1)S(1)} %fusion.46, bf16[4,4,4,128]{3,2,1,0:T(4,128)(2,1)S(1)} %reshape.518), kind=kOutput, calls=%fused_computation.164 | convolution fusion | flops 38481156 | bytes 2388752 | tf_op jit(solution)/shard_map/while/body/eval_jaxpr/sub | solution.py:34
  19.3 0.1 copy.126
  19.4 2.4 %copy.120 = bf16[1,2048,512]{1,2,0:T(8,128)(2,1)} copy(bf16[1,2048,512]{2,1,0:T(8,128)(2,1)S(1)} %copy-done.2) | data formatting | bytes 4194304 | tf_op args[5]
  21.8 4.1 %copy.121 = bf16[2048,4,128]{2,0,1:T(8,128)(2,1)} copy(bf16[2048,4,128]{0,2,1:T(8,128)(2,1)} %bitcast.199) | data formatting | bytes 4194304 | tf_op jit(solution)/shard_map/while/body/eval_jaxpr/concatenate | solution.py:27
  26.0 1.5 fusion.15
  27.6 2.5 %fusion.13 = f32[1,32,128]{2,0,1:T(1,128)S(1)} fusion(bf16[1,4,128]{2,1,0:T(4,128)(2,1)S(1)} %copy-done.29, f32[1,32,128,128]{3,2,1,0:T(8,128)S(1)} %copy-done.1, f32[128]{0:T(128)S(1)} %get-tuple-element.53, f32[32,128]{1,0:T(8,128)S(1)} %get-tuple-element.41, f32[32]{0:T(128)S(1)} %get-tuple-element.43, f32[128]{0:T(128)S(1)} %get-tuple-element.50, ...), kind=kOutput, calls=%fused_computation.20 | convolution fusion | flops 9437184 | bytes 2148864 | tf_op jit(solution)/shard_map/rhpn,rn->rhp/dot_general | solution.py:62
  30.0 3.0 %fusion.11 = f32[1,32,128]{2,0,1:T(1,128)S(1)} fusion(f32[128]{0:T(128)S(1)} %get-tuple-element.52, f32[32,128]{1,0:T(8,128)S(1)} %get-tuple-element.40, f32[32]{0:T(128)S(1)} %get-tuple-element.45, bf16[1,4,128]{2,1,0:T(4,128)(2,1)S(1)} %copy-done.29, f32[1,32,128,128]{3,2,1,0:T(8,128)S(1)} %copy-done.1, f32[128]{0:T(128)S(1)} %get-tuple-element.53, ...), kind=kOutput, calls=%fused_computation.18 | convolution fusion | flops 11010048 | bytes 2166272 | tf_op jit(solution)/shard_map/rhpn,rn->rhp/dot_general | solution.py:62
  33.2 3.6 %fusion.9 = f32[1,32,128]{2,0,1:T(1,128)S(1)} fusion(f32[128]{0:T(128)S(1)} %get-tuple-element.51, f32[32,128]{1,0:T(8,128)S(1)} %get-tuple-element.39, f32[32]{0:T(128)S(1)} %get-tuple-element.44, f32[128]{0:T(128)S(1)} %get-tuple-element.52, f32[32,128]{1,0:T(8,128)S(1)} %get-tuple-element.40, f32[32]{0:T(128)S(1)} %get-tuple-element.45, ...), kind=kOutput, calls=%fused_computation.16 | convolution fusion | flops 12582912 | bytes 2183680 | tf_op jit(solution)/shard_map/rhpn,rn->rhp/dot_general | solution.py:62
  36.9 0.4 fusion.19
  37.3 0.2 copy-done.30
  37.9 0.7 copy.127
  38.6 11.5 %all-to-all-start = ((bf16[32,4,192]{2,1,0:T(4,128)(2,1)}), bf16[32,4,192]{2,1,0:T(4,128)(2,1)S(1)}, u32[]{:S(2)}, u32[]{:S(2)}) async-start(bf16[32,4,192]{2,1,0:T(4,128)(2,1)} %copy.127), calls=%async_computation | async-start | bytes 131072 | tf_op jit(solution)/shard_map/all_to_all | solution.py:71
  50.1 9.9 %all-to-all-done = bf16[32,4,192]{2,1,0:T(4,128)(2,1)S(1)} async-done(((bf16[32,4,192]{2,1,0:T(4,128)(2,1)}), bf16[32,4,192]{2,1,0:T(4,128)(2,1)S(1)}, u32[]{:S(2)}, u32[]{:S(2)}) %all-to-all-start) | async-done | bytes 49184 | tf_op jit(solution)/shard_map/all_to_all | solution.py:71
  60.0 1.5 collective-permute-start
  61.5 1.1 collective-permute-start.1
  62.6 2.2 %collective-permute-start.2 = (bf16[32,4,192]{2,1,0:T(4,128)(2,1)S(1)}, bf16[32,4,192]{2,1,0:T(4,128)(2,1)S(1)}, u32[]{:S(2)}, u32[]{:S(2)}) collective-permute-start(bf16[32,4,192]{2,1,0:T(4,128)(2,1)S(1)} %all-to-all-done), channel_id=1, source_target_pairs={{0,96},{32,0},{64,32},{96,64},{1,97},{33,1},{65,33},{97,65},{2,98}... | collective-permute-start | bytes 147464 | tf_op jit(solution)/shard_map/ppermute | solution.py:78
  64.9 0.1 broadcast_in_dim.144
  65.0 2.4 %collective-permute-done.1 = bf16[32,4,192]{2,1,0:T(4,128)(2,1)S(1)} collective-permute-done((bf16[32,4,192]{2,1,0:T(4,128)(2,1)S(1)}, bf16[32,4,192]{2,1,0:T(4,128)(2,1)S(1)}, u32[]{:S(2)}, u32[]{:S(2)}) %collective-permute-start.1) | collective-permute-done | bytes 49184 | tf_op jit(solution)/shard_map/ppermute | solution.py:78
  67.4 0.2 collective-permute-done.2
  67.6 0.2 pad_maximum_fusion.1
  67.8 0.8 gather_fusion
  68.7 0.2 gather.13
  68.9 0.6 convolution_convert_fusion
  69.4 5.6 %all_to_all.30 = bf16[2,256,1280]{2,1,0:T(8,128)(2,1)} all-to-all(bf16[2,256,1280]{2,1,0:T(8,128)(2,1)S(1)} %bitcast.200), channel_id=1, replica_groups=mesh['grp'=2,'row'=4,'col'=32] {'grp'}, dimensions={0} | all-to-all | bytes 2621440 | tf_op jit(solution)/shard_map/all_to_all | solution.py:71
  75.0 2.5 %reduce_sum.61 = bf16[256,1280]{1,0:T(8,128)(2,1)} reduce(bf16[2,256,1280]{2,1,0:T(8,128)(2,1)} %all_to_all.30, bf16[]{:T(256)} %constant.128.clone.1), dimensions={0}, to_apply=%region_2.3 | reduce | flops 327680 | bytes 1966082 | tf_op jit(solution)/shard_map/reduce_sum | solution.py:127
  77.6 4.0 %all-to-all-start.2 = ((bf16[32,8,1280]{2,1,0:T(8,128)(2,1)}), bf16[32,8,1280]{2,1,0:T(8,128)(2,1)S(1)}, u32[]{:S(2)}, u32[]{:S(2)}) async-start(bf16[32,8,1280]{2,1,0:T(8,128)(2,1)} %bitcast.201), calls=%async_computation.2 | async-start | bytes 1310720 | tf_op jit(solution)/shard_map/all_to_all | solution.py:71
  81.7 0.7 all-gather.6.cloned.1.call-update
  82.4 20.1 %all-to-all-done.2 = bf16[32,8,1280]{2,1,0:T(8,128)(2,1)S(1)} async-done(((bf16[32,8,1280]{2,1,0:T(8,128)(2,1)}), bf16[32,8,1280]{2,1,0:T(8,128)(2,1)S(1)}, u32[]{:S(2)}, u32[]{:S(2)}) %all-to-all-start.2) | async-done | bytes 655392 | tf_op jit(solution)/shard_map/all_to_all | solution.py:71
  102.6 24.4 %all_to_all.31 = bf16[32,8,1280]{2,1,0:T(8,128)(2,1)S(1)} all-to-all(bf16[32,8,1280]{2,1,0:T(8,128)(2,1)S(1)} %broadcast_in_dim.155), channel_id=1, replica_groups=mesh['grp'=2,'row'=4,'col'=32] {'col'}, dimensions={0} | all-to-all | bytes 1310720 | tf_op jit(solution)/shard_map/all_to_all | solution.py:71
  127.0 0.3 multiply_reduce_fusion
  127.4 0.1 copy.134
  127.5 0.8 copy.135
  128.3 2.2 %convolution_convert_fusion.4 = bf16[256,336]{0,1:T(8,128)(2,1)} fusion(bf16[2,2,336,1280]{3,2,1,0:T(8,128)(2,1)} %bitcast.228, bf16[32,8,1280]{2,1,0:T(8,128)(2,1)S(1)} %all_to_all.31), kind=kOutput, calls=%fused_computation.35 | convolution fusion | flops 220286976 | bytes 1687552 | tf_op jit(solution)/shard_map/dot_general | solution.py:138
  130.5 1.1 copy.131
  131.6 2.3 %convolution_convert_fusion.3 = bf16[256,336]{0,1:T(8,128)(2,1)} fusion(bf16[2,2,336,1280]{3,2,1,0:T(8,128)(2,1)} %bitcast.229, bf16[32,8,1280]{2,1,0:T(8,128)(2,1)S(1)} %all_to_all.31), kind=kOutput, calls=%fused_computation.34 | convolution fusion | flops 220286976 | bytes 1687552 | tf_op jit(solution)/shard_map/dot_general | solution.py:138
  133.9 1.7 copy.132
  135.6 2.3 %convolution_convert_fusion.2 = bf16[256,336]{0,1:T(8,128)(2,1)} fusion(bf16[2,2,336,1280]{3,2,1,0:T(8,128)(2,1)} %bitcast.230, bf16[32,8,1280]{2,1,0:T(8,128)(2,1)S(1)} %all_to_all.31), kind=kOutput, calls=%fused_computation.33 | convolution fusion | flops 220286976 | bytes 1687552 | tf_op jit(solution)/shard_map/dot_general | solution.py:138
  137.9 1.7 copy.133
  139.6 2.3 %convolution_convert_fusion.5 = bf16[256,336]{0,1:T(8,128)(2,1)} fusion(bf16[2,2,336,1280]{3,2,1,0:T(8,128)(2,1)} %bitcast.231, bf16[32,8,1280]{2,1,0:T(8,128)(2,1)S(1)} %all_to_all.31), kind=kOutput, calls=%fused_computation.36 | convolution fusion | flops 220286976 | bytes 1687552 | tf_op jit(solution)/shard_map/dot_general | solution.py:138
  141.8 1.1 copy.130
  142.9 2.2 %concatenate.63 = bf16[4,64,1346]{2,1,0:T(8,128)(2,1)} concatenate(bf16[4,64,336]{2,1,0:T(8,128)(2,1)S(1)} %bitcast.207, bf16[4,64,336]{2,1,0:T(8,128)(2,1)S(1)} %bitcast.204, bf16[4,64,336]{2,1,0:T(8,128)(2,1)} %bitcast.205, bf16[4,64,336]{2,1,0:T(8,128)(2,1)} %bitcast.206, bf16[4,64,1]{2,1,0:T(8,128)(2,1)S(1)} %copy.134, bf16[4,64,1]{2,1,0:T(8,128)(2,1)} %copy.135), dimensions={2} | concatenate | bytes 1378304 | tf_op jit(solution)/shard_map/concatenate | solution.py:144
  145.1 5.3 %all-to-all-start.4 = ((bf16[4,64,1346]{2,1,0:T(8,128)(2,1)}), bf16[4,64,1346]{2,1,0:T(8,128)(2,1)S(1)}, u32[]{:S(2)}, u32[]{:S(2)}) async-start(bf16[4,64,1346]{2,1,0:T(8,128)(2,1)} %concatenate.63), calls=%async_computation.4 | async-start | bytes 1441792 | tf_op jit(solution)/shard_map/all_to_all | solution.py:71
  150.4 0.7 all-gather.4.cloned.1.call-update
  151.4 6.7 %all-to-all-done.4 = bf16[4,64,1346]{2,1,0:T(8,128)(2,1)S(1)} async-done(((bf16[4,64,1346]{2,1,0:T(8,128)(2,1)}), bf16[4,64,1346]{2,1,0:T(8,128)(2,1)S(1)}, u32[]{:S(2)}, u32[]{:S(2)}) %all-to-all-start.4) | async-done | bytes 689184 | tf_op jit(solution)/shard_map/all_to_all | solution.py:71
  158.2 0.2 fusion.50
  158.5 0.1 fusion.41
  158.8 0.4 collective-permute-start.3
  159.2 3.5 %collective-permute-start.4 = (bf16[64,672]{1,0:T(8,128)(2,1)S(1)}, bf16[64,672]{1,0:T(8,128)(2,1)S(1)}, u32[]{:S(2)}, u32[]{:S(2)}) collective-permute-start(bf16[64,672]{1,0:T(8,128)(2,1)S(1)} %pad_maximum_fusion.2), channel_id=1, source_target_pairs={{0,64},{32,96},{64,0},{96,32},{1,65},{33,97},{65,1},{97,33},{2,66}... | collective-permute-start | bytes 258056 | tf_op jit(solution)/shard_map/ppermute | solution.py:78
  162.6 0.3 collective-permute-start.5
  162.9 0.5 collective-permute-done.3
  163.4 1.9 collective-permute-done.4
  165.3 2.0 collective-permute-done.5
  167.3 0.6 gather_fusion.1
  168.2 3.0 %fusion.5 = bf16[32,8,1280]{2,1,0:T(8,128)(2,1)} fusion(bf16[256,672]{1,0:T(8,128)(2,1)S(1)} %bitcast_select_fusion, bf16[672,1280]{1,0:T(8,128)(2,1)} %all-gather.4.cloned.1.call-done), kind=kOutput, calls=%fused_computation.10 | convolution fusion | flops 440729600 | bytes 2719744 | tf_op jit(solution)/shard_map/dot_general | solution.py:160
  171.1 6.5 %all-to-all-start.5 = ((bf16[32,8,1280]{2,1,0:T(8,128)(2,1)}), bf16[32,8,1280]{2,1,0:T(8,128)(2,1)S(1)}, u32[]{:S(2)}, u32[]{:S(2)}) async-start(bf16[32,8,1280]{2,1,0:T(8,128)(2,1)} %fusion.5), calls=%async_computation.5 | async-start | bytes 1310720 | tf_op jit(solution)/shard_map/all_to_all | solution.py:71
  178.4 4.7 %select_select_fusion = f32[1,32,128,128]{3,2,1,0:T(8,128)} fusion(f32[1,32,128,128]{3,2,1,0:T(8,128)S(1)} %copy-done.1, f32[128]{0:T(128)S(1)} %copy-done.24, f32[32,128]{1,0:T(8,128)S(1)} %copy-done.9, f32[32]{0:T(128)S(1)} %copy-done.20, f32[128]{0:T(128)S(1)} %copy-done.26, f32[32,128]{1,0:T(8,128)S(1)} %copy-done.11, f32[32]{0:T(128)S(1)} %copy-done.22, ...), kind=kLoop, calls=%fused_computation.24 | loop fusion | flops 8388608 | bytes 4262404 | tf_op jit(solution)/shard_map/jit(_where)/select_n | solution.py:64
  183.1 15.4 %all-to-all-done.5 = bf16[32,8,1280]{2,1,0:T(8,128)(2,1)S(1)} async-done(((bf16[32,8,1280]{2,1,0:T(8,128)(2,1)}), bf16[32,8,1280]{2,1,0:T(8,128)(2,1)S(1)}, u32[]{:S(2)}, u32[]{:S(2)}) %all-to-all-start.5) | async-done | bytes 655392 | tf_op jit(solution)/shard_map/all_to_all | solution.py:71
  198.5 0.6 add_convert_fusion
  (102 shorter events, 1.9 us)
Async XLA Ops:
  7.2 61.7 %copy-start = (bf16[192,1280]{1,0:T(8,128)(2,1)S(1)}, bf16[192,1280]{1,0:T(8,128)(2,1)}, u32[]{:S(2)}) copy-start(bf16[192,1280]{1,0:T(8,128)(2,1)} %param.38) | copy-start | bytes 1474564
  9.5 23.6 %copy-start.23 = (f32[128]{0:T(128)}, f32[128]{0:T(128)S(1)}, u32[]{:S(2)}) copy-start(f32[128]{0:T(128)S(1)} %get-tuple-element.51) | copy-start | bytes 1540
  9.5 23.6 %copy-start.25 = (f32[128]{0:T(128)}, f32[128]{0:T(128)S(1)}, u32[]{:S(2)}) copy-start(f32[128]{0:T(128)S(1)} %get-tuple-element.52) | copy-start | bytes 1540
  9.5 23.6 %copy-start.27 = (f32[128]{0:T(128)}, f32[128]{0:T(128)S(1)}, u32[]{:S(2)}) copy-start(f32[128]{0:T(128)S(1)} %get-tuple-element.53) | copy-start | bytes 1540
  10.4 22.7 %copy-start.17 = (f32[32]{0:T(128)}, f32[32]{0:T(128)S(1)}, u32[]{:S(2)}) copy-start(f32[32]{0:T(128)S(1)} %get-tuple-element.43) | copy-start | bytes 388
  10.4 22.7 %copy-start.19 = (f32[32]{0:T(128)}, f32[32]{0:T(128)S(1)}, u32[]{:S(2)}) copy-start(f32[32]{0:T(128)S(1)} %get-tuple-element.44) | copy-start | bytes 388
  10.4 22.7 %copy-start.21 = (f32[32]{0:T(128)}, f32[32]{0:T(128)S(1)}, u32[]{:S(2)}) copy-start(f32[32]{0:T(128)S(1)} %get-tuple-element.45) | copy-start | bytes 388
  14.0 2.5 %copy-start.16 = (bf16[1,4,2048]{2,1,0:T(4,128)(2,1)S(1)}, bf16[1,4,2048]{2,1,0:T(4,128)(2,1)}, u32[]{:S(2)}) copy-start(bf16[1,4,2048]{2,1,0:T(4,128)(2,1)} %param.22) | copy-start | bytes 49156
  14.0 2.6 %copy-start.32 = (bf16[1,4,512]{2,1,0:T(4,128)(2,1)S(1)}, bf16[1,4,512]{2,1,0:T(4,128)(2,1)}, u32[]{:S(2)}) copy-start(bf16[1,4,512]{2,1,0:T(4,128)(2,1)} %param.23) | copy-start | bytes 12292
  16.6 2.9 %copy-start.2 = (bf16[1,2048,512]{2,1,0:T(8,128)(2,1)S(1)}, bf16[1,2048,512]{2,1,0:T(8,128)(2,1)}, u32[]{:S(2)}) copy-start(bf16[1,2048,512]{2,1,0:T(8,128)(2,1)} %param.26) | copy-start | bytes 6291460
  21.8 4.2 %copy-start.1 = (f32[1,32,128,128]{3,2,1,0:T(8,128)S(1)}, f32[1,32,128,128]{3,2,1,0:T(8,128)}, u32[]{:S(2)}) copy-start(f32[1,32,128,128]{3,2,1,0:T(8,128)} %param.35) | copy-start | bytes 6291460
  21.8 4.2 %copy-start.29 = (bf16[1,4,128]{2,1,0:T(4,128)(2,1)S(1)}, bf16[1,4,128]{2,1,0:T(4,128)(2,1)}, u32[]{:S(2)}) copy-start(bf16[1,4,128]{2,1,0:T(4,128)(2,1)} %param.31) | copy-start | bytes 3076
  26.0 7.2 %copy-start.4 = (f32[32,128]{1,0:T(8,128)}, f32[32,128]{1,0:T(8,128)S(1)}, u32[]{:S(2)}) copy-start(f32[32,128]{1,0:T(8,128)S(1)} %get-tuple-element.38) | copy-start | bytes 49156
  26.0 7.2 %copy-start.8 = (f32[32,128]{1,0:T(8,128)}, f32[32,128]{1,0:T(8,128)S(1)}, u32[]{:S(2)}) copy-start(f32[32,128]{1,0:T(8,128)S(1)} %get-tuple-element.39) | copy-start | bytes 49156
  26.0 7.2 %copy-start.10 = (f32[32,128]{1,0:T(8,128)}, f32[32,128]{1,0:T(8,128)S(1)}, u32[]{:S(2)}) copy-start(f32[32,128]{1,0:T(8,128)S(1)} %get-tuple-element.40) | copy-start | bytes 49156
  26.0 7.2 %copy-start.12 = (f32[32,128]{1,0:T(8,128)}, f32[32,128]{1,0:T(8,128)S(1)}, u32[]{:S(2)}) copy-start(f32[32,128]{1,0:T(8,128)S(1)} %get-tuple-element.41) | copy-start | bytes 49156
  33.2 3.7 %copy-start.3 = (bf16[2048,4,128]{2,0,1:T(8,128)(2,1)S(1)}, bf16[2048,4,128]{2,0,1:T(8,128)(2,1)}, u32[]{:S(2)}) copy-start(bf16[2048,4,128]{2,0,1:T(8,128)(2,1)} %copy.121) | copy-start | bytes 6291460
  33.2 3.7 %copy-start.33 = (bf16[1,4,512]{2,1,0:T(4,128)(2,1)S(1)}, bf16[1,4,512]{2,1,0:T(4,128)(2,1)}, u32[]{:S(2)}) copy-start(bf16[1,4,512]{2,1,0:T(4,128)(2,1)} %param.24) | copy-start | bytes 12292
  36.9 0.7 copy-start.30
  36.9 0.8 copy-start.15
  36.9 13.2 %copy-start.31 = (s32[128]{0:T(128)S(1)}, s32[128]{0:T(128)}, u32[]{:S(2)}) copy-start(s32[128]{0:T(128)} %param.37) | copy-start | bytes 1540
  38.6 21.5 %all-to-all-start = ((bf16[32,4,192]{2,1,0:T(4,128)(2,1)}), bf16[32,4,192]{2,1,0:T(4,128)(2,1)S(1)}, u32[]{:S(2)}, u32[]{:S(2)}) async-start(bf16[32,4,192]{2,1,0:T(4,128)(2,1)} %copy.127), calls=%async_computation | async-start | bytes 131072 | tf_op jit(solution)/shard_map/all_to_all | solution.py:71
  60.0 5.0 %collective-permute-start = (bf16[32,4,192]{2,1,0:T(4,128)(2,1)S(1)}, bf16[32,4,192]{2,1,0:T(4,128)(2,1)S(1)}, u32[]{:S(2)}, u32[]{:S(2)}) collective-permute-start(bf16[32,4,192]{2,1,0:T(4,128)(2,1)S(1)} %all-to-all-done), channel_id=1, source_target_pairs={{0,32},{32,64},{64,96},{96,0},{1,33},{33,65},{65,97},{97,1},{2,34}... | collective-permute-start | bytes 147464 | tf_op jit(solution)/shard_map/ppermute | solution.py:78
  61.5 5.9 %collective-permute-start.1 = (bf16[32,4,192]{2,1,0:T(4,128)(2,1)S(1)}, bf16[32,4,192]{2,1,0:T(4,128)(2,1)S(1)}, u32[]{:S(2)}, u32[]{:S(2)}) collective-permute-start(bf16[32,4,192]{2,1,0:T(4,128)(2,1)S(1)} %all-to-all-done), channel_id=1, source_target_pairs={{0,64},{32,96},{64,0},{96,32},{1,65},{33,97},{65,1},{97,33},{2,66}... | collective-permute-start | bytes 147464 | tf_op jit(solution)/shard_map/ppermute | solution.py:78
  62.6 5.0 %collective-permute-start.2 = (bf16[32,4,192]{2,1,0:T(4,128)(2,1)S(1)}, bf16[32,4,192]{2,1,0:T(4,128)(2,1)S(1)}, u32[]{:S(2)}, u32[]{:S(2)}) collective-permute-start(bf16[32,4,192]{2,1,0:T(4,128)(2,1)S(1)} %all-to-all-done), channel_id=1, source_target_pairs={{0,96},{32,0},{64,32},{96,64},{1,97},{33,1},{65,33},{97,65},{2,98}... | collective-permute-start | bytes 147464 | tf_op jit(solution)/shard_map/ppermute | solution.py:78
  77.6 24.9 %copy-start.6 = (bf16[8,1280]{1,0:T(8,128)(2,1)S(1)}, bf16[8,1280]{1,0:T(8,128)(2,1)}, u32[]{:S(2)}) copy-start(bf16[8,1280]{1,0:T(8,128)(2,1)} %param.21) | copy-start | bytes 61444
  77.6 24.9 %copy-start.14 = (f32[1280]{0:T(1024)S(1)}, f32[1280]{0:T(1024)}, u32[]{:S(2)}) copy-start(f32[1280]{0:T(1024)} %param.39) | copy-start | bytes 15364
  77.6 24.8 %all-to-all-start.2 = ((bf16[32,8,1280]{2,1,0:T(8,128)(2,1)}), bf16[32,8,1280]{2,1,0:T(8,128)(2,1)S(1)}, u32[]{:S(2)}, u32[]{:S(2)}) async-start(bf16[32,8,1280]{2,1,0:T(8,128)(2,1)} %bitcast.201), calls=%async_computation.2 | async-start | bytes 1310720 | tf_op jit(solution)/shard_map/all_to_all | solution.py:71
  81.6 46.7 %all-gather.6.cloned.1.call-start = ((), (), s32[]{:S(2)}) async-start(), calls=%async_computation.7 | async-start | bytes 5160960 | tf_op jit(solution)/shard_map/all_gather | solution.py:110
  145.1 13.0 %all-to-all-start.4 = ((bf16[4,64,1346]{2,1,0:T(8,128)(2,1)}), bf16[4,64,1346]{2,1,0:T(8,128)(2,1)S(1)}, u32[]{:S(2)}, u32[]{:S(2)}) async-start(bf16[4,64,1346]{2,1,0:T(8,128)(2,1)} %concatenate.63), calls=%async_computation.4 | async-start | bytes 1441792 | tf_op jit(solution)/shard_map/all_to_all | solution.py:71
  150.4 17.7 %all-gather.4.cloned.1.call-start = ((), (), s32[]{:S(2)}) async-start(), calls=%async_computation.6 | async-start | bytes 2580480 | tf_op jit(solution)/shard_map/all_gather | solution.py:111
  158.8 4.7 %collective-permute-start.3 = (bf16[64,672]{1,0:T(8,128)(2,1)S(1)}, bf16[64,672]{1,0:T(8,128)(2,1)S(1)}, u32[]{:S(2)}, u32[]{:S(2)}) collective-permute-start(bf16[64,672]{1,0:T(8,128)(2,1)S(1)} %pad_maximum_fusion.2), channel_id=1, source_target_pairs={{0,32},{32,64},{64,96},{96,0},{1,33},{33,65},{65,97},{97,1},{2,34}... | collective-permute-start | bytes 258056 | tf_op jit(solution)/shard_map/ppermute | solution.py:78
  159.2 6.1 %collective-permute-start.4 = (bf16[64,672]{1,0:T(8,128)(2,1)S(1)}, bf16[64,672]{1,0:T(8,128)(2,1)S(1)}, u32[]{:S(2)}, u32[]{:S(2)}) collective-permute-start(bf16[64,672]{1,0:T(8,128)(2,1)S(1)} %pad_maximum_fusion.2), channel_id=1, source_target_pairs={{0,64},{32,96},{64,0},{96,32},{1,65},{33,97},{65,1},{97,33},{2,66}... | collective-permute-start | bytes 258056 | tf_op jit(solution)/shard_map/ppermute | solution.py:78
  162.6 4.6 %collective-permute-start.5 = (bf16[64,672]{1,0:T(8,128)(2,1)S(1)}, bf16[64,672]{1,0:T(8,128)(2,1)S(1)}, u32[]{:S(2)}, u32[]{:S(2)}) collective-permute-start(bf16[64,672]{1,0:T(8,128)(2,1)S(1)} %pad_maximum_fusion.2), channel_id=1, source_target_pairs={{0,96},{32,0},{64,32},{96,64},{1,97},{33,1},{65,33},{97,65},{2,98}... | collective-permute-start | bytes 258056 | tf_op jit(solution)/shard_map/ppermute | solution.py:78
  168.0 10.3 %copy-start.5 = (f32[32,128]{1,0:T(8,128)S(1)}, f32[32,128]{1,0:T(8,128)}, u32[]{:S(2)}) copy-start(f32[32,128]{1,0:T(8,128)} %copy-done.4) | copy-start | bytes 49156
  168.0 10.3 %copy-start.9 = (f32[32,128]{1,0:T(8,128)S(1)}, f32[32,128]{1,0:T(8,128)}, u32[]{:S(2)}) copy-start(f32[32,128]{1,0:T(8,128)} %copy-done.8) | copy-start | bytes 49156
  168.1 10.3 %copy-start.11 = (f32[32,128]{1,0:T(8,128)S(1)}, f32[32,128]{1,0:T(8,128)}, u32[]{:S(2)}) copy-start(f32[32,128]{1,0:T(8,128)} %copy-done.10) | copy-start | bytes 49156
  168.1 10.3 %copy-start.13 = (f32[32,128]{1,0:T(8,128)S(1)}, f32[32,128]{1,0:T(8,128)}, u32[]{:S(2)}) copy-start(f32[32,128]{1,0:T(8,128)} %copy-done.12) | copy-start | bytes 49156
  168.1 10.3 %copy-start.18 = (f32[32]{0:T(128)S(1)}, f32[32]{0:T(128)}, u32[]{:S(2)}) copy-start(f32[32]{0:T(128)} %copy-done.17) | copy-start | bytes 388
  168.1 10.3 %copy-start.20 = (f32[32]{0:T(128)S(1)}, f32[32]{0:T(128)}, u32[]{:S(2)}) copy-start(f32[32]{0:T(128)} %copy-done.19) | copy-start | bytes 388
  168.1 10.3 %copy-start.22 = (f32[32]{0:T(128)S(1)}, f32[32]{0:T(128)}, u32[]{:S(2)}) copy-start(f32[32]{0:T(128)} %copy-done.21) | copy-start | bytes 388
  168.1 10.3 %copy-start.24 = (f32[128]{0:T(128)S(1)}, f32[128]{0:T(128)}, u32[]{:S(2)}) copy-start(f32[128]{0:T(128)} %copy-done.23) | copy-start | bytes 1540
  168.1 10.3 %copy-start.26 = (f32[128]{0:T(128)S(1)}, f32[128]{0:T(128)}, u32[]{:S(2)}) copy-start(f32[128]{0:T(128)} %copy-done.25) | copy-start | bytes 1540
  168.1 10.3 %copy-start.28 = (f32[128]{0:T(128)S(1)}, f32[128]{0:T(128)}, u32[]{:S(2)}) copy-start(f32[128]{0:T(128)} %copy-done.27) | copy-start | bytes 1540
  171.1 27.3 %all-to-all-start.5 = ((bf16[32,8,1280]{2,1,0:T(8,128)(2,1)}), bf16[32,8,1280]{2,1,0:T(8,128)(2,1)S(1)}, u32[]{:S(2)}, u32[]{:S(2)}) async-start(bf16[32,8,1280]{2,1,0:T(8,128)(2,1)} %fusion.5), calls=%async_computation.5 | async-start | bytes 1310720 | tf_op jit(solution)/shard_map/all_to_all | solution.py:71
  178.4 20.1 %copy-start.7 = (bf16[8,1280]{1,0:T(8,128)(2,1)S(1)}, bf16[8,1280]{1,0:T(8,128)(2,1)}, u32[]{:S(2)}) copy-start(bf16[8,1280]{1,0:T(8,128)(2,1)} %param.21) | copy-start | bytes 61444
Sparse Core Ops, SparseCore 0:
  84.3 19.6 all-gather.5
  153.1 11.7 all-gather.3

commit v2 on v1

v2 whole, which is shorter than its diff:
```python
import functools

import jax
import jax.numpy as jnp
from jax import lax
from jax.experimental import pallas as pl
from jax.experimental.pallas import tpu as pltpu
from jax.sharding import PartitionSpec as P

D = 5120
HD = 128
PH = 128


norm_eps = 1e-05


def fetch(pairs, sems):
    copies = [
        pltpu.make_async_copy(source, buffer, sems.at[i])
        for i, (source, buffer) in enumerate(pairs)
    ]
    for copy in copies:
        copy.start()
    return copies


def mixer_kernel(*refs):
    f32 = jnp.float32
    bf16 = jnp.bfloat16
    nt = (((1,), (1,)), ((), ()))
    small, (keys_hbm, values_hbm, state_hbm) = refs[:11], refs[11:14]
    pieces_ref = refs[14]
    buffers, (keys_ref, values_ref, state_ref, mixed_ref, sems, big_sems) = (
        refs[15:26],
        refs[26:],
    )
    copies = fetch(list(zip(small, buffers)), sems)
    kv_heads, _, head_size = keys_ref.shape
    heads = state_ref.shape[0] // kv_heads
    big = []
    for j in range(kv_heads):
        cols = pl.ds(j * head_size, head_size)
        big += [
            (state_hbm.at[0, pl.ds(j * heads, heads)], state_ref.at[pl.ds(j * heads, heads)]),
            (keys_hbm.at[0, :, cols], keys_ref.at[j]),
            (values_hbm.at[0, :, cols], values_ref.at[j]),
        ]
    big = fetch(big, big_sems)
    for copy in copies:
        copy.wait()
    (
        length_ref, query_ref, key_new_ref, value_new_ref, x_ref, gate_ref,
        in_map_ref, out_map_ref, dt_ref, rate_ref, skip_ref,
    ) = buffers
    drafts = query_ref.shape[1]
    groups = query_ref.shape[2] // (kv_heads * head_size)
    attended = query_ref.shape[2]

    dt = dt_ref[0]
    faded = [dt[0:1] * rate_ref[...]]
    for t in range(1, drafts):
        faded.append(faded[-1] + dt[t : t + 1] * rate_ref[...])
    fade = jnp.concatenate(faded, axis=0)
    row = lax.broadcasted_iota(jnp.int32, fade.shape, 0)
    kept = jnp.exp(-fade)
    out_map = out_map_ref[0]
    in_map = in_map_ref[0].astype(f32)
    readout = out_map.astype(f32)
    mixing = []
    for s in range(drafts):
        match = jnp.sum(readout * in_map[s : s + 1, :], axis=1, keepdims=True)
        since = jnp.where(row >= s, fade - faded[s], 0.0)
        share = jnp.where(row >= s, jnp.exp(-since) * match * dt[s : s + 1], 0.0)
        mixing.append(share + jnp.where(row == s, skip_ref[...], 0.0))
    out_maps = jnp.concatenate([out_map, out_map], axis=1)

    for j in range(kv_heads):
        for copy in big[3 * j : 3 * j + 3]:
            copy.wait()
        state = state_ref[j * heads : (j + 1) * heads].reshape(heads * PH, state_ref.shape[2])
        high = state.astype(bf16)
        low = (state - high.astype(f32)).astype(bf16)
        carried = lax.dot_general(
            out_maps, jnp.concatenate([high, low], axis=1), nt, preferred_element_type=f32
        )
        for i in range(heads):
            h = j * heads + i
            cols = slice(h * PH, (h + 1) * PH)
            inputs = x_ref[0, :, cols].astype(f32)
            gate = gate_ref[0, :, cols].astype(f32)
            y = kept[:, h : h + 1] * carried[:, i * PH : (i + 1) * PH]
            for s in range(drafts):
                y = y + mixing[s][:, h : h + 1] * inputs[s : s + 1]
            cols = slice(attended + h * PH, attended + (h + 1) * PH)
            mixed_ref[:, cols] = y * gate * jax.nn.sigmoid(gate)

        first = j * groups * head_size
        query = query_ref[0, :, first : first + groups * head_size].astype(f32)
        queries = jnp.concatenate(
            [query[:, g * head_size : (g + 1) * head_size] for g in range(groups)], axis=0
        )
        scores = lax.dot_general(
            queries.astype(bf16), keys_ref[j], nt, preferred_element_type=f32
        ) * head_size ** (-0.5)
        position = lax.broadcasted_iota(jnp.int32, scores.shape, 1)
        scores = jnp.where(position < length_ref[...], scores, -jnp.inf)
        peak = jnp.max(scores, axis=1, keepdims=True)
        draft = lax.broadcasted_iota(jnp.int32, peak.shape, 0) % drafts
        new_cols = slice(j * head_size, (j + 1) * head_size)
        keys_new = key_new_ref[0, :, new_cols].astype(f32)
        scores_new = []
        for u in range(drafts):
            score = jnp.sum(queries * keys_new[u : u + 1, :], axis=1, keepdims=True)
            score = jnp.where(draft >= u, score * head_size ** (-0.5), -jnp.inf)
            scores_new.append(score)
            peak = jnp.maximum(peak, score)
        weights = jnp.exp(scores - peak)
        total = jnp.sum(weights, axis=1, keepdims=True)
        summed = jnp.dot(weights.astype(bf16), values_ref[j], preferred_element_type=f32)
        values_new = value_new_ref[0, :, new_cols].astype(f32)
        for u in range(drafts):
            weight = jnp.exp(scores_new[u] - peak)
            total = total + weight
            summed = summed + weight.astype(bf16).astype(f32) * values_new[u : u + 1, :]
        result = summed / total
        for g in range(groups):
            cols = slice(first + g * head_size, first + (g + 1) * head_size)
            mixed_ref[:, cols] = result[g * drafts : (g + 1) * drafts]
    width = pieces_ref.shape[2]
    for c in range(pieces_ref.shape[0]):
        pieces_ref[c] = mixed_ref[:, c * width : (c + 1) * width].astype(bf16)


def mix(
    cols, query, key_new, value_new, key_cache, value_cache, ctx_len,
    ssm_x, ssm_gate, ssm_b, ssm_c, ssm_dt, decay_rate, skip_gain, ssm_state,
):
    kv_heads = key_new.shape[2] // HD
    features = query.shape[2] + ssm_x.shape[2]
    ctx_len = ctx_len.reshape(1, 1)
    small = (
        ctx_len, query, key_new, value_new, ssm_x, ssm_gate, ssm_b, ssm_c, ssm_dt,
        decay_rate.reshape(1, -1), skip_gain.reshape(1, -1),
    )
    big = (key_cache, value_cache, ssm_state)
    cached = (kv_heads, key_cache.shape[1], HD)
    return pl.pallas_call(
        mixer_kernel,
        in_specs=[pl.BlockSpec(memory_space=pltpu.HBM)] * (len(small) + len(big)),
        out_specs=pl.BlockSpec(memory_space=pltpu.VMEM),
        out_shape=jax.ShapeDtypeStruct((cols, query.shape[1], features // cols), jnp.bfloat16),
        scratch_shapes=[pltpu.VMEM(array.shape, array.dtype) for array in small]
        + [
            pltpu.VMEM(cached, key_cache.dtype),
            pltpu.VMEM(cached, value_cache.dtype),
            pltpu.VMEM(ssm_state.shape[1:], ssm_state.dtype),
            pltpu.VMEM((query.shape[1], features), jnp.float32),
            pltpu.SemaphoreType.DMA((len(small),)),
            pltpu.SemaphoreType.DMA((3 * kv_heads,)),
        ],
        compiler_params=pltpu.CompilerParams(vmem_limit_bytes=62 * 2**20),
        name="mixer",
    )(*small, *big)


def project_kernel(rows_ref, weights_ref, *out_refs):
    product = jnp.dot(rows_ref[...], weights_ref[...], preferred_element_type=jnp.float32)
    share = out_refs[0].shape[0]
    for i, out_ref in enumerate(out_refs):
        out_ref[...] = product[i * share : (i + 1) * share].astype(out_ref.dtype)


def merge_kernel(rows_ref, weights_ref, *refs):
    parts, out_ref = refs[:-1], refs[-1]
    product = jnp.dot(rows_ref[...], weights_ref[...], preferred_element_type=jnp.float32)
    share = parts[0].shape[0]
    for i, part in enumerate(parts):
        rows = slice(i * share, (i + 1) * share)
        out_ref[rows] = (product[rows] + part[...].astype(jnp.float32)).astype(out_ref.dtype)


def on_core(kernel, operands, out_shape, name, after=()):
    vmem = pl.BlockSpec(memory_space=pltpu.VMEM)
    count = len(operands)
    return pl.pallas_call(
        lambda *refs: kernel(*refs[:count], *refs[count + len(after) :]),
        in_specs=[vmem] * count + [pl.BlockSpec(memory_space=pl.ANY)] * len(after),
        out_specs=jax.tree.map(lambda _: vmem, out_shape),
        out_shape=out_shape,
        compiler_params=pltpu.CompilerParams(vmem_limit_bytes=16 * 2**20),
        name=name,
    )(*operands, *after)


def arrive_kernel(parts_ref, resid_ref, gain_ref, stream_ref, spread_ref):
    f32 = jnp.float32
    stream = resid_ref[...].astype(f32)
    for c in range(parts_ref.shape[0]):
        stream = stream + parts_ref[c].astype(f32)
    stream_ref[...] = stream
    scaled = (stream * gain_ref[...]).astype(spread_ref.dtype)
    for c in range(spread_ref.shape[0]):
        spread_ref[c] = scaled


def widen_kernel(rows, places, gain_ref, *refs):
    f32 = jnp.float32
    bf16 = jnp.bfloat16
    tokens, weights = refs[:rows], refs[rows : rows + len(places)]
    outs, ordered_ref = refs[rows + len(places) : -1], refs[-1]
    row = lax.axis_index("row")
    share = outs[0].shape[0]
    for q in range(rows):
        first = pl.multiple_of(lax.rem(q + rows - row, rows) * share, share)
        ordered_ref[pl.ds(first, share)] = tokens[q][...]
    for place, weight in zip(places, weights):
        units = weight.shape[0]
        sums = lax.dot_general(
            ordered_ref[...], weight[...], (((1,), (1,)), ((), ())), preferred_element_type=f32
        )
        if place + units == sum(w.shape[0] for w in weights):
            inverse = 1.0 / gain_ref[...]
            plain = ordered_ref[...].astype(f32) * inverse
            squares = jnp.sum(plain * plain, axis=1, keepdims=True)
            high = squares.astype(bf16).astype(f32)
            past = outs[0].shape[1] - (place + units)
            lane = lax.broadcasted_iota(jnp.int32, (squares.shape[0], past), 1)
            tail = jnp.where(lane == 0, high, jnp.where(lane == 1, squares - high, 0.0))
            sums = jnp.concatenate([sums, tail], axis=1)
        sums = sums.astype(bf16)
        for d in range(rows):
            outs[d][:, place : place + sums.shape[1]] = sums[d * share : (d + 1) * share]


def widen(tokens, gain, weights, places, rows):
    units = sum(weight.shape[0] for weight in weights)
    width = (units // 128 + 1) * 128
    share, depth = tokens[0].shape
    vmem = pl.BlockSpec(memory_space=pltpu.VMEM)
    return pl.pallas_call(
        functools.partial(widen_kernel, rows, places),
        in_specs=[vmem] * (1 + rows + len(weights)),
        out_specs=[vmem] * rows,
        out_shape=[jax.ShapeDtypeStruct((share, width), jnp.bfloat16)] * rows,
        scratch_shapes=[pltpu.VMEM((rows * share, depth), jnp.bfloat16)],
        compiler_params=pltpu.CompilerParams(vmem_limit_bytes=16 * 2**20),
        name="widen",
    )(gain, *tokens, *weights)


def narrow_kernel(rows, places, *refs):
    hidden_refs, weights = refs[:rows], refs[rows : rows + len(places)]
    outs, ordered_ref = refs[rows + len(places) : -1], refs[-1]
    row = lax.axis_index("row")
    share = hidden_refs[0].shape[0]
    for d in range(rows):
        first = pl.multiple_of(lax.rem(row + rows - d, rows) * share, share)
        ordered_ref[pl.ds(first, share)] = hidden_refs[d][...]
    down = None
    for place, weight in zip(places, weights):
        part = jnp.dot(
            ordered_ref[:, place : place + weight.shape[0]],
            weight[...],
            preferred_element_type=jnp.float32,
        )
        down = part if down is None else down + part
    down = down.astype(outs[0].dtype)
    for d in range(rows):
        outs[d][...] = down[d * share : (d + 1) * share]


def narrow(hidden, weights, places):
    rows = len(hidden)
    share, units = hidden[0].shape
    vmem = pl.BlockSpec(memory_space=pltpu.VMEM)
    return pl.pallas_call(
        functools.partial(narrow_kernel, rows, places),
        in_specs=[vmem] * (rows + len(weights)),
        out_specs=[vmem] * rows,
        out_shape=[jax.ShapeDtypeStruct((share, weights[0].shape[1]), jnp.bfloat16)] * rows,
        scratch_shapes=[pltpu.VMEM((rows * share, units), jnp.bfloat16)],
        compiler_params=pltpu.CompilerParams(vmem_limit_bytes=16 * 2**20),
        name="narrow",
    )(*hidden, *weights)


def state_kernel(accepted_ref, x_ref, in_map_ref, dt_ref, rate_ref, state_ref, *refs):
    f32 = jnp.float32
    out_ref = refs[-1]
    heads = state_ref.shape[1]
    dt = dt_ref[0]
    drafts = dt.shape[0]
    row = lax.broadcasted_iota(jnp.int32, dt.shape, 0)
    lane = lax.broadcasted_iota(jnp.int32, dt.shape, 1)
    taken = row < accepted_ref[0]
    step = jnp.where(taken, dt, 0.0) * rate_ref[...]
    after = [jnp.zeros_like(step[:1])]
    for t in range(drafts - 1, 0, -1):
        after.insert(0, after[0] + step[t : t + 1])
    whole = jnp.exp(-(after[0] + step[:1]))
    share = jnp.where(taken, jnp.exp(-jnp.concatenate(after, axis=0)) * dt, 0.0)
    terms = []
    for i in range(heads):
        mine = lane == pl.program_id(0) * heads + i
        part = jnp.sum(jnp.where(mine, share, 0.0), axis=1, keepdims=True)
        terms.append(part * x_ref[0, :, i * PH : (i + 1) * PH].astype(f32))
    added = lax.dot_general(
        jnp.concatenate(terms, axis=1),
        in_map_ref[0].astype(f32),
        (((0,), (0,)), ((), ())),
        precision=lax.Precision.HIGHEST,
        preferred_element_type=f32,
    )
    for i in range(heads):
        mine = lane[:1] == pl.program_id(0) * heads + i
        keep = jnp.sum(jnp.where(mine, whole, 0.0), axis=1, keepdims=True)
        out_ref[0, i] = keep * state_ref[0, i] + added[i * PH : (i + 1) * PH]


def final_state(ssm_x, ssm_b, ssm_dt, decay_rate, ssm_state, accepted, after):
    steps = 4
    heads = ssm_state.shape[1] // steps

    def whole(array):
        return pl.BlockSpec(array.shape, lambda j: (0,) * array.ndim)

    decay_rate = decay_rate.reshape(1, -1)
    block = pl.BlockSpec((1, heads) + ssm_state.shape[2:], lambda j: (0, j, 0, 0))
    return pl.pallas_call(
        state_kernel,
        grid=(steps,),
        in_specs=[
            pl.BlockSpec(memory_space=pltpu.SMEM),
            pl.BlockSpec(ssm_x.shape[:2] + (heads * PH,), lambda j: (0, 0, j)),
            whole(ssm_b),
            whole(ssm_dt),
            whole(decay_rate),
            block,
            pl.BlockSpec(memory_space=pl.ANY),
        ],
        out_specs=block,
        out_shape=jax.ShapeDtypeStruct(ssm_state.shape, ssm_state.dtype),
        compiler_params=pltpu.CompilerParams(vmem_limit_bytes=16 * 2**20),
        name="final_state",
    )(accepted, ssm_x, ssm_b, ssm_dt, decay_rate, ssm_state, after)


def exchange(blocks, axis, groups=None):
    return lax.all_to_all(blocks, axis, 0, 0, tiled=True, axis_index_groups=groups)


def shifted(blocks, axis):
    size = lax.axis_size(axis)
    return [blocks[0]] + [
        lax.ppermute(blocks[shift], axis, [(k, (k + shift) % size) for k in range(size)])
        for shift in range(1, size)
    ]


def around(blocks, size, sign):
    outer = lax.axis_size("col") // size
    return [blocks[0]] + [
        lax.ppermute(
            blocks[shift],
            "col",
            [
                (o * size + i, o * size + (i + sign * shift) % size)
                for o in range(outer)
                for i in range(size)
            ],
        )
        for shift in range(1, size)
    ]


def from_partner(weights, cut):
    swap = [(0, 1), (1, 0)]
    return [
        lax.ppermute(weights[first : first + cut], "grp", swap)
        for first in range(0, weights.shape[0], cut)
    ]


def shards(
    resid,
    query,
    key_new,
    value_new,
    key_cache,
    value_cache,
    ctx_len,
    ssm_x,
    ssm_gate,
    ssm_b,
    ssm_c,
    ssm_dt,
    decay_rate,
    skip_gain,
    ssm_state,
    accepted,
    slot_of,
    w_out,
    norm_gain,
    gate_up,
    w_down,
):
    f32 = jnp.float32
    bf16 = jnp.bfloat16
    rows = lax.axis_size("row")
    cols = lax.axis_size("col")
    steps_new = query.shape[1]
    inner = 4
    lines = [[o * inner + i for o in range(cols // inner)] for i in range(inner)]
    pieces = mix(
        cols, query, key_new, value_new, key_cache, value_cache, ctx_len,
        ssm_x, ssm_gate, ssm_b, ssm_c, ssm_dt, decay_rate, skip_gain, ssm_state,
    )
    width = pieces.shape[2]
    mine = exchange(pieces, "col")
    by_slot = jnp.concatenate(shifted([mine] * rows, "row"), axis=0)
    behind = (lax.axis_index("row") - slot_of // cols) % rows
    place = (behind * cols + slot_of % cols).reshape(2, -1)
    other = lax.axis_index("grp") ^ 1
    place = jnp.where(other == 0, place, place[::-1]).reshape(-1)
    mixed_req = jnp.take(by_slot, place, axis=0).reshape(2, -1, width)
    swap = [(0, 1), (1, 0)]
    sent = jax.ShapeDtypeStruct((mixed_req.shape[1] // 2, w_out.shape[1]), bf16)
    for_other = on_core(project_kernel, (mixed_req[0], w_out), [sent] * 2, "project")
    from_other = [lax.ppermute(part, "grp", swap) for part in for_other]
    held = jax.ShapeDtypeStruct((mixed_req.shape[1], w_out.shape[1]), bf16)
    half = on_core(merge_kernel, (mixed_req[1], w_out, *from_other), held, "merge")
    half, gate_up, w_down, gain = lax.optimization_barrier((half, gate_up, w_down, norm_gain))
    state_next = final_state(ssm_x, ssm_b, ssm_dt, decay_rate, ssm_state, accepted, half)
    half = exchange(half.reshape(cols, -1, half.shape[1]), "col")
    units = gate_up.shape[2]
    in_weights = jnp.transpose(gate_up, (1, 2, 0)).reshape(2 * units, -1)
    in_pieces = from_partner(in_weights, 128)
    whole = 2 * units // 128
    in_places = [128 * i for i in range(whole)] + [128 * whole + 2 * units, 128 * whole]
    if 2 * units % 128 == 0:
        in_places = in_places[:-2] + in_places[-1:]
    in_pieces = in_pieces + [in_weights]
    down_pieces = from_partner(w_down, 128) + [w_down]
    padded = -(-units // 128) * 128
    down_places = list(range(0, units, 128)) + [padded]
    gain = gain.reshape(1, -1)
    stream, spread = on_core(
        arrive_kernel,
        (half, resid, gain),
        [
            jax.ShapeDtypeStruct(resid.shape, f32),
            jax.ShapeDtypeStruct((cols // inner,) + resid.shape, bf16),
        ],
        "arrive",
    )
    spread = exchange(spread, "col", lines)
    tokens = [
        block.reshape(-1, block.shape[2]) for block in around([spread] * inner, inner, 1)
    ]
    sums = shifted(widen(tokens, gain, in_pieces, in_places, rows), "row")
    summed = functools.reduce(jnp.add, [part.astype(f32) for part in sums])
    mean_sq = (summed[:, 4 * units] + summed[:, 4 * units + 1]) / D
    summed = summed * lax.rsqrt(mean_sq[:, None] + norm_eps)
    first = 128 * whole
    gate = [summed[:, :units], summed[:, first : first + units]]
    up = [
        jnp.concatenate(
            [summed[:, units:first], summed[:, first + 2 * units : 4 * units]], axis=1
        ),
        summed[:, first + units : first + 2 * units],
    ]
    hidden = [(jax.nn.silu(g) * u).astype(bf16) for g, u in zip(gate, up)]
    blank = jnp.zeros((hidden[0].shape[0], padded - units), bf16)
    hidden = jnp.concatenate([hidden[0], blank, hidden[1]], axis=1)
    down = narrow(shifted([hidden] * rows, "row"), down_pieces, down_places)
    down = around(down, inner, -1)
    down = functools.reduce(jnp.add, [part.astype(f32) for part in down]).astype(bf16)
    down = exchange(down.reshape(cols // inner, -1, down.shape[1]), "col", lines)
    layer_out = (stream + jnp.sum(down.astype(f32), axis=0)).astype(bf16)
    return (layer_out, state_next)


def solution(mesh):
    placed = (
        P(("grp", "col"), "row"),
        P(("row", "col"), None, "grp"),
        P(("row", "col"), None, "grp"),
        P(("row", "col"), None, "grp"),
        P(("row", "col"), None, "grp"),
        P(("row", "col"), None, "grp"),
        P(("row", "col")),
        P(("row", "col"), None, "grp"),
        P(("row", "col"), None, "grp"),
        P(("row", "col"), None, None),
        P(("row", "col"), None, None),
        P(("row", "col"), None, "grp"),
        P("grp"),
        P("grp"),
        P(("row", "col"), "grp", None, None),
        P(("row", "col")),
        P(),
        P(("grp", "col"), "row"),
        P("row"),
        P("row", None, ("grp", "col")),
        P(("grp", "col"), "row"),
    )
    return jax.shard_map(
        shards,
        mesh=mesh,
        in_specs=placed,
        out_specs=(P(("grp", "col"), "row"), P(("row", "col"), "grp", None, None)),
        check_vma=False,
    )
```

time: 207 us -> 139 us (0.67)
  blocking collectives: 30 us -> 0 us
  matrix products: 26.4 us -> 0 us
  local copies, waits for them, and re-layouts: 24.8 us -> 2.93 us
  Pallas kernels: 0 us -> 17.3 us
  between operations: 16 us -> 2.24 us
  starting transfers between devices: 36.3 us -> 49.7 us
  other arithmetic: 12.1 us -> 2.4 us
  waiting for transfers between devices: 60.4 us -> 62.9 us
    all_to_all x2 -> x0, blocking collectives: 30 us -> none  [exchange(): return lax.all_to_all(blocks, axis, 0, 0, tiled=True)]
    dot_general x11 -> x0, matrix products: 23.7 us -> none  [the longest x4 10.7 us: ssm_scan(): jnp.einsum('rhpn,rn->rhp', state, out_map[:, t], precision=lax.Precision....]
    ppermute x6 -> x26, starting transfers between devices: 8.93 us -> 27.1 us  [the longest x9 14.1 us: shifted(): lax.ppermute(blocks[shift], axis, [(k, (k + shift) % size) for k in range...]
    pallas_call x0 -> x7, Pallas kernels: none -> 17.3 us  [the longest x1 6.27 us: mix(): pl.pallas_call(mixer_kernel, in_specs=[pl.BlockSpec(memory_space=pltpu.HB...]
    ppermute x6 -> x26, waiting for transfers between devices: 6.91 us -> 21.8 us  [the longest x9 11.3 us: shifted(): lax.ppermute(blocks[shift], axis, [(k, (k + shift) % size) for k in range...]
    all_to_all x4, waiting for transfers between devices: 52.1 us -> 41.1 us  [exchange(): lax.all_to_all(blocks, axis, 0, 0, tiled=True, axis_index_groups=groups)]
    concatenate x3 -> x1, local copies, waits for them, and re-layouts: 8.73 us -> 0.08 us  [shards(): hidden = jnp.concatenate([hidden[0], blank, hidden[1]], axis=1)]
    convert_element_type x6 -> x0, local copies, waits for them, and re-layouts: 6.52 us -> none  [the longest x4 5.61 us: shards(): sums = [lax.dot_general(tokens, in_weights[g, k], (((1,), (1,)), ((), ())...]
  transfers between devices with their start and end apart: 12 -> 30, of which waited for: 9 -> 19; matrix products, arithmetic and copies ran while one was open for 4% -> 2% of each run, Pallas kernels for 0% -> 3%
where the time goes in v2:
time: 139 us; the launch traced here: 137 us
  waiting for transfers between devices  62.9 us (45%)
  starting transfers between devices  49.7 us (36%)
  Pallas kernels  17.3 us (12%)
  local copies, waits for them, and re-layouts  2.93 us (2%)
  other arithmetic  2.4 us (2%)
  between operations  2.24 us (2%)
    all_to_all x4, waiting for transfers between devices, exchange(): lax.all_to_all(blocks, axis, 0, 0, tiled=True, axis_index_groups=groups)  41.1 us
    all_to_all x4, starting transfers between devices, exchange(): lax.all_to_all(blocks, axis, 0, 0, tiled=True, axis_index_groups=groups)  22.6 us
    ppermute x9, starting transfers between devices, shifted(): lax.ppermute(blocks[shift], axis, [(k, (k + shift) % size) for k in range...  14.1 us
    ppermute x9, waiting for transfers between devices, shifted(): lax.ppermute(blocks[shift], axis, [(k, (k + shift) % size) for k in range...  11.3 us
    ppermute x6, starting transfers between devices, around(): lax.ppermute(blocks[shift], 'col', [(o * size + i, o * size + (i + sign *...  10.5 us
    ppermute x6, waiting for transfers between devices, around(): lax.ppermute(blocks[shift], 'col', [(o * size + i, o * size + (i + sign *...  8.06 us
    pallas_call x1, Pallas kernels, mix(): pl.pallas_call(mixer_kernel, in_specs=[pl.BlockSpec(memory_space=pltpu.HB...  6.27 us
    pallas_call x1, Pallas kernels, final_state(): pl.pallas_call(state_kernel, grid=(steps,), in_specs=[pl.BlockSpec(memory...  4.02 us
  transfers between devices with their start and end apart: 30, of which 19 were waited for; matrix products, arithmetic and copies ran while one was open for 2% of the time, Pallas kernels for 3%

profile of v2, /device:TPU:2, one launch (start us, length us, event | category | flops | bytes accessed | tf_op | source)
XLA Modules:
  0.0 137.4 jit_solution(17983071229044969455)
XLA Ops:
  1.3 6.3 %mixer.1 = bf16[32,4,192]{2,1,0:T(4,128)(2,1)} custom-call(s32[1,1]{1,0:T(1,128)} %bitcast.15.refs_0_, bf16[1,4,2048]{2,1,0:T(4,128)(2,1)} %refs_1_.4, bf16[1,4,512]{2,1,0:T(4,128)(2,1)} %refs_2_.1, bf16[1,4,512]{2,1,0:T(4,128)(2,1)} %refs_3_.1, bf16[1,4,4096]{2,1,0:T(4,128)(2,1)} %x_ref.1, bf16[1,4,4096]{2,1,0:T(4,128)(2,1)} %refs_5_.1, ...), custom_call_target="tpu_custom_call" | custom-call | tf_op jit(solution)/shard_map/mixer/pallas_call | solution.py:148
  7.6 11.6 %all-to-all-start = ((bf16[32,4,192]{2,1,0:T(4,128)(2,1)}), bf16[32,4,192]{2,1,0:T(4,128)(2,1)S(1)}, u32[]{:S(2)}, u32[]{:S(2)}) async-start(bf16[32,4,192]{2,1,0:T(4,128)(2,1)} %mixer.1), calls=%async_computation | async-start | bytes 131072 | tf_op jit(solution)/shard_map/all_to_all | solution.py:350
  19.6 9.6 %all-to-all-done = bf16[32,4,192]{2,1,0:T(4,128)(2,1)S(1)} async-done(((bf16[32,4,192]{2,1,0:T(4,128)(2,1)}), bf16[32,4,192]{2,1,0:T(4,128)(2,1)S(1)}, u32[]{:S(2)}, u32[]{:S(2)}) %all-to-all-start) | async-done | bytes 49184 | tf_op jit(solution)/shard_map/all_to_all | solution.py:350
  29.2 0.5 collective-permute-start.2
  29.7 2.4 %collective-permute-start.1 = (bf16[32,4,192]{2,1,0:T(4,128)(2,1)S(1)}, bf16[32,4,192]{2,1,0:T(4,128)(2,1)S(1)}, u32[]{:S(2)}, u32[]{:S(2)}) collective-permute-start(bf16[32,4,192]{2,1,0:T(4,128)(2,1)S(1)} %all-to-all-done), channel_id=1, source_target_pairs={{0,64},{32,96},{64,0},{96,32},{1,65},{33,97},{65,1},{97,33},{2,66}... | collective-permute-start | bytes 147464 | tf_op jit(solution)/shard_map/ppermute | solution.py:356
  32.1 1.8 %collective-permute-start = (bf16[32,4,192]{2,1,0:T(4,128)(2,1)S(1)}, bf16[32,4,192]{2,1,0:T(4,128)(2,1)S(1)}, u32[]{:S(2)}, u32[]{:S(2)}) collective-permute-start(bf16[32,4,192]{2,1,0:T(4,128)(2,1)S(1)} %all-to-all-done), channel_id=1, source_target_pairs={{0,32},{32,64},{64,96},{96,0},{1,33},{33,65},{65,97},{97,1},{2,34}... | collective-permute-start | bytes 147464 | tf_op jit(solution)/shard_map/ppermute | solution.py:356
  34.0 1.5 %collective-permute-done.1 = bf16[32,4,192]{2,1,0:T(4,128)(2,1)S(1)} collective-permute-done((bf16[32,4,192]{2,1,0:T(4,128)(2,1)S(1)}, bf16[32,4,192]{2,1,0:T(4,128)(2,1)S(1)}, u32[]{:S(2)}, u32[]{:S(2)}) %collective-permute-start.1) | collective-permute-done | bytes 49184 | tf_op jit(solution)/shard_map/ppermute | solution.py:356
  35.5 0.9 collective-permute-done
  36.4 0.2 pad_maximum_fusion
  36.6 0.8 gather_fusion
  37.5 0.2 broadcast_select_fusion
  37.7 0.1 fusion.13
  37.9 1.0 project.1
  38.9 0.5 collective-permute-start.4
  39.5 1.7 %collective-permute-done.3.refs_2_ = bf16[128,1280]{1,0:T(8,128)(2,1)S(1)} collective-permute-done((bf16[128,1280]{1,0:T(8,128)(2,1)}, bf16[128,1280]{1,0:T(8,128)(2,1)S(1)}, u32[]{:S(2)}, u32[]{:S(2)}) %collective-permute-start.3) | collective-permute-done | bytes 327712 | tf_op jit(solution)/shard_map/ppermute | solution.py:430
  41.2 1.2 merge.1.refs_0_
  42.4 4.0 %all-to-all-start.1 = ((bf16[32,8,1280]{2,1,0:T(8,128)(2,1)}), bf16[32,8,1280]{2,1,0:T(8,128)(2,1)S(1)}, u32[]{:S(2)}, u32[]{:S(2)}) async-start(bf16[32,8,1280]{2,1,0:T(8,128)(2,1)} %bitcast.4), calls=%async_computation.1 | async-start | bytes 1310720 | tf_op jit(solution)/shard_map/all_to_all | solution.py:350
  46.4 1.2 fusion.11
  47.6 0.1 collective-permute-start.8
  47.8 0.4 collective-permute-start.9
  48.1 0.1 collective-permute-start.10
  48.3 18.9 %all-to-all-done.1.refs_0_ = bf16[32,8,1280]{2,1,0:T(8,128)(2,1)S(1)} async-done(((bf16[32,8,1280]{2,1,0:T(8,128)(2,1)}), bf16[32,8,1280]{2,1,0:T(8,128)(2,1)S(1)}, u32[]{:S(2)}, u32[]{:S(2)}) %all-to-all-start.1) | async-done | bytes 655392 | tf_op jit(solution)/shard_map/all_to_all | solution.py:350
  67.2 0.8 arrive.1
  68.0 3.5 %all-to-all-start.2 = ((bf16[8,8,1280]{2,1,0:T(8,128)(2,1)}), bf16[8,8,1280]{2,1,0:T(8,128)(2,1)S(1)}, u32[]{:S(2)}, u32[]{:S(2)}) async-start(bf16[8,8,1280]{2,1,0:T(8,128)(2,1)} %get-tuple-element.23), calls=%async_computation.2 | async-start | bytes 327680 | tf_op jit(solution)/shard_map/all_to_all | solution.py:350
  71.5 0.1 collective-permute-start.13
  71.6 0.5 collective-permute-start.11
  72.1 0.8 collective-permute-done.13.refs_9_
  72.9 0.2 collective-permute-start.12
  73.1 7.9 %all-to-all-done.2 = bf16[8,8,1280]{2,1,0:T(8,128)(2,1)S(1)} async-done(((bf16[8,8,1280]{2,1,0:T(8,128)(2,1)}), bf16[8,8,1280]{2,1,0:T(8,128)(2,1)S(1)}, u32[]{:S(2)}, u32[]{:S(2)}) %all-to-all-start.2) | async-done | bytes 163872 | tf_op jit(solution)/shard_map/all_to_all | solution.py:350
  80.9 0.9 collective-permute-start.5
  81.9 2.7 %collective-permute-start.6 = (bf16[8,8,1280]{2,1,0:T(8,128)(2,1)S(1)}, bf16[8,8,1280]{2,1,0:T(8,128)(2,1)S(1)}, u32[]{:S(2)}, u32[]{:S(2)}) collective-permute-start(bf16[8,8,1280]{2,1,0:T(8,128)(2,1)S(1)} %all-to-all-done.2), channel_id=1, source_target_pairs={{0,2},{1,3},{2,0},{3,1},{4,6},{5,7},{6,4},{7,5},{8,10},{9,11},{10,... | collective-permute-start | bytes 491528 | tf_op jit(solution)/shard_map/ppermute | solution.py:364
  84.6 1.5 %collective-permute-start.7 = (bf16[8,8,1280]{2,1,0:T(8,128)(2,1)S(1)}, bf16[8,8,1280]{2,1,0:T(8,128)(2,1)S(1)}, u32[]{:S(2)}, u32[]{:S(2)}) collective-permute-start(bf16[8,8,1280]{2,1,0:T(8,128)(2,1)S(1)} %all-to-all-done.2), channel_id=1, source_target_pairs={{0,3},{1,0},{2,1},{3,2},{4,7},{5,4},{6,5},{7,6},{8,11},{9,8},{10,9... | collective-permute-start | bytes 491528 | tf_op jit(solution)/shard_map/ppermute | solution.py:364
  86.1 2.1 %collective-permute-done.5 = bf16[8,8,1280]{2,1,0:T(8,128)(2,1)S(1)} collective-permute-done((bf16[8,8,1280]{2,1,0:T(8,128)(2,1)S(1)}, bf16[8,8,1280]{2,1,0:T(8,128)(2,1)S(1)}, u32[]{:S(2)}, u32[]{:S(2)}) %collective-permute-start.5) | collective-permute-done | bytes 163872 | tf_op jit(solution)/shard_map/ppermute | solution.py:364
  88.3 1.8 %collective-permute-done.6 = bf16[8,8,1280]{2,1,0:T(8,128)(2,1)S(1)} collective-permute-done((bf16[8,8,1280]{2,1,0:T(8,128)(2,1)S(1)}, bf16[8,8,1280]{2,1,0:T(8,128)(2,1)S(1)}, u32[]{:S(2)}, u32[]{:S(2)}) %collective-permute-start.6) | collective-permute-done | bytes 163872 | tf_op jit(solution)/shard_map/ppermute | solution.py:364
  90.1 3.0 %widen.1 = (bf16[64,1408]{1,0:T(8,128)(2,1)S(1)}, bf16[64,1408]{1,0:T(8,128)(2,1)S(1)}, bf16[64,1408]{1,0:T(8,128)(2,1)S(1)}, bf16[64,1408]{1,0:T(8,128)(2,1)S(1)}) custom-call(f32[1,1280]{1,0:T(1,128)S(1)} %reshape.94.refs_2_.gain_ref, bf16[64,1280]{1,0:T(8,128)(2,1)S(1)} %bitcast.19, bf16[64,1280]{1,0:T(8,128)(2,1)S(1)} %bitcast.20, ...), custom_call_target="tpu_custom_call" | custom-call | tf_op jit(solution)/shard_map/widen/pallas_call | solution.py:241
  93.1 2.6 %collective-permute-start.16 = (bf16[64,1408]{1,0:T(8,128)(2,1)S(1)}, bf16[64,1408]{1,0:T(8,128)(2,1)S(1)}, u32[]{:S(2)}, u32[]{:S(2)}) collective-permute-start(bf16[64,1408]{1,0:T(8,128)(2,1)S(1)} %get-tuple-element.28), channel_id=1, source_target_pairs={{0,96},{32,0},{64,32},{96,64},{1,97},{33,1},{65,33},{97,65},{2,98}... | collective-permute-start | bytes 540680 | tf_op jit(solution)/shard_map/ppermute | solution.py:356
  95.7 0.7 collective-permute-start.15
  96.5 1.3 collective-permute-start.14
  97.8 0.1 collective-permute-start.20
  97.9 0.5 collective-permute-start.21
  98.4 1.6 %collective-permute-done.16 = bf16[64,1408]{1,0:T(8,128)(2,1)S(1)} collective-permute-done((bf16[64,1408]{1,0:T(8,128)(2,1)S(1)}, bf16[64,1408]{1,0:T(8,128)(2,1)S(1)}, u32[]{:S(2)}, u32[]{:S(2)}) %collective-permute-start.16) | collective-permute-done | bytes 180256 | tf_op jit(solution)/shard_map/ppermute | solution.py:356
  100.0 2.7 %collective-permute-done.15 = bf16[64,1408]{1,0:T(8,128)(2,1)S(1)} collective-permute-done((bf16[64,1408]{1,0:T(8,128)(2,1)S(1)}, bf16[64,1408]{1,0:T(8,128)(2,1)S(1)}, u32[]{:S(2)}, u32[]{:S(2)}) %collective-permute-start.15) | collective-permute-done | bytes 180256 | tf_op jit(solution)/shard_map/ppermute | solution.py:356
  102.7 0.1 convert_add_fusion
  102.8 0.2 fusion.6
  103.0 0.1 broadcast_multiply_fusion
  103.3 0.1 fusion.2
  103.5 1.5 %collective-permute-start.17 = (bf16[64,720]{1,0:T(8,128)(2,1)S(1)}, bf16[64,720]{1,0:T(8,128)(2,1)S(1)}, u32[]{:S(2)}, u32[]{:S(2)}) collective-permute-start(bf16[64,720]{1,0:T(8,128)(2,1)S(1)} %pad_maximum_fusion.1.refs_0_), channel_id=1, source_target_pairs={{0,32},{32,64},{64,96},{96,0},{1,33},{33,65},{65,97},{97,1},{2,34}... | collective-permute-start | bytes 276488 | tf_op jit(solution)/shard_map/ppermute | solution.py:356
  105.0 3.2 %collective-permute-start.18 = (bf16[64,720]{1,0:T(8,128)(2,1)S(1)}, bf16[64,720]{1,0:T(8,128)(2,1)S(1)}, u32[]{:S(2)}, u32[]{:S(2)}) collective-permute-start(bf16[64,720]{1,0:T(8,128)(2,1)S(1)} %pad_maximum_fusion.1.refs_0_), channel_id=1, source_target_pairs={{0,64},{32,96},{64,0},{96,32},{1,65},{33,97},{65,1},{97,33},{2,66}... | collective-permute-start | bytes 276488 | tf_op jit(solution)/shard_map/ppermute | solution.py:356
  108.1 0.1 collective-permute-start.19
  108.2 0.4 collective-permute-done.17.refs_1_
  108.7 2.4 %collective-permute-done.18.refs_2_ = bf16[64,720]{1,0:T(8,128)(2,1)S(1)} collective-permute-done((bf16[64,720]{1,0:T(8,128)(2,1)S(1)}, bf16[64,720]{1,0:T(8,128)(2,1)S(1)}, u32[]{:S(2)}, u32[]{:S(2)}) %collective-permute-start.18) | collective-permute-done | bytes 92192 | tf_op jit(solution)/shard_map/ppermute | solution.py:356
  111.1 1.7 %collective-permute-done.19.refs_3_ = bf16[64,720]{1,0:T(8,128)(2,1)S(1)} collective-permute-done((bf16[64,720]{1,0:T(8,128)(2,1)S(1)}, bf16[64,720]{1,0:T(8,128)(2,1)S(1)}, u32[]{:S(2)}, u32[]{:S(2)}) %collective-permute-start.19) | collective-permute-done | bytes 92192 | tf_op jit(solution)/shard_map/ppermute | solution.py:356
  112.7 1.0 narrow.1
  113.8 2.1 %collective-permute-start.25 = (bf16[64,1280]{1,0:T(8,128)(2,1)S(1)}, bf16[64,1280]{1,0:T(8,128)(2,1)S(1)}, u32[]{:S(2)}, u32[]{:S(2)}) collective-permute-start(bf16[64,1280]{1,0:T(8,128)(2,1)S(1)} %get-tuple-element.33), channel_id=1, source_target_pairs={{0,1},{1,2},{2,3},{3,0},{4,5},{5,6},{6,7},{7,4},{8,9},{9,10},{10,1... | collective-permute-start | bytes 491528 | tf_op jit(solution)/shard_map/ppermute | solution.py:364
  115.8 2.2 %collective-permute-start.24 = (bf16[64,1280]{1,0:T(8,128)(2,1)S(1)}, bf16[64,1280]{1,0:T(8,128)(2,1)S(1)}, u32[]{:S(2)}, u32[]{:S(2)}) collective-permute-start(bf16[64,1280]{1,0:T(8,128)(2,1)S(1)} %get-tuple-element.32), channel_id=1, source_target_pairs={{0,2},{1,3},{2,0},{3,1},{4,6},{5,7},{6,4},{7,5},{8,10},{9,11},{10,... | collective-permute-start | bytes 491528 | tf_op jit(solution)/shard_map/ppermute | solution.py:364
  118.0 1.2 collective-permute-start.23
  119.2 1.2 collective-permute-done.25
  120.4 2.7 %collective-permute-done.24 = bf16[64,1280]{1,0:T(8,128)(2,1)S(1)} collective-permute-done((bf16[64,1280]{1,0:T(8,128)(2,1)S(1)}, bf16[64,1280]{1,0:T(8,128)(2,1)S(1)}, u32[]{:S(2)}, u32[]{:S(2)}) %collective-permute-start.24) | collective-permute-done | bytes 163872 | tf_op jit(solution)/shard_map/ppermute | solution.py:364
  123.0 0.3 collective-permute-done.23
  123.3 0.8 fusion
  124.1 3.4 %all-to-all-start.3 = ((bf16[8,8,1280]{2,1,0:T(8,128)(2,1)}), bf16[8,8,1280]{2,1,0:T(8,128)(2,1)S(1)}, u32[]{:S(2)}, u32[]{:S(2)}) async-start(bf16[8,8,1280]{2,1,0:T(8,128)(2,1)} %fusion), calls=%async_computation.3 | async-start | bytes 327680 | tf_op jit(solution)/shard_map/all_to_all | solution.py:350
  128.1 4.0 %final_state.1 = f32[1,32,128,128]{3,2,1,0:T(8,128)} custom-call(s32[1]{0:T(128)S(6)} %copy.24.accepted_ref, bf16[1,4,4096]{2,1,0:T(4,128)(2,1)S(1)} %copy-done.4, bf16[1,4,128]{2,1,0:T(4,128)(2,1)S(1)} %copy-done.7, f32[1,4,32]{2,1,0:T(4,128)S(1)} %copy-done.6, f32[1,32]{1,0:T(1,128)S(1)} %bitcast.24, f32[1,32,128,128]{3,2,1,0:T(8,128)S(1)} %copy-done, ...), custom_call_target="tpu_custom_call" | custom-call | tf_op jit(solution)/shard_map/final_state/pallas_call | solution.py:330
  132.2 4.6 %all-to-all-done.3 = bf16[8,8,1280]{2,1,0:T(8,128)(2,1)S(1)} async-done(((bf16[8,8,1280]{2,1,0:T(8,128)(2,1)}), bf16[8,8,1280]{2,1,0:T(8,128)(2,1)S(1)}, u32[]{:S(2)}, u32[]{:S(2)}) %all-to-all-start.3) | async-done | bytes 163872 | tf_op jit(solution)/shard_map/all_to_all | solution.py:350
  136.8 0.6 add_convert_fusion.1
  (57 shorter events, 1.0 us)
Async XLA Ops:
  1.3 17.9 %copy-start.10 = (s32[128]{0:T(128)S(1)}, s32[128]{0:T(128)}, u32[]{:S(2)}) copy-start(s32[128]{0:T(128)} %param.37) | copy-start | bytes 1540
  7.6 30.3 %copy-start.3 = (bf16[192,1280]{1,0:T(8,128)(2,1)S(1)}, bf16[192,1280]{1,0:T(8,128)(2,1)}, u32[]{:S(2)}) copy-start(bf16[192,1280]{1,0:T(8,128)(2,1)} %refs_1_.6) | copy-start | bytes 1474564
  7.6 21.6 %all-to-all-start = ((bf16[32,4,192]{2,1,0:T(4,128)(2,1)}), bf16[32,4,192]{2,1,0:T(4,128)(2,1)S(1)}, u32[]{:S(2)}, u32[]{:S(2)}) async-start(bf16[32,4,192]{2,1,0:T(4,128)(2,1)} %mixer.1), calls=%async_computation | async-start | bytes 131072 | tf_op jit(solution)/shard_map/all_to_all | solution.py:350
  29.2 4.8 %collective-permute-start.2 = (bf16[32,4,192]{2,1,0:T(4,128)(2,1)S(1)}, bf16[32,4,192]{2,1,0:T(4,128)(2,1)S(1)}, u32[]{:S(2)}, u32[]{:S(2)}) collective-permute-start(bf16[32,4,192]{2,1,0:T(4,128)(2,1)S(1)} %all-to-all-done), channel_id=1, source_target_pairs={{0,96},{32,0},{64,32},{96,64},{1,97},{33,1},{65,33},{97,65},{2,98}... | collective-permute-start | bytes 147464 | tf_op jit(solution)/shard_map/ppermute | solution.py:356
  29.7 5.8 %collective-permute-start.1 = (bf16[32,4,192]{2,1,0:T(4,128)(2,1)S(1)}, bf16[32,4,192]{2,1,0:T(4,128)(2,1)S(1)}, u32[]{:S(2)}, u32[]{:S(2)}) collective-permute-start(bf16[32,4,192]{2,1,0:T(4,128)(2,1)S(1)} %all-to-all-done), channel_id=1, source_target_pairs={{0,64},{32,96},{64,0},{96,32},{1,65},{33,97},{65,1},{97,33},{2,66}... | collective-permute-start | bytes 147464 | tf_op jit(solution)/shard_map/ppermute | solution.py:356
  32.1 4.3 %collective-permute-start = (bf16[32,4,192]{2,1,0:T(4,128)(2,1)S(1)}, bf16[32,4,192]{2,1,0:T(4,128)(2,1)S(1)}, u32[]{:S(2)}, u32[]{:S(2)}) collective-permute-start(bf16[32,4,192]{2,1,0:T(4,128)(2,1)S(1)} %all-to-all-done), channel_id=1, source_target_pairs={{0,32},{32,64},{64,96},{96,0},{1,33},{33,65},{65,97},{97,1},{2,34}... | collective-permute-start | bytes 147464 | tf_op jit(solution)/shard_map/ppermute | solution.py:356
  37.9 8.5 %copy-start.1 = (bf16[1280,2,336]{0,2,1:T(8,128)(2,1)S(1)}, bf16[1280,2,336]{0,2,1:T(8,128)(2,1)}, u32[]{:S(2)}) copy-start(bf16[1280,2,336]{0,2,1:T(8,128)(2,1)} %param.40) | copy-start | bytes 5160964
  38.9 2.3 %collective-permute-start.3 = (bf16[128,1280]{1,0:T(8,128)(2,1)}, bf16[128,1280]{1,0:T(8,128)(2,1)S(1)}, u32[]{:S(2)}, u32[]{:S(2)}) collective-permute-start(bf16[128,1280]{1,0:T(8,128)(2,1)} %get-tuple-element.18), channel_id=1, source_target_pairs={{0,128},{128,0},{1,129},{129,1},{2,130},{130,2},{3,131},{131,3},{4... | collective-permute-start | bytes 983048 | tf_op jit(solution)/shard_map/ppermute | solution.py:430
  38.9 2.3 %collective-permute-start.4 = (bf16[128,1280]{1,0:T(8,128)(2,1)S(1)}, bf16[128,1280]{1,0:T(8,128)(2,1)S(1)}, u32[]{:S(2)}, u32[]{:S(2)}) collective-permute-start(bf16[128,1280]{1,0:T(8,128)(2,1)S(1)} %get-tuple-element.19), channel_id=1, source_target_pairs={{0,128},{128,0},{1,129},{129,1},{2,130},{130,2},{3,131},{131,3},{4... | collective-permute-start | bytes 983048 | tf_op jit(solution)/shard_map/ppermute | solution.py:430
  42.4 5.9 %copy-start.9 = (f32[1280]{0:T(1024)S(1)}, f32[1280]{0:T(1024)}, u32[]{:S(2)}) copy-start(f32[1280]{0:T(1024)} %param.39) | copy-start | bytes 15364
  42.4 24.8 %copy-start.5 = (bf16[8,1280]{1,0:T(8,128)(2,1)S(1)}, bf16[8,1280]{1,0:T(8,128)(2,1)}, u32[]{:S(2)}) copy-start(bf16[8,1280]{1,0:T(8,128)(2,1)} %refs_1_.7) | copy-start | bytes 61444
  42.4 24.8 %all-to-all-start.1 = ((bf16[32,8,1280]{2,1,0:T(8,128)(2,1)}), bf16[32,8,1280]{2,1,0:T(8,128)(2,1)S(1)}, u32[]{:S(2)}, u32[]{:S(2)}) async-start(bf16[32,8,1280]{2,1,0:T(8,128)(2,1)} %bitcast.4), calls=%async_computation.1 | async-start | bytes 1310720 | tf_op jit(solution)/shard_map/all_to_all | solution.py:350
  47.6 25.4 %collective-permute-start.8 = (bf16[128,1280]{1,0:T(8,128)(2,1)}, bf16[128,1280]{1,0:T(8,128)(2,1)S(1)}, u32[]{:S(2)}, u32[]{:S(2)}) collective-permute-start(bf16[128,1280]{1,0:T(8,128)(2,1)} %get-tuple-element.38), channel_id=1, source_target_pairs={{0,128},{128,0},{1,129},{129,1},{2,130},{130,2},{3,131},{131,3},{4... | collective-permute-start | bytes 983048 | tf_op jit(solution)/shard_map/ppermute | solution.py:380
  47.8 34.1 %collective-permute-start.9 = (bf16[128,1280]{1,0:T(8,128)(2,1)}, bf16[128,1280]{1,0:T(8,128)(2,1)}, u32[]{:S(2)}, u32[]{:S(2)}) collective-permute-start(bf16[128,1280]{1,0:T(8,128)(2,1)} %get-tuple-element.37), channel_id=1, source_target_pairs={{0,128},{128,0},{1,129},{129,1},{2,130},{130,2},{3,131},{131,3},{4... | collective-permute-start | bytes 983048 | tf_op jit(solution)/shard_map/ppermute | solution.py:380
  48.1 36.4 %collective-permute-start.10 = (bf16[128,1280]{1,0:T(8,128)(2,1)}, bf16[128,1280]{1,0:T(8,128)(2,1)}, u32[]{:S(2)}, u32[]{:S(2)}) collective-permute-start(bf16[128,1280]{1,0:T(8,128)(2,1)} %get-tuple-element.36), channel_id=1, source_target_pairs={{0,128},{128,0},{1,129},{129,1},{2,130},{130,2},{3,131},{131,3},{4... | collective-permute-start | bytes 983048 | tf_op jit(solution)/shard_map/ppermute | solution.py:380
  68.0 13.0 %all-to-all-start.2 = ((bf16[8,8,1280]{2,1,0:T(8,128)(2,1)}), bf16[8,8,1280]{2,1,0:T(8,128)(2,1)S(1)}, u32[]{:S(2)}, u32[]{:S(2)}) async-start(bf16[8,8,1280]{2,1,0:T(8,128)(2,1)} %get-tuple-element.23), calls=%async_computation.2 | async-start | bytes 327680 | tf_op jit(solution)/shard_map/all_to_all | solution.py:350
  71.5 26.2 %copy-start.2 = (bf16[336,1280]{1,0:T(8,128)(2,1)S(1)}, bf16[336,1280]{1,0:T(8,128)(2,1)}, u32[]{:S(2)}) copy-start(bf16[336,1280]{1,0:T(8,128)(2,1)} %refs_7_.2) | copy-start | bytes 2580484
  71.5 1.4 collective-permute-start.13
  71.6 14.5 %collective-permute-start.11 = (bf16[128,1280]{1,0:T(8,128)(2,1)}, bf16[128,1280]{1,0:T(8,128)(2,1)}, u32[]{:S(2)}, u32[]{:S(2)}) collective-permute-start(bf16[128,1280]{1,0:T(8,128)(2,1)} %get-tuple-element.35), channel_id=1, source_target_pairs={{0,128},{128,0},{1,129},{129,1},{2,130},{130,2},{3,131},{131,3},{4... | collective-permute-start | bytes 983048 | tf_op jit(solution)/shard_map/ppermute | solution.py:380
  72.9 13.2 %collective-permute-start.12 = (bf16[128,1280]{1,0:T(8,128)(2,1)}, bf16[128,1280]{1,0:T(8,128)(2,1)}, u32[]{:S(2)}, u32[]{:S(2)}) collective-permute-start(bf16[128,1280]{1,0:T(8,128)(2,1)} %get-tuple-element.34), channel_id=1, source_target_pairs={{0,128},{128,0},{1,129},{129,1},{2,130},{130,2},{3,131},{131,3},{4... | collective-permute-start | bytes 983048 | tf_op jit(solution)/shard_map/ppermute | solution.py:380
  80.9 7.3 %collective-permute-start.5 = (bf16[8,8,1280]{2,1,0:T(8,128)(2,1)S(1)}, bf16[8,8,1280]{2,1,0:T(8,128)(2,1)S(1)}, u32[]{:S(2)}, u32[]{:S(2)}) collective-permute-start(bf16[8,8,1280]{2,1,0:T(8,128)(2,1)S(1)} %all-to-all-done.2), channel_id=1, source_target_pairs={{0,1},{1,2},{2,3},{3,0},{4,5},{5,6},{6,7},{7,4},{8,9},{9,10},{10,1... | collective-permute-start | bytes 491528 | tf_op jit(solution)/shard_map/ppermute | solution.py:364
  81.9 8.1 %collective-permute-start.6 = (bf16[8,8,1280]{2,1,0:T(8,128)(2,1)S(1)}, bf16[8,8,1280]{2,1,0:T(8,128)(2,1)S(1)}, u32[]{:S(2)}, u32[]{:S(2)}) collective-permute-start(bf16[8,8,1280]{2,1,0:T(8,128)(2,1)S(1)} %all-to-all-done.2), channel_id=1, source_target_pairs={{0,2},{1,3},{2,0},{3,1},{4,6},{5,7},{6,4},{7,5},{8,10},{9,11},{10,... | collective-permute-start | bytes 491528 | tf_op jit(solution)/shard_map/ppermute | solution.py:364
  84.6 5.5 %collective-permute-start.7 = (bf16[8,8,1280]{2,1,0:T(8,128)(2,1)S(1)}, bf16[8,8,1280]{2,1,0:T(8,128)(2,1)S(1)}, u32[]{:S(2)}, u32[]{:S(2)}) collective-permute-start(bf16[8,8,1280]{2,1,0:T(8,128)(2,1)S(1)} %all-to-all-done.2), channel_id=1, source_target_pairs={{0,3},{1,0},{2,1},{3,2},{4,7},{5,4},{6,5},{7,6},{8,11},{9,8},{10,9... | collective-permute-start | bytes 491528 | tf_op jit(solution)/shard_map/ppermute | solution.py:364
  93.1 6.9 %collective-permute-start.16 = (bf16[64,1408]{1,0:T(8,128)(2,1)S(1)}, bf16[64,1408]{1,0:T(8,128)(2,1)S(1)}, u32[]{:S(2)}, u32[]{:S(2)}) collective-permute-start(bf16[64,1408]{1,0:T(8,128)(2,1)S(1)} %get-tuple-element.28), channel_id=1, source_target_pairs={{0,96},{32,0},{64,32},{96,64},{1,97},{33,1},{65,33},{97,65},{2,98}... | collective-permute-start | bytes 540680 | tf_op jit(solution)/shard_map/ppermute | solution.py:356
  95.7 7.0 %collective-permute-start.15 = (bf16[64,1408]{1,0:T(8,128)(2,1)S(1)}, bf16[64,1408]{1,0:T(8,128)(2,1)S(1)}, u32[]{:S(2)}, u32[]{:S(2)}) collective-permute-start(bf16[64,1408]{1,0:T(8,128)(2,1)S(1)} %get-tuple-element.27), channel_id=1, source_target_pairs={{0,64},{32,96},{64,0},{96,32},{1,65},{33,97},{65,1},{97,33},{2,66}... | collective-permute-start | bytes 540680 | tf_op jit(solution)/shard_map/ppermute | solution.py:356
  96.5 6.3 %collective-permute-start.14 = (bf16[64,1408]{1,0:T(8,128)(2,1)S(1)}, bf16[64,1408]{1,0:T(8,128)(2,1)S(1)}, u32[]{:S(2)}, u32[]{:S(2)}) collective-permute-start(bf16[64,1408]{1,0:T(8,128)(2,1)S(1)} %get-tuple-element.26), channel_id=1, source_target_pairs={{0,32},{32,64},{64,96},{96,0},{1,33},{33,65},{65,97},{97,1},{2,34}... | collective-permute-start | bytes 540680 | tf_op jit(solution)/shard_map/ppermute | solution.py:356
  97.8 10.4 %collective-permute-start.20 = (bf16[128,1280]{1,0:T(8,128)(2,1)S(1)}, bf16[128,1280]{1,0:T(8,128)(2,1)S(1)}, u32[]{:S(2)}, u32[]{:S(2)}) collective-permute-start(bf16[128,1280]{1,0:T(8,128)(2,1)S(1)} %get-tuple-element.40), channel_id=1, source_target_pairs={{0,128},{128,0},{1,129},{129,1},{2,130},{130,2},{3,131},{131,3},{4... | collective-permute-start | bytes 983048 | tf_op jit(solution)/shard_map/ppermute | solution.py:380
  97.9 10.3 %collective-permute-start.21 = (bf16[128,1280]{1,0:T(8,128)(2,1)S(1)}, bf16[128,1280]{1,0:T(8,128)(2,1)S(1)}, u32[]{:S(2)}, u32[]{:S(2)}) collective-permute-start(bf16[128,1280]{1,0:T(8,128)(2,1)S(1)} %get-tuple-element.39), channel_id=1, source_target_pairs={{0,128},{128,0},{1,129},{129,1},{2,130},{130,2},{3,131},{131,3},{4... | collective-permute-start | bytes 983048 | tf_op jit(solution)/shard_map/ppermute | solution.py:380
  100.0 8.1 %collective-permute-start.22 = (bf16[80,1280]{1,0:T(8,128)(2,1)S(1)}, bf16[80,1280]{1,0:T(8,128)(2,1)S(1)}, u32[]{:S(2)}, u32[]{:S(2)}) collective-permute-start(bf16[80,1280]{1,0:T(8,128)(2,1)S(1)} %slice.73), channel_id=1, source_target_pairs={{0,128},{128,0},{1,129},{129,1},{2,130},{130,2},{3,131},{131,3},{4... | collective-permute-start | bytes 614408 | tf_op jit(solution)/shard_map/ppermute | solution.py:380
  103.2 24.9 %copy-start = (f32[1,32,128,128]{3,2,1,0:T(8,128)S(1)}, f32[1,32,128,128]{3,2,1,0:T(8,128)}, u32[]{:S(2)}) copy-start(f32[1,32,128,128]{3,2,1,0:T(8,128)} %state_ref.1) | copy-start | bytes 6291460
  103.2 24.9 %copy-start.4 = (bf16[1,4,4096]{2,1,0:T(4,128)(2,1)S(1)}, bf16[1,4,4096]{2,1,0:T(4,128)(2,1)}, u32[]{:S(2)}) copy-start(bf16[1,4,4096]{2,1,0:T(4,128)(2,1)} %x_ref.1) | copy-start | bytes 98308
  103.2 24.9 %copy-start.6 = (f32[1,4,32]{2,1,0:T(4,128)S(1)}, f32[1,4,32]{2,1,0:T(4,128)}, u32[]{:S(2)}) copy-start(f32[1,4,32]{2,1,0:T(4,128)} %dt_ref.1) | copy-start | bytes 1540
  103.2 24.9 %copy-start.7 = (bf16[1,4,128]{2,1,0:T(4,128)(2,1)S(1)}, bf16[1,4,128]{2,1,0:T(4,128)(2,1)}, u32[]{:S(2)}) copy-start(bf16[1,4,128]{2,1,0:T(4,128)(2,1)} %in_map_ref.1) | copy-start | bytes 3076
  103.2 24.9 %copy-start.8 = (f32[32]{0:T(128)S(1)}, f32[32]{0:T(128)}, u32[]{:S(2)}) copy-start(f32[32]{0:T(128)} %param.33) | copy-start | bytes 388
  103.5 5.2 %collective-permute-start.17 = (bf16[64,720]{1,0:T(8,128)(2,1)S(1)}, bf16[64,720]{1,0:T(8,128)(2,1)S(1)}, u32[]{:S(2)}, u32[]{:S(2)}) collective-permute-start(bf16[64,720]{1,0:T(8,128)(2,1)S(1)} %pad_maximum_fusion.1.refs_0_), channel_id=1, source_target_pairs={{0,32},{32,64},{64,96},{96,0},{1,33},{33,65},{65,97},{97,1},{2,34}... | collective-permute-start | bytes 276488 | tf_op jit(solution)/shard_map/ppermute | solution.py:356
  105.0 6.1 %collective-permute-start.18 = (bf16[64,720]{1,0:T(8,128)(2,1)S(1)}, bf16[64,720]{1,0:T(8,128)(2,1)S(1)}, u32[]{:S(2)}, u32[]{:S(2)}) collective-permute-start(bf16[64,720]{1,0:T(8,128)(2,1)S(1)} %pad_maximum_fusion.1.refs_0_), channel_id=1, source_target_pairs={{0,64},{32,96},{64,0},{96,32},{1,65},{33,97},{65,1},{97,33},{2,66}... | collective-permute-start | bytes 276488 | tf_op jit(solution)/shard_map/ppermute | solution.py:356
  108.1 4.6 %collective-permute-start.19 = (bf16[64,720]{1,0:T(8,128)(2,1)S(1)}, bf16[64,720]{1,0:T(8,128)(2,1)S(1)}, u32[]{:S(2)}, u32[]{:S(2)}) collective-permute-start(bf16[64,720]{1,0:T(8,128)(2,1)S(1)} %pad_maximum_fusion.1.refs_0_), channel_id=1, source_target_pairs={{0,96},{32,0},{64,32},{96,64},{1,97},{33,1},{65,33},{97,65},{2,98}... | collective-permute-start | bytes 276488 | tf_op jit(solution)/shard_map/ppermute | solution.py:356
  113.8 6.6 %collective-permute-start.25 = (bf16[64,1280]{1,0:T(8,128)(2,1)S(1)}, bf16[64,1280]{1,0:T(8,128)(2,1)S(1)}, u32[]{:S(2)}, u32[]{:S(2)}) collective-permute-start(bf16[64,1280]{1,0:T(8,128)(2,1)S(1)} %get-tuple-element.33), channel_id=1, source_target_pairs={{0,1},{1,2},{2,3},{3,0},{4,5},{5,6},{6,7},{7,4},{8,9},{9,10},{10,1... | collective-permute-start | bytes 491528 | tf_op jit(solution)/shard_map/ppermute | solution.py:364
  115.8 7.2 %collective-permute-start.24 = (bf16[64,1280]{1,0:T(8,128)(2,1)S(1)}, bf16[64,1280]{1,0:T(8,128)(2,1)S(1)}, u32[]{:S(2)}, u32[]{:S(2)}) collective-permute-start(bf16[64,1280]{1,0:T(8,128)(2,1)S(1)} %get-tuple-element.32), channel_id=1, source_target_pairs={{0,2},{1,3},{2,0},{3,1},{4,6},{5,7},{6,4},{7,5},{8,10},{9,11},{10,... | collective-permute-start | bytes 491528 | tf_op jit(solution)/shard_map/ppermute | solution.py:364
  118.0 5.3 %collective-permute-start.23 = (bf16[64,1280]{1,0:T(8,128)(2,1)S(1)}, bf16[64,1280]{1,0:T(8,128)(2,1)S(1)}, u32[]{:S(2)}, u32[]{:S(2)}) collective-permute-start(bf16[64,1280]{1,0:T(8,128)(2,1)S(1)} %get-tuple-element.31), channel_id=1, source_target_pairs={{0,3},{1,0},{2,1},{3,2},{4,7},{5,4},{6,5},{7,6},{8,11},{9,8},{10,9... | collective-permute-start | bytes 491528 | tf_op jit(solution)/shard_map/ppermute | solution.py:364
  124.1 12.7 %all-to-all-start.3 = ((bf16[8,8,1280]{2,1,0:T(8,128)(2,1)}), bf16[8,8,1280]{2,1,0:T(8,128)(2,1)S(1)}, u32[]{:S(2)}, u32[]{:S(2)}) async-start(bf16[8,8,1280]{2,1,0:T(8,128)(2,1)} %fusion), calls=%async_computation.3 | async-start | bytes 327680 | tf_op jit(solution)/shard_map/all_to_all | solution.py:350

commit v3 on v2

--- a/solution.py
+++ b/solution.py
@@ -36,17 +36,14 @@
         refs[26:],
     )
     copies = fetch(list(zip(small, buffers)), sems)
-    kv_heads, _, head_size = keys_ref.shape
-    heads = state_ref.shape[0] // kv_heads
-    big = []
-    for j in range(kv_heads):
-        cols = pl.ds(j * head_size, head_size)
-        big += [
-            (state_hbm.at[0, pl.ds(j * heads, heads)], state_ref.at[pl.ds(j * heads, heads)]),
-            (keys_hbm.at[0, :, cols], keys_ref.at[j]),
-            (values_hbm.at[0, :, cols], values_ref.at[j]),
-        ]
-    big = fetch(big, big_sems)
+    state_copy, key_copy, value_copy = [
+        pltpu.make_async_copy(source.at[0], buffer, big_sems.at[i])
+        for i, (source, buffer) in enumerate(
+            [(state_hbm, state_ref), (keys_hbm, keys_ref), (values_hbm, values_ref)]
+        )
+    ]
+    state_copy.start()
+    key_copy.start()
     for copy in copies:
         copy.wait()
     (
@@ -54,6 +51,9 @@
         in_map_ref, out_map_ref, dt_ref, rate_ref, skip_ref,
     ) = buffers
     drafts = query_ref.shape[1]
+    head_size = HD
+    kv_heads = keys_ref.shape[1] // head_size
+    heads = state_ref.shape[0] // kv_heads
     groups = query_ref.shape[2] // (kv_heads * head_size)
     attended = query_ref.shape[2]
 
@@ -75,9 +75,9 @@
         mixing.append(share + jnp.where(row == s, skip_ref[...], 0.0))
     out_maps = jnp.concatenate([out_map, out_map], axis=1)
 
+    state_copy.wait()
+    value_copy.start()
     for j in range(kv_heads):
-        for copy in big[3 * j : 3 * j + 3]:
-            copy.wait()
         state = state_ref[j * heads : (j + 1) * heads].reshape(heads * PH, state_ref.shape[2])
         high = state.astype(bf16)
         low = (state - high.astype(f32)).astype(bf16)
@@ -95,13 +95,16 @@
             cols = slice(attended + h * PH, attended + (h + 1) * PH)
             mixed_ref[:, cols] = y * gate * jax.nn.sigmoid(gate)
 
+    key_copy.wait()
+    held = []
+    for j in range(kv_heads):
         first = j * groups * head_size
         query = query_ref[0, :, first : first + groups * head_size].astype(f32)
         queries = jnp.concatenate(
             [query[:, g * head_size : (g + 1) * head_size] for g in range(groups)], axis=0
         )
         scores = lax.dot_general(
-            queries.astype(bf16), keys_ref[j], nt, preferred_element_type=f32
+            queries.astype(bf16), keys_ref[:, j * head_size : (j + 1) * head_size], nt, preferred_element_type=f32
         ) * head_size ** (-0.5)
         position = lax.broadcasted_iota(jnp.int32, scores.shape, 1)
         scores = jnp.where(position < length_ref[...], scores, -jnp.inf)
@@ -117,23 +120,33 @@
             peak = jnp.maximum(peak, score)
         weights = jnp.exp(scores - peak)
         total = jnp.sum(weights, axis=1, keepdims=True)
-        summed = jnp.dot(weights.astype(bf16), values_ref[j], preferred_element_type=f32)
+        held.append((weights.astype(bf16), total, [jnp.exp(s - peak) for s in scores_new]))
+
+    value_copy.wait()
+    for j in range(kv_heads):
+        first = j * groups * head_size
+        new_cols = slice(j * head_size, (j + 1) * head_size)
+        weights, total, weights_new = held[j]
+        summed = jnp.dot(weights, values_ref[:, new_cols], preferred_element_type=f32)
         values_new = value_new_ref[0, :, new_cols].astype(f32)
         for u in range(drafts):
-            weight = jnp.exp(scores_new[u] - peak)
+            weight = weights_new[u]
             total = total + weight
             summed = summed + weight.astype(bf16).astype(f32) * values_new[u : u + 1, :]
         result = summed / total
         for g in range(groups):
             cols = slice(first + g * head_size, first + (g + 1) * head_size)
             mixed_ref[:, cols] = result[g * drafts : (g + 1) * drafts]
-    width = pieces_ref.shape[2]
-    for c in range(pieces_ref.shape[0]):
-        pieces_ref[c] = mixed_ref[:, c * width : (c + 1) * width].astype(bf16)
+    width = pieces_ref.shape[3]
+    cols = pieces_ref.shape[1]
+    for c in range(cols):
+        piece = mixed_ref[:, c * width : (c + 1) * width].astype(bf16)
+        for r in range(pieces_ref.shape[0]):
+            pieces_ref[r, c] = piece
 
 
 def mix(
-    cols, query, key_new, value_new, key_cache, value_cache, ctx_len,
+    rows, cols, query, key_new, value_new, key_cache, value_cache, ctx_len,
     ssm_x, ssm_gate, ssm_b, ssm_c, ssm_dt, decay_rate, skip_gain, ssm_state,
 ):
     kv_heads = key_new.shape[2] // HD
@@ -144,12 +157,14 @@
         decay_rate.reshape(1, -1), skip_gain.reshape(1, -1),
     )
     big = (key_cache, value_cache, ssm_state)
-    cached = (kv_heads, key_cache.shape[1], HD)
+    cached = key_cache.shape[1:]
     return pl.pallas_call(
         mixer_kernel,
         in_specs=[pl.BlockSpec(memory_space=pltpu.HBM)] * (len(small) + len(big)),
         out_specs=pl.BlockSpec(memory_space=pltpu.VMEM),
-        out_shape=jax.ShapeDtypeStruct((cols, query.shape[1], features // cols), jnp.bfloat16),
+        out_shape=jax.ShapeDtypeStruct(
+            (rows, cols, query.shape[1], features // cols), jnp.bfloat16
+        ),
         scratch_shapes=[pltpu.VMEM(array.shape, array.dtype) for array in small]
         + [
             pltpu.VMEM(cached, key_cache.dtype),
@@ -157,27 +172,22 @@
             pltpu.VMEM(ssm_state.shape[1:], ssm_state.dtype),
             pltpu.VMEM((query.shape[1], features), jnp.float32),
             pltpu.SemaphoreType.DMA((len(small),)),
-            pltpu.SemaphoreType.DMA((3 * kv_heads,)),
+            pltpu.SemaphoreType.DMA((3,)),
         ],
         compiler_params=pltpu.CompilerParams(vmem_limit_bytes=62 * 2**20),
         name="mixer",
     )(*small, *big)
 
 
-def project_kernel(rows_ref, weights_ref, *out_refs):
+def project_kernel(rows_ref, weights_ref, out_ref):
+    out_ref[...] = jnp.dot(
+        rows_ref[...], weights_ref[...], preferred_element_type=jnp.float32
+    ).astype(out_ref.dtype)
+
+
+def merge_kernel(rows_ref, weights_ref, part_ref, out_ref):
     product = jnp.dot(rows_ref[...], weights_ref[...], preferred_element_type=jnp.float32)
-    share = out_refs[0].shape[0]
-    for i, out_ref in enumerate(out_refs):
-        out_ref[...] = product[i * share : (i + 1) * share].astype(out_ref.dtype)
-
-
-def merge_kernel(rows_ref, weights_ref, *refs):
-    parts, out_ref = refs[:-1], refs[-1]
-    product = jnp.dot(rows_ref[...], weights_ref[...], preferred_element_type=jnp.float32)
-    share = parts[0].shape[0]
-    for i, part in enumerate(parts):
-        rows = slice(i * share, (i + 1) * share)
-        out_ref[rows] = (product[rows] + part[...].astype(jnp.float32)).astype(out_ref.dtype)
+    out_ref[...] = (product + part_ref[...].astype(jnp.float32)).astype(out_ref.dtype)
 
 
 def on_core(kernel, operands, out_shape, name, after=()):
@@ -374,12 +384,8 @@
     ]
 
 
-def from_partner(weights, cut):
-    swap = [(0, 1), (1, 0)]
-    return [
-        lax.ppermute(weights[first : first + cut], "grp", swap)
-        for first in range(0, weights.shape[0], cut)
-    ]
+def from_partner(weights):
+    return lax.ppermute(weights, "grp", [(0, 1), (1, 0)])
 
 
 def shards(
@@ -413,37 +419,28 @@
     inner = 4
     lines = [[o * inner + i for o in range(cols // inner)] for i in range(inner)]
     pieces = mix(
-        cols, query, key_new, value_new, key_cache, value_cache, ctx_len,
+        rows, cols, query, key_new, value_new, key_cache, value_cache, ctx_len,
         ssm_x, ssm_gate, ssm_b, ssm_c, ssm_dt, decay_rate, skip_gain, ssm_state,
     )
-    width = pieces.shape[2]
-    mine = exchange(pieces, "col")
-    by_slot = jnp.concatenate(shifted([mine] * rows, "row"), axis=0)
-    behind = (lax.axis_index("row") - slot_of // cols) % rows
-    place = (behind * cols + slot_of % cols).reshape(2, -1)
-    other = lax.axis_index("grp") ^ 1
-    place = jnp.where(other == 0, place, place[::-1]).reshape(-1)
-    mixed_req = jnp.take(by_slot, place, axis=0).reshape(2, -1, width)
-    swap = [(0, 1), (1, 0)]
-    sent = jax.ShapeDtypeStruct((mixed_req.shape[1] // 2, w_out.shape[1]), bf16)
-    for_other = on_core(project_kernel, (mixed_req[0], w_out), [sent] * 2, "project")
-    from_other = [lax.ppermute(part, "grp", swap) for part in for_other]
-    held = jax.ShapeDtypeStruct((mixed_req.shape[1], w_out.shape[1]), bf16)
-    half = on_core(merge_kernel, (mixed_req[1], w_out, *from_other), held, "merge")
+    width = pieces.shape[3]
+    by_slot = exchange(pieces.reshape((rows * cols,) + pieces.shape[2:]), ("row", "col"))
+    place = slot_of.reshape(2, -1)
+    place = jnp.where(lax.axis_index("grp") == 1, place, place[::-1])
+    for_other = jnp.take(by_slot, place[0], axis=0).reshape(-1, width)
+    own = jnp.take(by_slot, place[1], axis=0).reshape(-1, width)
+    held = jax.ShapeDtypeStruct((own.shape[0], w_out.shape[1]), bf16)
+    for_other = on_core(project_kernel, (for_other, w_out), held, "project")
+    half = on_core(merge_kernel, (own, w_out, from_partner(for_other)), held, "merge")
     half, gate_up, w_down, gain = lax.optimization_barrier((half, gate_up, w_down, norm_gain))
     state_next = final_state(ssm_x, ssm_b, ssm_dt, decay_rate, ssm_state, accepted, half)
     half = exchange(half.reshape(cols, -1, half.shape[1]), "col")
     units = gate_up.shape[2]
     in_weights = jnp.transpose(gate_up, (1, 2, 0)).reshape(2 * units, -1)
-    in_pieces = from_partner(in_weights, 128)
-    whole = 2 * units // 128
-    in_places = [128 * i for i in range(whole)] + [128 * whole + 2 * units, 128 * whole]
-    if 2 * units % 128 == 0:
-        in_places = in_places[:-2] + in_places[-1:]
-    in_pieces = in_pieces + [in_weights]
-    down_pieces = from_partner(w_down, 128) + [w_down]
+    in_pieces = [from_partner(in_weights), in_weights]
+    in_places = [0, 2 * units]
+    down_pieces = [from_partner(w_down), w_down]
     padded = -(-units // 128) * 128
-    down_places = list(range(0, units, 128)) + [padded]
+    down_places = [0, padded]
     gain = gain.reshape(1, -1)
     stream, spread = on_core(
         arrive_kernel,
@@ -453,6 +450,7 @@
             jax.ShapeDtypeStruct((cols // inner,) + resid.shape, bf16),
         ],
         "arrive",
+        [piece[:16, :128] for piece in in_pieces[:-1] + down_pieces[:-1]],
     )
     spread = exchange(spread, "col", lines)
     tokens = [
@@ -462,14 +460,8 @@
     summed = functools.reduce(jnp.add, [part.astype(f32) for part in sums])
     mean_sq = (summed[:, 4 * units] + summed[:, 4 * units + 1]) / D
     summed = summed * lax.rsqrt(mean_sq[:, None] + norm_eps)
-    first = 128 * whole
-    gate = [summed[:, :units], summed[:, first : first + units]]
-    up = [
-        jnp.concatenate(
-            [summed[:, units:first], summed[:, first + 2 * units : 4 * units]], axis=1
-        ),
-        summed[:, first + units : first + 2 * units],
-    ]
+    gate = [summed[:, :units], summed[:, 2 * units : 3 * units]]
+    up = [summed[:, units : 2 * units], summed[:, 3 * units : 4 * units]]
     hidden = [(jax.nn.silu(g) * u).astype(bf16) for g, u in zip(gate, up)]
     blank = jnp.zeros((hidden[0].shape[0], padded - units), bf16)
     hidden = jnp.concatenate([hidden[0], blank, hidden[1]], axis=1)

time: 139 us -> 135 us (0.971)
  blocking collectives: 0 us -> 12.6 us
  starting transfers between devices: 49.7 us -> 41 us
  Pallas kernels: 17.3 us -> 12.7 us
  waiting for transfers between devices: 62.9 us -> 60.3 us
    all_to_all x0 -> x1, blocking collectives: none -> 12.6 us  [exchange(): lax.all_to_all(blocks, axis, 0, 0, tiled=True, axis_index_groups=groups)]
    ppermute x9 -> x6, starting transfers between devices: 14.1 us -> 8.74 us  [shifted(): lax.ppermute(blocks[shift], axis, [(k, (k + shift) % size) for k in range...]
    all_to_all x4 -> x3, waiting for transfers between devices: 41.1 us -> 36.2 us  [exchange(): lax.all_to_all(blocks, axis, 0, 0, tiled=True, axis_index_groups=groups)]
    ppermute x11 -> x3, starting transfers between devices: 2.49 us -> 0.4 us  [from_partner(): return lax.ppermute(weights, 'grp', [(0, 1), (1, 0)])]
    ppermute x6, waiting for transfers between devices: 8.06 us -> 9.97 us  [around(): lax.ppermute(blocks[shift], 'col', [(o * size + i, o * size + (i + sign *...]
    ppermute x6, starting transfers between devices: 10.5 us -> 8.71 us  [around(): lax.ppermute(blocks[shift], 'col', [(o * size + i, o * size + (i + sign *...]
    pallas_call x1, Pallas kernels: 3.01 us -> 1.33 us  [widen(): pl.pallas_call(functools.partial(widen_kernel, rows, places), in_specs=[v...]
    slice x7 -> x2, local copies, waits for them, and re-layouts: 1.52 us -> 0.01 us  [shards(): piece[:16, :128]]
  transfers between devices with their start and end apart: 30 -> 18, of which waited for: 19 -> 16; matrix products, arithmetic and copies ran while one was open for 2% -> 1% of each run, Pallas kernels for 3% -> 3%
where the time goes in v3:
time: 135 us; the launch traced here: 134 us
  waiting for transfers between devices  60.3 us (45%)
  starting transfers between devices  41 us (30%)
  Pallas kernels  12.7 us (9%)
  blocking collectives  12.6 us (9%)
  local copies, waits for them, and re-layouts  3.26 us (2%)
  other arithmetic  2.25 us (2%)
  between operations  2.22 us (2%)
    all_to_all x3, waiting for transfers between devices, exchange(): lax.all_to_all(blocks, axis, 0, 0, tiled=True, axis_index_groups=groups)  36.2 us
    all_to_all x3, starting transfers between devices, exchange(): lax.all_to_all(blocks, axis, 0, 0, tiled=True, axis_index_groups=groups)  23.1 us
    all_to_all x1, blocking collectives, exchange(): lax.all_to_all(blocks, axis, 0, 0, tiled=True, axis_index_groups=groups)  12.6 us
    ppermute x6, waiting for transfers between devices, shifted(): lax.ppermute(blocks[shift], axis, [(k, (k + shift) % size) for k in range...  10.5 us
    ppermute x6, waiting for transfers between devices, around(): lax.ppermute(blocks[shift], 'col', [(o * size + i, o * size + (i + sign *...  9.97 us
    ppermute x6, starting transfers between devices, shifted(): lax.ppermute(blocks[shift], axis, [(k, (k + shift) % size) for k in range...  8.74 us
    ppermute x6, starting transfers between devices, around(): lax.ppermute(blocks[shift], 'col', [(o * size + i, o * size + (i + sign *...  8.71 us
    pallas_call x1, Pallas kernels, mix(): pl.pallas_call(mixer_kernel, in_specs=[pl.BlockSpec(memory_space=pltpu.HB...  4.84 us
  transfers between devices with their start and end apart: 18, of which 16 were waited for; matrix products, arithmetic and copies ran while one was open for 1% of the time, Pallas kernels for 3%

profile of v3, /device:TPU:2, one launch (start us, length us, event | category | flops | bytes accessed | tf_op | source)
XLA Modules:
  0.0 134.3 jit_solution(2139856497747809871)
XLA Ops:
  1.3 4.8 %mixer.1 = bf16[4,32,4,192]{3,2,1,0:T(4,128)(2,1)} custom-call(s32[1,1]{1,0:T(1,128)} %bitcast.20.refs_0_, bf16[1,4,2048]{2,1,0:T(4,128)(2,1)} %refs_1_.4, bf16[1,4,512]{2,1,0:T(4,128)(2,1)} %refs_2_.1, bf16[1,4,512]{2,1,0:T(4,128)(2,1)} %refs_3_.1, bf16[1,4,4096]{2,1,0:T(4,128)(2,1)} %x_ref.1, bf16[1,4,4096]{2,1,0:T(4,128)(2,1)} %refs_5_.1, ...), custom_call_target="tpu_custom_call" | custom-call | tf_op jit(solution)/shard_map/mixer/pallas_call | solution.py:161
  6.2 15.5 %all-to-all-start = ((bf16[128,4,192]{2,1,0:T(4,128)(2,1)}), bf16[128,4,192]{2,1,0:T(4,128)(2,1)S(1)}, u32[]{:S(2)}, u32[]{:S(2)}) async-start(bf16[128,4,192]{2,1,0:T(4,128)(2,1)} %bitcast.29), calls=%async_computation | async-start | bytes 524288 | tf_op jit(solution)/shard_map/all_to_all | solution.py:360
  21.7 0.1 reshape.61
  21.9 13.3 %all-to-all-done = bf16[128,4,192]{2,1,0:T(4,128)(2,1)S(1)} async-done(((bf16[128,4,192]{2,1,0:T(4,128)(2,1)}), bf16[128,4,192]{2,1,0:T(4,128)(2,1)S(1)}, u32[]{:S(2)}, u32[]{:S(2)}) %all-to-all-start) | async-done | bytes 196640 | tf_op jit(solution)/shard_map/all_to_all | solution.py:360
  35.2 0.7 gather_fusion.1
  35.9 0.1 broadcast_select_fusion
  36.0 0.1 reshape.63.refs_0_
  36.1 0.3 project.1
  36.5 0.0 copy-start.9
  36.5 0.0 copy-start.5
  36.5 0.1 collective-permute-start
  36.6 0.7 gather_fusion
  37.3 0.1 broadcast_select_fusion.1
  37.4 0.1 reshape.62.refs_0_
  37.5 1.1 collective-permute-done.refs_2_
  38.7 1.2 merge.1.refs_0_
  39.8 0.1 collective-permute-start.1
  40.0 4.2 %all-to-all-start.1 = ((bf16[32,8,1280]{2,1,0:T(8,128)(2,1)}), bf16[32,8,1280]{2,1,0:T(8,128)(2,1)S(1)}, u32[]{:S(2)}, u32[]{:S(2)}) async-start(bf16[32,8,1280]{2,1,0:T(8,128)(2,1)} %bitcast.6), calls=%async_computation.1 | async-start | bytes 1310720 | tf_op jit(solution)/shard_map/all_to_all | solution.py:360
  44.2 0.2 collective-permute-start.2
  44.4 2.5 %collective-permute-done.2.refs_4_ = bf16[336,1280]{1,0:T(8,128)(2,1)S(1)} collective-permute-done((bf16[336,1280]{1,0:T(8,128)(2,1)}, bf16[336,1280]{1,0:T(8,128)(2,1)S(1)}, u32[]{:S(2)}, u32[]{:S(2)}) %collective-permute-start.2) | collective-permute-done | bytes 860192 | tf_op jit(solution)/shard_map/ppermute | solution.py:388
  46.9 18.2 %all-to-all-done.1.refs_0_ = bf16[32,8,1280]{2,1,0:T(8,128)(2,1)S(1)} async-done(((bf16[32,8,1280]{2,1,0:T(8,128)(2,1)}), bf16[32,8,1280]{2,1,0:T(8,128)(2,1)S(1)}, u32[]{:S(2)}, u32[]{:S(2)}) %all-to-all-start.1) | async-done | bytes 655392 | tf_op jit(solution)/shard_map/all_to_all | solution.py:360
  65.1 0.1 arrive.1
  65.2 12.6 %all_to_all.20 = bf16[8,8,1280]{2,1,0:T(8,128)(2,1)S(1)} all-to-all(bf16[8,8,1280]{2,1,0:T(8,128)(2,1)S(1)} %get-tuple-element.22), channel_id=1, replica_groups={{0,4,8,12,16,20,24,28},{1,5,9,13,17,21,25,29},{2,6,10,14,18,22,26,30},{..., dimensions={0} | all-to-all | bytes 327680 | tf_op jit(solution)/shard_map/all_to_all | solution.py:360
  77.8 0.5 collective-permute-start.3
  78.4 2.4 %collective-permute-start.4 = (bf16[8,8,1280]{2,1,0:T(8,128)(2,1)S(1)}, bf16[8,8,1280]{2,1,0:T(8,128)(2,1)S(1)}, u32[]{:S(2)}, u32[]{:S(2)}) collective-permute-start(bf16[8,8,1280]{2,1,0:T(8,128)(2,1)S(1)} %all_to_all.20), channel_id=1, source_target_pairs={{0,2},{1,3},{2,0},{3,1},{4,6},{5,7},{6,4},{7,5},{8,10},{9,11},{10,... | collective-permute-start | bytes 491528 | tf_op jit(solution)/shard_map/ppermute | solution.py:374
  80.8 1.5 %collective-permute-start.5 = (bf16[8,8,1280]{2,1,0:T(8,128)(2,1)S(1)}, bf16[8,8,1280]{2,1,0:T(8,128)(2,1)S(1)}, u32[]{:S(2)}, u32[]{:S(2)}) collective-permute-start(bf16[8,8,1280]{2,1,0:T(8,128)(2,1)S(1)} %all_to_all.20), channel_id=1, source_target_pairs={{0,3},{1,0},{2,1},{3,2},{4,7},{5,4},{6,5},{7,6},{8,11},{9,8},{10,9... | collective-permute-start | bytes 491528 | tf_op jit(solution)/shard_map/ppermute | solution.py:374
  82.2 4.1 %collective-permute-done.3 = bf16[8,8,1280]{2,1,0:T(8,128)(2,1)S(1)} collective-permute-done((bf16[8,8,1280]{2,1,0:T(8,128)(2,1)S(1)}, bf16[8,8,1280]{2,1,0:T(8,128)(2,1)S(1)}, u32[]{:S(2)}, u32[]{:S(2)}) %collective-permute-start.3) | collective-permute-done | bytes 163872 | tf_op jit(solution)/shard_map/ppermute | solution.py:374
  86.3 0.6 collective-permute-done.5
  87.0 1.5 %copy-done.2 = bf16[1280,2,336]{0,2,1:T(8,128)(2,1)S(1)} copy-done((bf16[1280,2,336]{0,2,1:T(8,128)(2,1)S(1)}, bf16[1280,2,336]{0,2,1:T(8,128)(2,1)}, u32[]{:S(2)}) %copy-start.2) | copy-done | bytes 1720344
  88.4 1.3 widen.1
  89.8 0.0 copy-start.3
  89.8 2.1 %collective-permute-start.8 = (bf16[64,1408]{1,0:T(8,128)(2,1)S(1)}, bf16[64,1408]{1,0:T(8,128)(2,1)S(1)}, u32[]{:S(2)}, u32[]{:S(2)}) collective-permute-start(bf16[64,1408]{1,0:T(8,128)(2,1)S(1)} %get-tuple-element.26), channel_id=1, source_target_pairs={{0,96},{32,0},{64,32},{96,64},{1,97},{33,1},{65,33},{97,65},{2,98}... | collective-permute-start | bytes 540680 | tf_op jit(solution)/shard_map/ppermute | solution.py:366
  91.9 1.0 collective-permute-start.7
  92.9 1.1 collective-permute-start.6
  94.0 0.1 pad.1.clone
  94.1 2.2 %collective-permute-done.8 = bf16[64,1408]{1,0:T(8,128)(2,1)S(1)} collective-permute-done((bf16[64,1408]{1,0:T(8,128)(2,1)S(1)}, bf16[64,1408]{1,0:T(8,128)(2,1)S(1)}, u32[]{:S(2)}, u32[]{:S(2)}) %collective-permute-start.8) | collective-permute-done | bytes 180256 | tf_op jit(solution)/shard_map/ppermute | solution.py:366
  96.3 2.6 %collective-permute-done.7 = bf16[64,1408]{1,0:T(8,128)(2,1)S(1)} collective-permute-done((bf16[64,1408]{1,0:T(8,128)(2,1)S(1)}, bf16[64,1408]{1,0:T(8,128)(2,1)S(1)}, u32[]{:S(2)}, u32[]{:S(2)}) %collective-permute-start.7) | collective-permute-done | bytes 180256 | tf_op jit(solution)/shard_map/ppermute | solution.py:366
  98.9 1.4 %collective-permute-done.6 = bf16[64,1408]{1,0:T(8,128)(2,1)S(1)} collective-permute-done((bf16[64,1408]{1,0:T(8,128)(2,1)S(1)}, bf16[64,1408]{1,0:T(8,128)(2,1)S(1)}, u32[]{:S(2)}, u32[]{:S(2)}) %collective-permute-start.6) | collective-permute-done | bytes 180256 | tf_op jit(solution)/shard_map/ppermute | solution.py:366
  100.3 0.1 convert_add_fusion
  100.4 0.2 fusion.6
  100.6 0.1 broadcast_multiply_fusion
  100.7 0.0 copy-start
  100.7 0.0 copy-start.4
  100.7 0.0 copy-start.6
  100.7 0.0 copy-start.7
  100.8 0.1 fusion.2
  100.9 1.6 %collective-permute-start.9 = (bf16[64,720]{1,0:T(8,128)(2,1)S(1)}, bf16[64,720]{1,0:T(8,128)(2,1)S(1)}, u32[]{:S(2)}, u32[]{:S(2)}) collective-permute-start(bf16[64,720]{1,0:T(8,128)(2,1)S(1)} %pad_maximum_fusion.refs_0_), channel_id=1, source_target_pairs={{0,32},{32,64},{64,96},{96,0},{1,33},{33,65},{65,97},{97,1},{2,34}... | collective-permute-start | bytes 276488 | tf_op jit(solution)/shard_map/ppermute | solution.py:366
  102.6 1.8 %collective-permute-start.10 = (bf16[64,720]{1,0:T(8,128)(2,1)S(1)}, bf16[64,720]{1,0:T(8,128)(2,1)S(1)}, u32[]{:S(2)}, u32[]{:S(2)}) collective-permute-start(bf16[64,720]{1,0:T(8,128)(2,1)S(1)} %pad_maximum_fusion.refs_0_), channel_id=1, source_target_pairs={{0,64},{32,96},{64,0},{96,32},{1,65},{33,97},{65,1},{97,33},{2,66}... | collective-permute-start | bytes 276488 | tf_op jit(solution)/shard_map/ppermute | solution.py:366
  104.4 1.1 collective-permute-start.11
  105.5 0.2 collective-permute-done.9.refs_1_
  105.6 3.1 %collective-permute-done.10.refs_2_ = bf16[64,720]{1,0:T(8,128)(2,1)S(1)} collective-permute-done((bf16[64,720]{1,0:T(8,128)(2,1)S(1)}, bf16[64,720]{1,0:T(8,128)(2,1)S(1)}, u32[]{:S(2)}, u32[]{:S(2)}) %collective-permute-start.10) | collective-permute-done | bytes 92192 | tf_op jit(solution)/shard_map/ppermute | solution.py:366
  108.8 1.0 collective-permute-done.11.refs_3_
  109.7 0.9 narrow.1
  110.6 1.0 collective-permute-start.14
  111.6 3.2 %collective-permute-start.13 = (bf16[64,1280]{1,0:T(8,128)(2,1)S(1)}, bf16[64,1280]{1,0:T(8,128)(2,1)S(1)}, u32[]{:S(2)}, u32[]{:S(2)}) collective-permute-start(bf16[64,1280]{1,0:T(8,128)(2,1)S(1)} %get-tuple-element.29), channel_id=1, source_target_pairs={{0,2},{1,3},{2,0},{3,1},{4,6},{5,7},{6,4},{7,5},{8,10},{9,11},{10,... | collective-permute-start | bytes 491528 | tf_op jit(solution)/shard_map/ppermute | solution.py:374
  114.8 0.1 collective-permute-start.12
  114.9 2.3 %collective-permute-done.14 = bf16[64,1280]{1,0:T(8,128)(2,1)S(1)} collective-permute-done((bf16[64,1280]{1,0:T(8,128)(2,1)S(1)}, bf16[64,1280]{1,0:T(8,128)(2,1)S(1)}, u32[]{:S(2)}, u32[]{:S(2)}) %collective-permute-start.14) | collective-permute-done | bytes 163872 | tf_op jit(solution)/shard_map/ppermute | solution.py:374
  117.2 2.7 %collective-permute-done.13 = bf16[64,1280]{1,0:T(8,128)(2,1)S(1)} collective-permute-done((bf16[64,1280]{1,0:T(8,128)(2,1)S(1)}, bf16[64,1280]{1,0:T(8,128)(2,1)S(1)}, u32[]{:S(2)}, u32[]{:S(2)}) %collective-permute-start.13) | collective-permute-done | bytes 163872 | tf_op jit(solution)/shard_map/ppermute | solution.py:374
  119.9 0.3 collective-permute-done.12
  120.2 0.7 fusion
  120.9 3.4 %all-to-all-start.3 = ((bf16[8,8,1280]{2,1,0:T(8,128)(2,1)}), bf16[8,8,1280]{2,1,0:T(8,128)(2,1)S(1)}, u32[]{:S(2)}, u32[]{:S(2)}) async-start(bf16[8,8,1280]{2,1,0:T(8,128)(2,1)} %fusion), calls=%async_computation.3 | async-start | bytes 327680 | tf_op jit(solution)/shard_map/all_to_all | solution.py:360
  125.0 4.0 %final_state.1 = f32[1,32,128,128]{3,2,1,0:T(8,128)} custom-call(s32[1]{0:T(128)S(6)} %copy.24.accepted_ref, bf16[1,4,4096]{2,1,0:T(4,128)(2,1)S(1)} %copy-done.4, bf16[1,4,128]{2,1,0:T(4,128)(2,1)S(1)} %copy-done.7, f32[1,4,32]{2,1,0:T(4,128)S(1)} %copy-done.6, f32[1,32]{1,0:T(1,128)S(1)} %bitcast.28, f32[1,32,128,128]{3,2,1,0:T(8,128)S(1)} %copy-done, ...), custom_call_target="tpu_custom_call" | custom-call | tf_op jit(solution)/shard_map/final_state/pallas_call | solution.py:340
  129.0 4.6 %all-to-all-done.3 = bf16[8,8,1280]{2,1,0:T(8,128)(2,1)S(1)} async-done(((bf16[8,8,1280]{2,1,0:T(8,128)(2,1)}), bf16[8,8,1280]{2,1,0:T(8,128)(2,1)S(1)}, u32[]{:S(2)}, u32[]{:S(2)}) %all-to-all-start.3) | async-done | bytes 163872 | tf_op jit(solution)/shard_map/all_to_all | solution.py:360
  133.7 0.6 add_convert_fusion.1
  (26 shorter events, 0.2 us)
Async XLA Ops:
  1.3 20.4 %copy-start.10 = (s32[128]{0:T(128)S(1)}, s32[128]{0:T(128)}, u32[]{:S(2)}) copy-start(s32[128]{0:T(128)} %param.39) | copy-start | bytes 1540
  1.3 34.8 %copy-start.1 = (bf16[192,1280]{1,0:T(8,128)(2,1)S(1)}, bf16[192,1280]{1,0:T(8,128)(2,1)}, u32[]{:S(2)}) copy-start(bf16[192,1280]{1,0:T(8,128)(2,1)} %refs_1_.6) | copy-start | bytes 1474564
  6.2 29.0 %all-to-all-start = ((bf16[128,4,192]{2,1,0:T(4,128)(2,1)}), bf16[128,4,192]{2,1,0:T(4,128)(2,1)S(1)}, u32[]{:S(2)}, u32[]{:S(2)}) async-start(bf16[128,4,192]{2,1,0:T(4,128)(2,1)} %bitcast.29), calls=%async_computation | async-start | bytes 524288 | tf_op jit(solution)/shard_map/all_to_all | solution.py:360
  36.5 7.9 %copy-start.9 = (f32[1280]{0:T(1024)S(1)}, f32[1280]{0:T(1024)}, u32[]{:S(2)}) copy-start(f32[1280]{0:T(1024)} %param.41) | copy-start | bytes 15364
  36.5 28.6 %copy-start.5 = (bf16[8,1280]{1,0:T(8,128)(2,1)S(1)}, bf16[8,1280]{1,0:T(8,128)(2,1)}, u32[]{:S(2)}) copy-start(bf16[8,1280]{1,0:T(8,128)(2,1)} %refs_1_.7) | copy-start | bytes 61444
  36.5 2.2 %collective-permute-start = (bf16[256,1280]{1,0:T(8,128)(2,1)S(1)}, bf16[256,1280]{1,0:T(8,128)(2,1)S(1)}, u32[]{:S(2)}, u32[]{:S(2)}) collective-permute-start(bf16[256,1280]{1,0:T(8,128)(2,1)S(1)} %project.1), channel_id=1, source_target_pairs={{0,128},{128,0},{1,129},{129,1},{2,130},{130,2},{3,131},{131,3},{4... | collective-permute-start | bytes 1966088 | tf_op jit(solution)/shard_map/ppermute | solution.py:388
  39.8 7.0 %collective-permute-start.1 = (bf16[672,1280]{1,0:T(8,128)(2,1)}, bf16[672,1280]{1,0:T(8,128)(2,1)S(1)}, u32[]{:S(2)}, u32[]{:S(2)}) collective-permute-start(bf16[672,1280]{1,0:T(8,128)(2,1)} %bitcast.21), channel_id=1, source_target_pairs={{0,128},{128,0},{1,129},{129,1},{2,130},{130,2},{3,131},{131,3},{4... | collective-permute-start | bytes 5160968 | tf_op jit(solution)/shard_map/ppermute | solution.py:388
  40.0 25.1 %all-to-all-start.1 = ((bf16[32,8,1280]{2,1,0:T(8,128)(2,1)}), bf16[32,8,1280]{2,1,0:T(8,128)(2,1)S(1)}, u32[]{:S(2)}, u32[]{:S(2)}) async-start(bf16[32,8,1280]{2,1,0:T(8,128)(2,1)} %bitcast.6), calls=%async_computation.1 | async-start | bytes 1310720 | tf_op jit(solution)/shard_map/all_to_all | solution.py:360
  44.2 2.7 %collective-permute-start.2 = (bf16[336,1280]{1,0:T(8,128)(2,1)}, bf16[336,1280]{1,0:T(8,128)(2,1)S(1)}, u32[]{:S(2)}, u32[]{:S(2)}) collective-permute-start(bf16[336,1280]{1,0:T(8,128)(2,1)} %refs_5_.2), channel_id=1, source_target_pairs={{0,128},{128,0},{1,129},{129,1},{2,130},{130,2},{3,131},{131,3},{4... | collective-permute-start | bytes 2580488 | tf_op jit(solution)/shard_map/ppermute | solution.py:388
  77.8 8.5 %collective-permute-start.3 = (bf16[8,8,1280]{2,1,0:T(8,128)(2,1)S(1)}, bf16[8,8,1280]{2,1,0:T(8,128)(2,1)S(1)}, u32[]{:S(2)}, u32[]{:S(2)}) collective-permute-start(bf16[8,8,1280]{2,1,0:T(8,128)(2,1)S(1)} %all_to_all.20), channel_id=1, source_target_pairs={{0,1},{1,2},{2,3},{3,0},{4,5},{5,6},{6,7},{7,4},{8,9},{9,10},{10,1... | collective-permute-start | bytes 491528 | tf_op jit(solution)/shard_map/ppermute | solution.py:374
  78.4 8.0 %collective-permute-start.4 = (bf16[8,8,1280]{2,1,0:T(8,128)(2,1)S(1)}, bf16[8,8,1280]{2,1,0:T(8,128)(2,1)S(1)}, u32[]{:S(2)}, u32[]{:S(2)}) collective-permute-start(bf16[8,8,1280]{2,1,0:T(8,128)(2,1)S(1)} %all_to_all.20), channel_id=1, source_target_pairs={{0,2},{1,3},{2,0},{3,1},{4,6},{5,7},{6,4},{7,5},{8,10},{9,11},{10,... | collective-permute-start | bytes 491528 | tf_op jit(solution)/shard_map/ppermute | solution.py:374
  80.8 6.2 %collective-permute-start.5 = (bf16[8,8,1280]{2,1,0:T(8,128)(2,1)S(1)}, bf16[8,8,1280]{2,1,0:T(8,128)(2,1)S(1)}, u32[]{:S(2)}, u32[]{:S(2)}) collective-permute-start(bf16[8,8,1280]{2,1,0:T(8,128)(2,1)S(1)} %all_to_all.20), channel_id=1, source_target_pairs={{0,3},{1,0},{2,1},{3,2},{4,7},{5,4},{6,5},{7,6},{8,11},{9,8},{10,9... | collective-permute-start | bytes 491528 | tf_op jit(solution)/shard_map/ppermute | solution.py:374
  87.0 1.5 %copy-start.2 = (bf16[1280,2,336]{0,2,1:T(8,128)(2,1)S(1)}, bf16[1280,2,336]{0,2,1:T(8,128)(2,1)}, u32[]{:S(2)}) copy-start(bf16[1280,2,336]{0,2,1:T(8,128)(2,1)} %param.42) | copy-start | bytes 5160964
  89.8 20.0 %copy-start.3 = (bf16[336,1280]{1,0:T(8,128)(2,1)S(1)}, bf16[336,1280]{1,0:T(8,128)(2,1)}, u32[]{:S(2)}) copy-start(bf16[336,1280]{1,0:T(8,128)(2,1)} %refs_5_.2) | copy-start | bytes 2580484
  89.8 6.5 %collective-permute-start.8 = (bf16[64,1408]{1,0:T(8,128)(2,1)S(1)}, bf16[64,1408]{1,0:T(8,128)(2,1)S(1)}, u32[]{:S(2)}, u32[]{:S(2)}) collective-permute-start(bf16[64,1408]{1,0:T(8,128)(2,1)S(1)} %get-tuple-element.26), channel_id=1, source_target_pairs={{0,96},{32,0},{64,32},{96,64},{1,97},{33,1},{65,33},{97,65},{2,98}... | collective-permute-start | bytes 540680 | tf_op jit(solution)/shard_map/ppermute | solution.py:366
  91.9 7.0 %collective-permute-start.7 = (bf16[64,1408]{1,0:T(8,128)(2,1)S(1)}, bf16[64,1408]{1,0:T(8,128)(2,1)S(1)}, u32[]{:S(2)}, u32[]{:S(2)}) collective-permute-start(bf16[64,1408]{1,0:T(8,128)(2,1)S(1)} %get-tuple-element.25), channel_id=1, source_target_pairs={{0,64},{32,96},{64,0},{96,32},{1,65},{33,97},{65,1},{97,33},{2,66}... | collective-permute-start | bytes 540680 | tf_op jit(solution)/shard_map/ppermute | solution.py:366
  92.9 7.4 %collective-permute-start.6 = (bf16[64,1408]{1,0:T(8,128)(2,1)S(1)}, bf16[64,1408]{1,0:T(8,128)(2,1)S(1)}, u32[]{:S(2)}, u32[]{:S(2)}) collective-permute-start(bf16[64,1408]{1,0:T(8,128)(2,1)S(1)} %get-tuple-element.24), channel_id=1, source_target_pairs={{0,32},{32,64},{64,96},{96,0},{1,33},{33,65},{65,97},{97,1},{2,34}... | collective-permute-start | bytes 540680 | tf_op jit(solution)/shard_map/ppermute | solution.py:366
  100.7 24.2 %copy-start = (f32[1,32,128,128]{3,2,1,0:T(8,128)S(1)}, f32[1,32,128,128]{3,2,1,0:T(8,128)}, u32[]{:S(2)}) copy-start(f32[1,32,128,128]{3,2,1,0:T(8,128)} %state_ref.1) | copy-start | bytes 6291460
  100.7 24.2 %copy-start.4 = (bf16[1,4,4096]{2,1,0:T(4,128)(2,1)S(1)}, bf16[1,4,4096]{2,1,0:T(4,128)(2,1)}, u32[]{:S(2)}) copy-start(bf16[1,4,4096]{2,1,0:T(4,128)(2,1)} %x_ref.1) | copy-start | bytes 98308
  100.7 24.2 %copy-start.6 = (f32[1,4,32]{2,1,0:T(4,128)S(1)}, f32[1,4,32]{2,1,0:T(4,128)}, u32[]{:S(2)}) copy-start(f32[1,4,32]{2,1,0:T(4,128)} %dt_ref.1) | copy-start | bytes 1540
  100.7 24.2 %copy-start.7 = (bf16[1,4,128]{2,1,0:T(4,128)(2,1)S(1)}, bf16[1,4,128]{2,1,0:T(4,128)(2,1)}, u32[]{:S(2)}) copy-start(bf16[1,4,128]{2,1,0:T(4,128)(2,1)} %in_map_ref.1) | copy-start | bytes 3076
  100.7 24.2 %copy-start.8 = (f32[32]{0:T(128)S(1)}, f32[32]{0:T(128)}, u32[]{:S(2)}) copy-start(f32[32]{0:T(128)} %param.35) | copy-start | bytes 388
  100.9 4.7 %collective-permute-start.9 = (bf16[64,720]{1,0:T(8,128)(2,1)S(1)}, bf16[64,720]{1,0:T(8,128)(2,1)S(1)}, u32[]{:S(2)}, u32[]{:S(2)}) collective-permute-start(bf16[64,720]{1,0:T(8,128)(2,1)S(1)} %pad_maximum_fusion.refs_0_), channel_id=1, source_target_pairs={{0,32},{32,64},{64,96},{96,0},{1,33},{33,65},{65,97},{97,1},{2,34}... | collective-permute-start | bytes 276488 | tf_op jit(solution)/shard_map/ppermute | solution.py:366
  102.6 6.2 %collective-permute-start.10 = (bf16[64,720]{1,0:T(8,128)(2,1)S(1)}, bf16[64,720]{1,0:T(8,128)(2,1)S(1)}, u32[]{:S(2)}, u32[]{:S(2)}) collective-permute-start(bf16[64,720]{1,0:T(8,128)(2,1)S(1)} %pad_maximum_fusion.refs_0_), channel_id=1, source_target_pairs={{0,64},{32,96},{64,0},{96,32},{1,65},{33,97},{65,1},{97,33},{2,66}... | collective-permute-start | bytes 276488 | tf_op jit(solution)/shard_map/ppermute | solution.py:366
  104.4 5.4 %collective-permute-start.11 = (bf16[64,720]{1,0:T(8,128)(2,1)S(1)}, bf16[64,720]{1,0:T(8,128)(2,1)S(1)}, u32[]{:S(2)}, u32[]{:S(2)}) collective-permute-start(bf16[64,720]{1,0:T(8,128)(2,1)S(1)} %pad_maximum_fusion.refs_0_), channel_id=1, source_target_pairs={{0,96},{32,0},{64,32},{96,64},{1,97},{33,1},{65,33},{97,65},{2,98}... | collective-permute-start | bytes 276488 | tf_op jit(solution)/shard_map/ppermute | solution.py:366
  110.6 6.6 %collective-permute-start.14 = (bf16[64,1280]{1,0:T(8,128)(2,1)S(1)}, bf16[64,1280]{1,0:T(8,128)(2,1)S(1)}, u32[]{:S(2)}, u32[]{:S(2)}) collective-permute-start(bf16[64,1280]{1,0:T(8,128)(2,1)S(1)} %get-tuple-element.30), channel_id=1, source_target_pairs={{0,1},{1,2},{2,3},{3,0},{4,5},{5,6},{6,7},{7,4},{8,9},{9,10},{10,1... | collective-permute-start | bytes 491528 | tf_op jit(solution)/shard_map/ppermute | solution.py:374
  111.6 8.3 %collective-permute-start.13 = (bf16[64,1280]{1,0:T(8,128)(2,1)S(1)}, bf16[64,1280]{1,0:T(8,128)(2,1)S(1)}, u32[]{:S(2)}, u32[]{:S(2)}) collective-permute-start(bf16[64,1280]{1,0:T(8,128)(2,1)S(1)} %get-tuple-element.29), channel_id=1, source_target_pairs={{0,2},{1,3},{2,0},{3,1},{4,6},{5,7},{6,4},{7,5},{8,10},{9,11},{10,... | collective-permute-start | bytes 491528 | tf_op jit(solution)/shard_map/ppermute | solution.py:374
  114.8 5.3 %collective-permute-start.12 = (bf16[64,1280]{1,0:T(8,128)(2,1)S(1)}, bf16[64,1280]{1,0:T(8,128)(2,1)S(1)}, u32[]{:S(2)}, u32[]{:S(2)}) collective-permute-start(bf16[64,1280]{1,0:T(8,128)(2,1)S(1)} %get-tuple-element.28), channel_id=1, source_target_pairs={{0,3},{1,0},{2,1},{3,2},{4,7},{5,4},{6,5},{7,6},{8,11},{9,8},{10,9... | collective-permute-start | bytes 491528 | tf_op jit(solution)/shard_map/ppermute | solution.py:374
  120.9 12.7 %all-to-all-start.3 = ((bf16[8,8,1280]{2,1,0:T(8,128)(2,1)}), bf16[8,8,1280]{2,1,0:T(8,128)(2,1)S(1)}, u32[]{:S(2)}, u32[]{:S(2)}) async-start(bf16[8,8,1280]{2,1,0:T(8,128)(2,1)} %fusion), calls=%async_computation.3 | async-start | bytes 327680 | tf_op jit(solution)/shard_map/all_to_all | solution.py:360

commit v4 on v3

--- a/solution.py
+++ b/solution.py
@@ -257,6 +257,38 @@
         compiler_params=pltpu.CompilerParams(vmem_limit_bytes=16 * 2**20),
         name="widen",
     )(gain, *tokens, *weights)
+
+
+def gate_kernel(units, *refs):
+    f32 = jnp.float32
+    parts, out_ref = refs[:-1], refs[-1]
+    summed = parts[0][...].astype(f32)
+    for part in parts[1:]:
+        summed = summed + part[...].astype(f32)
+    squares = summed[:, 4 * units : 4 * units + 1] + summed[:, 4 * units + 1 : 4 * units + 2]
+    summed = summed * lax.rsqrt(squares / D + norm_eps)
+    hidden = []
+    for first in (0, 2 * units):
+        gate = summed[:, first : first + units]
+        up = summed[:, first + units : first + 2 * units]
+        hidden.append(gate * jax.nn.sigmoid(gate) * up)
+    blank = jnp.zeros((summed.shape[0], out_ref.shape[1] - 2 * units), f32)
+    hidden = jnp.concatenate([hidden[0], blank, hidden[1]], axis=1)
+    out_ref[...] = hidden.astype(out_ref.dtype)
+
+
+def add_kernel(*refs):
+    total = refs[0][...].astype(jnp.float32)
+    for ref in refs[1:-1]:
+        total = total + ref[...].astype(jnp.float32)
+    refs[-1][...] = total.astype(refs[-1].dtype)
+
+
+def finish_kernel(parts_ref, stream_ref, out_ref):
+    total = stream_ref[...]
+    for c in range(parts_ref.shape[0]):
+        total = total + parts_ref[c].astype(jnp.float32)
+    out_ref[...] = total.astype(out_ref.dtype)
 
 
 def narrow_kernel(rows, places, *refs):
@@ -457,19 +489,15 @@
         block.reshape(-1, block.shape[2]) for block in around([spread] * inner, inner, 1)
     ]
     sums = shifted(widen(tokens, gain, in_pieces, in_places, rows), "row")
-    summed = functools.reduce(jnp.add, [part.astype(f32) for part in sums])
-    mean_sq = (summed[:, 4 * units] + summed[:, 4 * units + 1]) / D
-    summed = summed * lax.rsqrt(mean_sq[:, None] + norm_eps)
-    gate = [summed[:, :units], summed[:, 2 * units : 3 * units]]
-    up = [summed[:, units : 2 * units], summed[:, 3 * units : 4 * units]]
-    hidden = [(jax.nn.silu(g) * u).astype(bf16) for g, u in zip(gate, up)]
-    blank = jnp.zeros((hidden[0].shape[0], padded - units), bf16)
-    hidden = jnp.concatenate([hidden[0], blank, hidden[1]], axis=1)
+    held = jax.ShapeDtypeStruct((sums[0].shape[0], padded + units), bf16)
+    hidden = on_core(functools.partial(gate_kernel, units), sums, held, "gate")
     down = narrow(shifted([hidden] * rows, "row"), down_pieces, down_places)
     down = around(down, inner, -1)
-    down = functools.reduce(jnp.add, [part.astype(f32) for part in down]).astype(bf16)
+    held = jax.ShapeDtypeStruct(down[0].shape, bf16)
+    down = on_core(add_kernel, down, held, "add")
     down = exchange(down.reshape(cols // inner, -1, down.shape[1]), "col", lines)
-    layer_out = (stream + jnp.sum(down.astype(f32), axis=0)).astype(bf16)
+    held = jax.ShapeDtypeStruct(stream.shape, bf16)
+    layer_out = on_core(finish_kernel, (down, stream), held, "finish")
     return (layer_out, state_next)
 
 

time: 135 us -> 136 us (level)
  other arithmetic: 2.25 us -> 0.32 us
  Pallas kernels: 12.7 us -> 14.4 us
    ppermute x6, waiting for transfers between devices: 9.97 us -> 12.3 us  [around(): lax.ppermute(blocks[shift], 'col', [(o * size + i, o * size + (i + sign *...]
    pallas_call x3 -> x6, Pallas kernels: 1.61 us -> 3.35 us  [on_core(): pl.pallas_call(lambda *refs: kernel(*refs[:count], *refs[count + len(afte...]
where the time goes in v4:
time: 136 us; the launch traced here: 135 us
  waiting for transfers between devices  61.3 us (45%)
  starting transfers between devices  40.5 us (30%)
  Pallas kernels  14.4 us (11%)
  blocking collectives  12.6 us (9%)
  local copies, waits for them, and re-layouts  3.18 us (2%)
  between operations  2.19 us (2%)
    all_to_all x3, waiting for transfers between devices, exchange(): lax.all_to_all(blocks, axis, 0, 0, tiled=True, axis_index_groups=groups)  36.2 us
    all_to_all x3, starting transfers between devices, exchange(): lax.all_to_all(blocks, axis, 0, 0, tiled=True, axis_index_groups=groups)  23.1 us
    all_to_all x1, blocking collectives, exchange(): lax.all_to_all(blocks, axis, 0, 0, tiled=True, axis_index_groups=groups)  12.6 us
    ppermute x6, waiting for transfers between devices, around(): lax.ppermute(blocks[shift], 'col', [(o * size + i, o * size + (i + sign *...  12.3 us
    ppermute x6, waiting for transfers between devices, shifted(): lax.ppermute(blocks[shift], axis, [(k, (k + shift) % size) for k in range...  9.2 us
    ppermute x6, starting transfers between devices, shifted(): lax.ppermute(blocks[shift], axis, [(k, (k + shift) % size) for k in range...  8.85 us
    ppermute x6, starting transfers between devices, around(): lax.ppermute(blocks[shift], 'col', [(o * size + i, o * size + (i + sign *...  8.14 us
    pallas_call x1, Pallas kernels, mix(): pl.pallas_call(mixer_kernel, in_specs=[pl.BlockSpec(memory_space=pltpu.HB...  4.84 us
  transfers between devices with their start and end apart: 18, of which 16 were waited for; matrix products, arithmetic and copies ran while one was open for 1% of the time, Pallas kernels for 3%

profile of v4, /device:TPU:2, one launch (start us, length us, event | category | flops | bytes accessed | tf_op | source)
XLA Modules:
  0.0 134.6 jit_solution(11806223330842202711)
XLA Ops:
  1.3 0.0 copy-start.10
  1.3 0.0 copy-start.1
  1.3 4.8 %mixer.1 = bf16[4,32,4,192]{3,2,1,0:T(4,128)(2,1)} custom-call(s32[1,1]{1,0:T(1,128)} %bitcast.19.refs_0_, bf16[1,4,2048]{2,1,0:T(4,128)(2,1)} %refs_1_.4, bf16[1,4,512]{2,1,0:T(4,128)(2,1)} %refs_2_.1, bf16[1,4,512]{2,1,0:T(4,128)(2,1)} %refs_3_.1, bf16[1,4,4096]{2,1,0:T(4,128)(2,1)} %x_ref.1, bf16[1,4,4096]{2,1,0:T(4,128)(2,1)} %refs_5_.1, ...), custom_call_target="tpu_custom_call" | custom-call | tf_op jit(solution)/shard_map/mixer/pallas_call | solution.py:161
  6.2 15.5 %all-to-all-start = ((bf16[128,4,192]{2,1,0:T(4,128)(2,1)}), bf16[128,4,192]{2,1,0:T(4,128)(2,1)S(1)}, u32[]{:S(2)}, u32[]{:S(2)}) async-start(bf16[128,4,192]{2,1,0:T(4,128)(2,1)} %bitcast.28), calls=%async_computation | async-start | bytes 524288 | tf_op jit(solution)/shard_map/all_to_all | solution.py:392
  21.7 0.1 reshape.59
  21.9 13.3 %all-to-all-done = bf16[128,4,192]{2,1,0:T(4,128)(2,1)S(1)} async-done(((bf16[128,4,192]{2,1,0:T(4,128)(2,1)}), bf16[128,4,192]{2,1,0:T(4,128)(2,1)S(1)}, u32[]{:S(2)}, u32[]{:S(2)}) %all-to-all-start) | async-done | bytes 196640 | tf_op jit(solution)/shard_map/all_to_all | solution.py:392
  35.2 0.7 gather_fusion.1
  35.9 0.1 broadcast_select_fusion
  36.0 0.1 reshape.61.refs_0_
  36.1 0.3 project.1
  36.5 0.0 copy-start.9
  36.5 0.0 copy-start.5
  36.5 0.1 collective-permute-start
  36.6 0.7 gather_fusion
  37.3 0.1 broadcast_select_fusion.1
  37.4 0.1 reshape.60.refs_0_
  37.5 1.1 collective-permute-done.refs_2_
  38.7 1.2 merge.1.refs_0_
  39.9 0.1 collective-permute-start.1
  40.0 4.2 %all-to-all-start.1 = ((bf16[32,8,1280]{2,1,0:T(8,128)(2,1)}), bf16[32,8,1280]{2,1,0:T(8,128)(2,1)S(1)}, u32[]{:S(2)}, u32[]{:S(2)}) async-start(bf16[32,8,1280]{2,1,0:T(8,128)(2,1)} %bitcast.6), calls=%async_computation.1 | async-start | bytes 1310720 | tf_op jit(solution)/shard_map/all_to_all | solution.py:392
  44.2 0.2 collective-permute-start.2
  44.4 2.5 %collective-permute-done.2.refs_4_ = bf16[336,1280]{1,0:T(8,128)(2,1)S(1)} collective-permute-done((bf16[336,1280]{1,0:T(8,128)(2,1)}, bf16[336,1280]{1,0:T(8,128)(2,1)S(1)}, u32[]{:S(2)}, u32[]{:S(2)}) %collective-permute-start.2) | collective-permute-done | bytes 860192 | tf_op jit(solution)/shard_map/ppermute | solution.py:420
  46.9 0.0 collective-permute-done.1.refs_4_
  46.9 18.2 %all-to-all-done.1.refs_0_ = bf16[32,8,1280]{2,1,0:T(8,128)(2,1)S(1)} async-done(((bf16[32,8,1280]{2,1,0:T(8,128)(2,1)}), bf16[32,8,1280]{2,1,0:T(8,128)(2,1)S(1)}, u32[]{:S(2)}, u32[]{:S(2)}) %all-to-all-start.1) | async-done | bytes 655392 | tf_op jit(solution)/shard_map/all_to_all | solution.py:392
  65.1 0.1 arrive.1
  65.2 12.6 %all_to_all.20 = bf16[8,8,1280]{2,1,0:T(8,128)(2,1)S(1)} all-to-all(bf16[8,8,1280]{2,1,0:T(8,128)(2,1)S(1)} %get-tuple-element.21), channel_id=1, replica_groups={{0,4,8,12,16,20,24,28},{1,5,9,13,17,21,25,29},{2,6,10,14,18,22,26,30},{..., dimensions={0} | all-to-all | bytes 327680 | tf_op jit(solution)/shard_map/all_to_all | solution.py:392
  77.8 0.5 collective-permute-start.3
  78.4 2.4 %collective-permute-start.4 = (bf16[8,8,1280]{2,1,0:T(8,128)(2,1)S(1)}, bf16[8,8,1280]{2,1,0:T(8,128)(2,1)S(1)}, u32[]{:S(2)}, u32[]{:S(2)}) collective-permute-start(bf16[8,8,1280]{2,1,0:T(8,128)(2,1)S(1)} %all_to_all.20), channel_id=1, source_target_pairs={{0,2},{1,3},{2,0},{3,1},{4,6},{5,7},{6,4},{7,5},{8,10},{9,11},{10,... | collective-permute-start | bytes 491528 | tf_op jit(solution)/shard_map/ppermute | solution.py:406
  80.8 1.5 %collective-permute-start.5 = (bf16[8,8,1280]{2,1,0:T(8,128)(2,1)S(1)}, bf16[8,8,1280]{2,1,0:T(8,128)(2,1)S(1)}, u32[]{:S(2)}, u32[]{:S(2)}) collective-permute-start(bf16[8,8,1280]{2,1,0:T(8,128)(2,1)S(1)} %all_to_all.20), channel_id=1, source_target_pairs={{0,3},{1,0},{2,1},{3,2},{4,7},{5,4},{6,5},{7,6},{8,11},{9,8},{10,9... | collective-permute-start | bytes 491528 | tf_op jit(solution)/shard_map/ppermute | solution.py:406
  82.2 4.1 %collective-permute-done.3 = bf16[8,8,1280]{2,1,0:T(8,128)(2,1)S(1)} collective-permute-done((bf16[8,8,1280]{2,1,0:T(8,128)(2,1)S(1)}, bf16[8,8,1280]{2,1,0:T(8,128)(2,1)S(1)}, u32[]{:S(2)}, u32[]{:S(2)}) %collective-permute-start.3) | collective-permute-done | bytes 163872 | tf_op jit(solution)/shard_map/ppermute | solution.py:406
  86.3 0.0 collective-permute-done.4
  86.3 0.6 collective-permute-done.5
  87.0 1.5 %copy-done.2 = bf16[1280,2,336]{0,2,1:T(8,128)(2,1)S(1)} copy-done((bf16[1280,2,336]{0,2,1:T(8,128)(2,1)S(1)}, bf16[1280,2,336]{0,2,1:T(8,128)(2,1)}, u32[]{:S(2)}) %copy-start.2) | copy-done | bytes 1720344
  88.4 1.3 widen.1
  89.8 0.0 copy-start
  89.8 0.0 copy-start.4
  89.8 0.0 copy-start.6
  89.8 0.0 copy-start.7
  89.8 0.0 copy-start.8
  89.8 1.6 %collective-permute-start.6 = (bf16[64,1408]{1,0:T(8,128)(2,1)S(1)}, bf16[64,1408]{1,0:T(8,128)(2,1)S(1)}, u32[]{:S(2)}, u32[]{:S(2)}) collective-permute-start(bf16[64,1408]{1,0:T(8,128)(2,1)S(1)} %get-tuple-element.23), channel_id=1, source_target_pairs={{0,32},{32,64},{64,96},{96,0},{1,33},{33,65},{65,97},{97,1},{2,34}... | collective-permute-start | bytes 540680 | tf_op jit(solution)/shard_map/ppermute | solution.py:398
  91.5 2.5 %collective-permute-start.7 = (bf16[64,1408]{1,0:T(8,128)(2,1)S(1)}, bf16[64,1408]{1,0:T(8,128)(2,1)S(1)}, u32[]{:S(2)}, u32[]{:S(2)}) collective-permute-start(bf16[64,1408]{1,0:T(8,128)(2,1)S(1)} %get-tuple-element.24), channel_id=1, source_target_pairs={{0,64},{32,96},{64,0},{96,32},{1,65},{33,97},{65,1},{97,33},{2,66}... | collective-permute-start | bytes 540680 | tf_op jit(solution)/shard_map/ppermute | solution.py:398
  94.0 0.0 collective-permute-start.8
  94.1 1.4 %collective-permute-done.6.refs_1_ = bf16[64,1408]{1,0:T(8,128)(2,1)S(1)} collective-permute-done((bf16[64,1408]{1,0:T(8,128)(2,1)S(1)}, bf16[64,1408]{1,0:T(8,128)(2,1)S(1)}, u32[]{:S(2)}, u32[]{:S(2)}) %collective-permute-start.6) | collective-permute-done | bytes 180256 | tf_op jit(solution)/shard_map/ppermute | solution.py:398
  95.4 3.2 %collective-permute-done.7.refs_2_ = bf16[64,1408]{1,0:T(8,128)(2,1)S(1)} collective-permute-done((bf16[64,1408]{1,0:T(8,128)(2,1)S(1)}, bf16[64,1408]{1,0:T(8,128)(2,1)S(1)}, u32[]{:S(2)}, u32[]{:S(2)}) %collective-permute-start.7) | collective-permute-done | bytes 180256 | tf_op jit(solution)/shard_map/ppermute | solution.py:398
  98.6 1.9 %collective-permute-done.8.refs_3_ = bf16[64,1408]{1,0:T(8,128)(2,1)S(1)} collective-permute-done((bf16[64,1408]{1,0:T(8,128)(2,1)S(1)}, bf16[64,1408]{1,0:T(8,128)(2,1)S(1)}, u32[]{:S(2)}, u32[]{:S(2)}) %collective-permute-start.8) | collective-permute-done | bytes 180256 | tf_op jit(solution)/shard_map/ppermute | solution.py:398
  100.5 0.3 gate.1.refs_0_
  100.9 2.6 %collective-permute-start.10 = (bf16[64,720]{1,0:T(8,128)(2,1)S(1)}, bf16[64,720]{1,0:T(8,128)(2,1)S(1)}, u32[]{:S(2)}, u32[]{:S(2)}) collective-permute-start(bf16[64,720]{1,0:T(8,128)(2,1)S(1)} %gate.1.refs_0_), channel_id=1, source_target_pairs={{0,64},{32,96},{64,0},{96,32},{1,65},{33,97},{65,1},{97,33},{2,66}... | collective-permute-start | bytes 276488 | tf_op jit(solution)/shard_map/ppermute | solution.py:398
  103.5 0.1 collective-permute-start.11
  103.6 1.9 %collective-permute-start.9 = (bf16[64,720]{1,0:T(8,128)(2,1)S(1)}, bf16[64,720]{1,0:T(8,128)(2,1)S(1)}, u32[]{:S(2)}, u32[]{:S(2)}) collective-permute-start(bf16[64,720]{1,0:T(8,128)(2,1)S(1)} %gate.1.refs_0_), channel_id=1, source_target_pairs={{0,32},{32,64},{64,96},{96,0},{1,33},{33,65},{65,97},{97,1},{2,34}... | collective-permute-start | bytes 276488 | tf_op jit(solution)/shard_map/ppermute | solution.py:398
  105.5 1.6 %collective-permute-done.10.refs_2_ = bf16[64,720]{1,0:T(8,128)(2,1)S(1)} collective-permute-done((bf16[64,720]{1,0:T(8,128)(2,1)S(1)}, bf16[64,720]{1,0:T(8,128)(2,1)S(1)}, u32[]{:S(2)}, u32[]{:S(2)}) %collective-permute-start.10) | collective-permute-done | bytes 92192 | tf_op jit(solution)/shard_map/ppermute | solution.py:398
  107.1 1.1 collective-permute-done.11.refs_3_
  108.1 0.1 collective-permute-done.9.refs_1_
  108.3 0.9 narrow.1
  109.1 2.7 %collective-permute-start.12 = (bf16[64,1280]{1,0:T(8,128)(2,1)S(1)}, bf16[64,1280]{1,0:T(8,128)(2,1)S(1)}, u32[]{:S(2)}, u32[]{:S(2)}) collective-permute-start(bf16[64,1280]{1,0:T(8,128)(2,1)S(1)} %get-tuple-element.27), channel_id=1, source_target_pairs={{0,3},{1,0},{2,1},{3,2},{4,7},{5,4},{6,5},{7,6},{8,11},{9,8},{10,9... | collective-permute-start | bytes 491528 | tf_op jit(solution)/shard_map/ppermute | solution.py:406
  111.9 0.9 collective-permute-start.13
  112.8 0.1 collective-permute-start.14
  112.9 3.6 %collective-permute-done.12.refs_1_ = bf16[64,1280]{1,0:T(8,128)(2,1)S(1)} collective-permute-done((bf16[64,1280]{1,0:T(8,128)(2,1)S(1)}, bf16[64,1280]{1,0:T(8,128)(2,1)S(1)}, u32[]{:S(2)}, u32[]{:S(2)}) %collective-permute-start.12) | collective-permute-done | bytes 163872 | tf_op jit(solution)/shard_map/ppermute | solution.py:406
  116.5 2.3 %collective-permute-done.13.refs_2_ = bf16[64,1280]{1,0:T(8,128)(2,1)S(1)} collective-permute-done((bf16[64,1280]{1,0:T(8,128)(2,1)S(1)}, bf16[64,1280]{1,0:T(8,128)(2,1)S(1)}, u32[]{:S(2)}, u32[]{:S(2)}) %collective-permute-start.13) | collective-permute-done | bytes 163872 | tf_op jit(solution)/shard_map/ppermute | solution.py:406
  118.8 1.7 %collective-permute-done.14.refs_3_ = bf16[64,1280]{1,0:T(8,128)(2,1)S(1)} collective-permute-done((bf16[64,1280]{1,0:T(8,128)(2,1)S(1)}, bf16[64,1280]{1,0:T(8,128)(2,1)S(1)}, u32[]{:S(2)}, u32[]{:S(2)}) %collective-permute-start.14) | collective-permute-done | bytes 163872 | tf_op jit(solution)/shard_map/ppermute | solution.py:406
  120.5 0.7 add.21
  121.2 3.4 %all-to-all-start.3 = ((bf16[8,8,1280]{2,1,0:T(8,128)(2,1)}), bf16[8,8,1280]{2,1,0:T(8,128)(2,1)S(1)}, u32[]{:S(2)}, u32[]{:S(2)}) async-start(bf16[8,8,1280]{2,1,0:T(8,128)(2,1)} %bitcast.13), calls=%async_computation.3 | async-start | bytes 327680 | tf_op jit(solution)/shard_map/all_to_all | solution.py:392
  125.3 4.0 %final_state.1 = f32[1,32,128,128]{3,2,1,0:T(8,128)} custom-call(s32[1]{0:T(128)S(6)} %copy.24.accepted_ref, bf16[1,4,4096]{2,1,0:T(4,128)(2,1)S(1)} %copy-done.4, bf16[1,4,128]{2,1,0:T(4,128)(2,1)S(1)} %copy-done.7, f32[1,4,32]{2,1,0:T(4,128)S(1)} %copy-done.6, f32[1,32]{1,0:T(1,128)S(1)} %bitcast.27, f32[1,32,128,128]{3,2,1,0:T(8,128)S(1)} %copy-done, ...), custom_call_target="tpu_custom_call" | custom-call | tf_op jit(solution)/shard_map/final_state/pallas_call | solution.py:372
  129.3 4.6 %all-to-all-done.3.refs_0_ = bf16[8,8,1280]{2,1,0:T(8,128)(2,1)S(1)} async-done(((bf16[8,8,1280]{2,1,0:T(8,128)(2,1)}), bf16[8,8,1280]{2,1,0:T(8,128)(2,1)S(1)}, u32[]{:S(2)}, u32[]{:S(2)}) %all-to-all-start.3) | async-done | bytes 163872 | tf_op jit(solution)/shard_map/all_to_all | solution.py:392
  133.9 0.6 finish.1
  (19 shorter events, 0.1 us)
Async XLA Ops:
  1.3 20.4 %copy-start.10 = (s32[128]{0:T(128)S(1)}, s32[128]{0:T(128)}, u32[]{:S(2)}) copy-start(s32[128]{0:T(128)} %param.39) | copy-start | bytes 1540
  1.3 34.8 %copy-start.1 = (bf16[192,1280]{1,0:T(8,128)(2,1)S(1)}, bf16[192,1280]{1,0:T(8,128)(2,1)}, u32[]{:S(2)}) copy-start(bf16[192,1280]{1,0:T(8,128)(2,1)} %refs_1_.6) | copy-start | bytes 1474564
  6.2 29.0 %all-to-all-start = ((bf16[128,4,192]{2,1,0:T(4,128)(2,1)}), bf16[128,4,192]{2,1,0:T(4,128)(2,1)S(1)}, u32[]{:S(2)}, u32[]{:S(2)}) async-start(bf16[128,4,192]{2,1,0:T(4,128)(2,1)} %bitcast.28), calls=%async_computation | async-start | bytes 524288 | tf_op jit(solution)/shard_map/all_to_all | solution.py:392
  36.5 7.9 %copy-start.9 = (f32[1280]{0:T(1024)S(1)}, f32[1280]{0:T(1024)}, u32[]{:S(2)}) copy-start(f32[1280]{0:T(1024)} %param.41) | copy-start | bytes 15364
  36.5 28.6 %copy-start.5 = (bf16[8,1280]{1,0:T(8,128)(2,1)S(1)}, bf16[8,1280]{1,0:T(8,128)(2,1)}, u32[]{:S(2)}) copy-start(bf16[8,1280]{1,0:T(8,128)(2,1)} %refs_1_.7) | copy-start | bytes 61444
  36.5 2.2 %collective-permute-start = (bf16[256,1280]{1,0:T(8,128)(2,1)S(1)}, bf16[256,1280]{1,0:T(8,128)(2,1)S(1)}, u32[]{:S(2)}, u32[]{:S(2)}) collective-permute-start(bf16[256,1280]{1,0:T(8,128)(2,1)S(1)} %project.1), channel_id=1, source_target_pairs={{0,128},{128,0},{1,129},{129,1},{2,130},{130,2},{3,131},{131,3},{4... | collective-permute-start | bytes 1966088 | tf_op jit(solution)/shard_map/ppermute | solution.py:420
  39.9 7.0 %collective-permute-start.1 = (bf16[672,1280]{1,0:T(8,128)(2,1)}, bf16[672,1280]{1,0:T(8,128)(2,1)S(1)}, u32[]{:S(2)}, u32[]{:S(2)}) collective-permute-start(bf16[672,1280]{1,0:T(8,128)(2,1)} %bitcast.20), channel_id=1, source_target_pairs={{0,128},{128,0},{1,129},{129,1},{2,130},{130,2},{3,131},{131,3},{4... | collective-permute-start | bytes 5160968 | tf_op jit(solution)/shard_map/ppermute | solution.py:420
  40.0 25.1 %all-to-all-start.1 = ((bf16[32,8,1280]{2,1,0:T(8,128)(2,1)}), bf16[32,8,1280]{2,1,0:T(8,128)(2,1)S(1)}, u32[]{:S(2)}, u32[]{:S(2)}) async-start(bf16[32,8,1280]{2,1,0:T(8,128)(2,1)} %bitcast.6), calls=%async_computation.1 | async-start | bytes 1310720 | tf_op jit(solution)/shard_map/all_to_all | solution.py:392
  44.2 2.7 %collective-permute-start.2 = (bf16[336,1280]{1,0:T(8,128)(2,1)}, bf16[336,1280]{1,0:T(8,128)(2,1)S(1)}, u32[]{:S(2)}, u32[]{:S(2)}) collective-permute-start(bf16[336,1280]{1,0:T(8,128)(2,1)} %refs_5_.2), channel_id=1, source_target_pairs={{0,128},{128,0},{1,129},{129,1},{2,130},{130,2},{3,131},{131,3},{4... | collective-permute-start | bytes 2580488 | tf_op jit(solution)/shard_map/ppermute | solution.py:420
  77.8 8.5 %collective-permute-start.3 = (bf16[8,8,1280]{2,1,0:T(8,128)(2,1)S(1)}, bf16[8,8,1280]{2,1,0:T(8,128)(2,1)S(1)}, u32[]{:S(2)}, u32[]{:S(2)}) collective-permute-start(bf16[8,8,1280]{2,1,0:T(8,128)(2,1)S(1)} %all_to_all.20), channel_id=1, source_target_pairs={{0,1},{1,2},{2,3},{3,0},{4,5},{5,6},{6,7},{7,4},{8,9},{9,10},{10,1... | collective-permute-start | bytes 491528 | tf_op jit(solution)/shard_map/ppermute | solution.py:406
  78.4 8.0 %collective-permute-start.4 = (bf16[8,8,1280]{2,1,0:T(8,128)(2,1)S(1)}, bf16[8,8,1280]{2,1,0:T(8,128)(2,1)S(1)}, u32[]{:S(2)}, u32[]{:S(2)}) collective-permute-start(bf16[8,8,1280]{2,1,0:T(8,128)(2,1)S(1)} %all_to_all.20), channel_id=1, source_target_pairs={{0,2},{1,3},{2,0},{3,1},{4,6},{5,7},{6,4},{7,5},{8,10},{9,11},{10,... | collective-permute-start | bytes 491528 | tf_op jit(solution)/shard_map/ppermute | solution.py:406
  80.8 6.2 %collective-permute-start.5 = (bf16[8,8,1280]{2,1,0:T(8,128)(2,1)S(1)}, bf16[8,8,1280]{2,1,0:T(8,128)(2,1)S(1)}, u32[]{:S(2)}, u32[]{:S(2)}) collective-permute-start(bf16[8,8,1280]{2,1,0:T(8,128)(2,1)S(1)} %all_to_all.20), channel_id=1, source_target_pairs={{0,3},{1,0},{2,1},{3,2},{4,7},{5,4},{6,5},{7,6},{8,11},{9,8},{10,9... | collective-permute-start | bytes 491528 | tf_op jit(solution)/shard_map/ppermute | solution.py:406
  87.0 1.5 %copy-start.2 = (bf16[1280,2,336]{0,2,1:T(8,128)(2,1)S(1)}, bf16[1280,2,336]{0,2,1:T(8,128)(2,1)}, u32[]{:S(2)}) copy-start(bf16[1280,2,336]{0,2,1:T(8,128)(2,1)} %param.42) | copy-start | bytes 5160964
  88.4 19.8 %copy-start.3 = (bf16[336,1280]{1,0:T(8,128)(2,1)S(1)}, bf16[336,1280]{1,0:T(8,128)(2,1)}, u32[]{:S(2)}) copy-start(bf16[336,1280]{1,0:T(8,128)(2,1)} %refs_5_.2) | copy-start | bytes 2580484
  89.8 35.5 %copy-start = (f32[1,32,128,128]{3,2,1,0:T(8,128)S(1)}, f32[1,32,128,128]{3,2,1,0:T(8,128)}, u32[]{:S(2)}) copy-start(f32[1,32,128,128]{3,2,1,0:T(8,128)} %state_ref.1) | copy-start | bytes 6291460
  89.8 35.5 %copy-start.4 = (bf16[1,4,4096]{2,1,0:T(4,128)(2,1)S(1)}, bf16[1,4,4096]{2,1,0:T(4,128)(2,1)}, u32[]{:S(2)}) copy-start(bf16[1,4,4096]{2,1,0:T(4,128)(2,1)} %x_ref.1) | copy-start | bytes 98308
  89.8 35.5 %copy-start.6 = (f32[1,4,32]{2,1,0:T(4,128)S(1)}, f32[1,4,32]{2,1,0:T(4,128)}, u32[]{:S(2)}) copy-start(f32[1,4,32]{2,1,0:T(4,128)} %dt_ref.1) | copy-start | bytes 1540
  89.8 35.5 %copy-start.7 = (bf16[1,4,128]{2,1,0:T(4,128)(2,1)S(1)}, bf16[1,4,128]{2,1,0:T(4,128)(2,1)}, u32[]{:S(2)}) copy-start(bf16[1,4,128]{2,1,0:T(4,128)(2,1)} %in_map_ref.1) | copy-start | bytes 3076
  89.8 35.5 %copy-start.8 = (f32[32]{0:T(128)S(1)}, f32[32]{0:T(128)}, u32[]{:S(2)}) copy-start(f32[32]{0:T(128)} %param.35) | copy-start | bytes 388
  89.8 5.6 %collective-permute-start.6 = (bf16[64,1408]{1,0:T(8,128)(2,1)S(1)}, bf16[64,1408]{1,0:T(8,128)(2,1)S(1)}, u32[]{:S(2)}, u32[]{:S(2)}) collective-permute-start(bf16[64,1408]{1,0:T(8,128)(2,1)S(1)} %get-tuple-element.23), channel_id=1, source_target_pairs={{0,32},{32,64},{64,96},{96,0},{1,33},{33,65},{65,97},{97,1},{2,34}... | collective-permute-start | bytes 540680 | tf_op jit(solution)/shard_map/ppermute | solution.py:398
  91.5 7.1 %collective-permute-start.7 = (bf16[64,1408]{1,0:T(8,128)(2,1)S(1)}, bf16[64,1408]{1,0:T(8,128)(2,1)S(1)}, u32[]{:S(2)}, u32[]{:S(2)}) collective-permute-start(bf16[64,1408]{1,0:T(8,128)(2,1)S(1)} %get-tuple-element.24), channel_id=1, source_target_pairs={{0,64},{32,96},{64,0},{96,32},{1,65},{33,97},{65,1},{97,33},{2,66}... | collective-permute-start | bytes 540680 | tf_op jit(solution)/shard_map/ppermute | solution.py:398
  94.0 6.5 %collective-permute-start.8 = (bf16[64,1408]{1,0:T(8,128)(2,1)S(1)}, bf16[64,1408]{1,0:T(8,128)(2,1)S(1)}, u32[]{:S(2)}, u32[]{:S(2)}) collective-permute-start(bf16[64,1408]{1,0:T(8,128)(2,1)S(1)} %get-tuple-element.25), channel_id=1, source_target_pairs={{0,96},{32,0},{64,32},{96,64},{1,97},{33,1},{65,33},{97,65},{2,98}... | collective-permute-start | bytes 540680 | tf_op jit(solution)/shard_map/ppermute | solution.py:398
  100.9 6.2 %collective-permute-start.10 = (bf16[64,720]{1,0:T(8,128)(2,1)S(1)}, bf16[64,720]{1,0:T(8,128)(2,1)S(1)}, u32[]{:S(2)}, u32[]{:S(2)}) collective-permute-start(bf16[64,720]{1,0:T(8,128)(2,1)S(1)} %gate.1.refs_0_), channel_id=1, source_target_pairs={{0,64},{32,96},{64,0},{96,32},{1,65},{33,97},{65,1},{97,33},{2,66}... | collective-permute-start | bytes 276488 | tf_op jit(solution)/shard_map/ppermute | solution.py:398
  103.5 4.6 %collective-permute-start.11 = (bf16[64,720]{1,0:T(8,128)(2,1)S(1)}, bf16[64,720]{1,0:T(8,128)(2,1)S(1)}, u32[]{:S(2)}, u32[]{:S(2)}) collective-permute-start(bf16[64,720]{1,0:T(8,128)(2,1)S(1)} %gate.1.refs_0_), channel_id=1, source_target_pairs={{0,96},{32,0},{64,32},{96,64},{1,97},{33,1},{65,33},{97,65},{2,98}... | collective-permute-start | bytes 276488 | tf_op jit(solution)/shard_map/ppermute | solution.py:398
  103.6 4.7 %collective-permute-start.9 = (bf16[64,720]{1,0:T(8,128)(2,1)S(1)}, bf16[64,720]{1,0:T(8,128)(2,1)S(1)}, u32[]{:S(2)}, u32[]{:S(2)}) collective-permute-start(bf16[64,720]{1,0:T(8,128)(2,1)S(1)} %gate.1.refs_0_), channel_id=1, source_target_pairs={{0,32},{32,64},{64,96},{96,0},{1,33},{33,65},{65,97},{97,1},{2,34}... | collective-permute-start | bytes 276488 | tf_op jit(solution)/shard_map/ppermute | solution.py:398
  109.1 7.4 %collective-permute-start.12 = (bf16[64,1280]{1,0:T(8,128)(2,1)S(1)}, bf16[64,1280]{1,0:T(8,128)(2,1)S(1)}, u32[]{:S(2)}, u32[]{:S(2)}) collective-permute-start(bf16[64,1280]{1,0:T(8,128)(2,1)S(1)} %get-tuple-element.27), channel_id=1, source_target_pairs={{0,3},{1,0},{2,1},{3,2},{4,7},{5,4},{6,5},{7,6},{8,11},{9,8},{10,9... | collective-permute-start | bytes 491528 | tf_op jit(solution)/shard_map/ppermute | solution.py:406
  111.9 6.9 %collective-permute-start.13 = (bf16[64,1280]{1,0:T(8,128)(2,1)S(1)}, bf16[64,1280]{1,0:T(8,128)(2,1)S(1)}, u32[]{:S(2)}, u32[]{:S(2)}) collective-permute-start(bf16[64,1280]{1,0:T(8,128)(2,1)S(1)} %get-tuple-element.28), channel_id=1, source_target_pairs={{0,2},{1,3},{2,0},{3,1},{4,6},{5,7},{6,4},{7,5},{8,10},{9,11},{10,... | collective-permute-start | bytes 491528 | tf_op jit(solution)/shard_map/ppermute | solution.py:406
  112.8 7.6 %collective-permute-start.14 = (bf16[64,1280]{1,0:T(8,128)(2,1)S(1)}, bf16[64,1280]{1,0:T(8,128)(2,1)S(1)}, u32[]{:S(2)}, u32[]{:S(2)}) collective-permute-start(bf16[64,1280]{1,0:T(8,128)(2,1)S(1)} %get-tuple-element.29), channel_id=1, source_target_pairs={{0,1},{1,2},{2,3},{3,0},{4,5},{5,6},{6,7},{7,4},{8,9},{9,10},{10,1... | collective-permute-start | bytes 491528 | tf_op jit(solution)/shard_map/ppermute | solution.py:406
  121.2 12.7 %all-to-all-start.3 = ((bf16[8,8,1280]{2,1,0:T(8,128)(2,1)}), bf16[8,8,1280]{2,1,0:T(8,128)(2,1)S(1)}, u32[]{:S(2)}, u32[]{:S(2)}) async-start(bf16[8,8,1280]{2,1,0:T(8,128)(2,1)} %bitcast.13), calls=%async_computation.3 | async-start | bytes 327680 | tf_op jit(solution)/shard_map/all_to_all | solution.py:392
